TPU v7x, 32 devices: a whole 2x2x4 slice. The times are simulated.
32 devices in a mesh: shard: 8 (over z, core), ctx: 4 (over y, x).
Axes of the slice: x: 2, y: 2, z: 4, core: 2. Of those that a mesh axis runs over, the one named last changes fastest.
Arguments:
- tokens: bfloat16 [32, 384, 512], P('shard', 'ctx'), may hold values from -6 to 6
- lengths: int32 [32], P('shard'), may hold values from 96 to 384, as said below
- out_weight: float32 [512, 1024], P('shard'), may hold values from -0.25 to 0.25
- out_bias: float32 [1024], P('shard'), may hold values from -3 to 3
- decay_rate: float32 [512, 64], P('shard'), may hold values from 0.00026041668 to 0.05
- frequency: float32 [512, 64], P('shard'), may hold values from -0.5 to 0.5
- coef_real: float32 [512, 64], P('shard'), may hold values from -0.5 to 0.5
- coef_imag: float32 [512, 64], P('shard'), may hold values from -0.5 to 0.5
- skip: float32 [512], P('shard'), may hold values from -4 to 4
- gain: float32 [512], P('shard'), may hold values from 0.5 to 1.5
- shift: float32 [512], P('shard'), may hold values from -3 to 3
- cotangent: bfloat16 [32, 384, 512], P('shard', 'ctx'), may hold values from -6 to 6
Outputs:
- block_out: bfloat16 [32, 384, 512], P('shard', 'ctx')
- tokens_grad: bfloat16 [32, 384, 512], P('shard', 'ctx')
- out_weight_grad: float32 [512, 1024], P('shard')
- out_bias_grad: float32 [1024], P('shard')
- decay_grad: float32 [512, 64], P('shard')
- frequency_grad: float32 [512, 64], P('shard')
- coef_real_grad: float32 [512, 64], P('shard')
- coef_imag_grad: float32 [512, 64], P('shard')
- skip_grad: float32 [512], P('shard')
- gain_grad: float32 [512], P('shard')
- shift_grad: float32 [512], P('shard')
Inputs may be any that keep to these rules, and one draw needn't show every extreme that they name: `lengths`: the number of valid positions of each sequence; the first sequence has all 384.
All inputs are finite; a program needn't handle non-finite values.
Results may differ from a plain program's by a relative error of at most 0.02.
Values may be sent and summed in bfloat16 or wider, within the bound.
No kernel may reach another device: no remote copies, remote signals or barrier semaphores. Data moves between devices by JAX's collectives and lax.ppermute only.
A program may use at most 128 MiB of HBM per device.

v0:
```python
import jax
import jax.numpy as jnp
from jax import lax
from jax.sharding import PartitionSpec as P

HIGH = lax.Precision.HIGHEST
EPSILON = 1e-05


def carried_in(value, axis, join, neutral):
    count, mine = (lax.axis_size(axis), lax.axis_index(axis))
    pieces = jax.tree.map(lambda part: lax.all_gather(part, axis), value)
    total = jax.tree.map(
        lambda part, zero: jnp.full_like(part, 0) + jnp.asarray(zero, part.dtype), value, neutral
    )

    def turn(position, total):
        longer = join(total, jax.tree.map(lambda part: part[position], pieces))
        return jax.tree.map(lambda new, old: jnp.where(position < mine, new, old), longer, total)

    return lax.fori_loop(0, count - 1, turn, total)


def carried_in_2(x, axis, join, neutral):
    count = lax.axis_size(axis)
    place = lax.axis_index(axis)
    ahead = count - 1 - place
    gathered = jax.tree.map(
        lambda a, kind: lax.all_gather(a.astype(kind), axis),
        x,
        (jnp.bfloat16, jnp.bfloat16, jnp.bfloat16),
    )
    state = jax.tree.map(lambda a, e: jnp.zeros_like(a) + jnp.asarray(e, a.dtype), x, neutral)

    def one(turn, state):
        source = count - 1 - turn
        return join(
            state,
            jax.tree.map(
                lambda a, own: lax.dynamic_index_in_dim(a, source, 0, False).astype(own.dtype),
                gathered,
                x,
            ),
        )

    return lax.fori_loop(0, ahead, one, state)


def powers(decay_grp, freq_grp, offsets):
    magnitude = jnp.exp(-decay_grp[:, :, None] * offsets)
    phase = freq_grp[:, :, None] * offsets
    return (magnitude * jnp.cos(phase), magnitude * jnp.sin(phase))


def split_product(form, table, data):
    high_part = table.astype(jnp.bfloat16)
    rest_part = (table - high_part.astype(jnp.float32)).astype(jnp.bfloat16)
    first = jnp.einsum(form, high_part, data, preferred_element_type=jnp.float32)
    return first + jnp.einsum(form, rest_part, data, preferred_element_type=jnp.float32)


def norm_forward(row_vals, gain_vec, shift_vec, valid):
    row_mean = jnp.mean(row_vals, axis=-1, keepdims=True)
    centered = row_vals - row_mean
    row_var = jnp.mean(centered * centered, axis=-1, keepdims=True)
    return valid * (centered * lax.rsqrt(row_var + EPSILON) * gain_vec + shift_vec)


def to_groups(values, groups):
    seq_count, row_count, channels = values.shape
    return values.reshape(seq_count, row_count, groups, channels // groups).transpose(2, 0, 1, 3)


def from_groups(values):
    groups, seq_count, row_count, group_size = values.shape
    return values.transpose(1, 2, 0, 3).reshape(seq_count, row_count, groups * group_size)


def state_groups(values, groups):
    seq_count, channels, state_count = values.shape
    return values.reshape(seq_count, groups, channels // groups, state_count).transpose(1, 0, 2, 3)


def state_merge(values):
    groups, seq_count, group_size, state_count = values.shape
    return values.transpose(1, 0, 2, 3).reshape(seq_count, groups * group_size, state_count)


def lower_toeplitz(kernel):
    chans, count = kernel.shape
    pattern = jnp.concatenate(
        [kernel[:, :1], jnp.zeros((chans, count), kernel.dtype), kernel[:, :0:-1]], axis=1
    )
    repeated = jnp.tile(pattern, (1, count))[:, : count * (2 * count - 1)]
    return repeated.reshape(chans, count, 2 * count - 1)[:, :, :count]


def lag_sums(outer_prod):
    chans, count, _ = outer_prod.shape
    flipped = jnp.concatenate([outer_prod[:, :, ::-1], jnp.zeros_like(outer_prod)], axis=2).reshape(
        chans, -1
    )
    sheared = flipped[:, count - 1 : count - 1 + count * (2 * count - 1)].reshape(
        chans, count, 2 * count - 1
    )[:, :, :count]
    return jnp.sum(sheared, axis=1)


def per_device(
    tokens,
    lengths,
    out_weight,
    out_bias,
    decay_rate,
    frequency,
    coef_real,
    coef_imag,
    skip,
    gain,
    shift,
    cotangent,
):
    seq_count, seq_rows, channels = tokens.shape
    group_size = min(32, channels)
    groups = channels // group_size
    decay_all, freq_all, real_all, imag_all, skip_all, gain_all, shift_all = (
        lax.all_gather(decay_rate, "shard", axis=0, tiled=True),
        lax.all_gather(frequency, "shard", axis=0, tiled=True),
        lax.all_gather(coef_real, "shard", axis=0, tiled=True),
        lax.all_gather(coef_imag, "shard", axis=0, tiled=True),
        lax.all_gather(skip, "shard", axis=0, tiled=True),
        lax.all_gather(gain, "shard", axis=0, tiled=True),
        lax.all_gather(shift, "shard", axis=0, tiled=True),
    )
    weight_all, bias_all = (
        lax.all_gather(out_weight.astype(jnp.bfloat16), "shard", axis=0, tiled=True),
        lax.all_gather(out_bias.astype(jnp.bfloat16), "shard", axis=0, tiled=True),
    )
    scale_all = jnp.sqrt(-jnp.expm1(-2.0 * decay_all))
    hat_real = scale_all * real_all
    hat_imag = scale_all * imag_all
    decay_grp = decay_all.reshape(groups, group_size, -1)
    freq_grp = freq_all.reshape(groups, group_size, -1)
    real_grp = real_all.reshape(groups, group_size, -1)
    imag_grp = imag_all.reshape(groups, group_size, -1)
    hre_grp = hat_real.reshape(groups, group_size, -1)
    him_grp = hat_imag.reshape(groups, group_size, -1)
    own_index = lax.axis_index("ctx")
    positions = own_index * seq_rows + jnp.arange(seq_rows, dtype=jnp.int32)
    valid = (positions[None, :] < lengths[:, None]).astype(jnp.float32)[:, :, None]
    lag_steps = jnp.arange(seq_rows, dtype=jnp.float32)
    tokens_wide = tokens.astype(jnp.float32)

    def apply_norm(row_vals, gain_vec, shift_vec):
        return norm_forward(row_vals, gain_vec, shift_vec, valid)

    normed_full, norm_pull = jax.vjp(apply_norm, tokens_wide, gain_all, shift_all)
    normed_low = normed_full.astype(jnp.bfloat16)
    normed = normed_low.astype(jnp.float32)
    normed_grp = to_groups(normed_low, groups)

    def make_toeplitz(hre_one, him_one, pow_re, pow_im):
        kernel = jnp.sum(hre_one[:, :, None] * pow_re - him_one[:, :, None] * pow_im, axis=1)
        return lower_toeplitz(kernel)

    def local_forward(inputs):
        decay_one, freq_one, hre_one, him_one, input_one = inputs
        pow_re, pow_im = powers(decay_one, freq_one, lag_steps)
        toeplitz = make_toeplitz(hre_one, him_one, pow_re, pow_im)
        conv_local = split_product("hts,zsh->zth", toeplitz, input_one)
        back_re = pow_re[:, :, ::-1]
        back_im = pow_im[:, :, ::-1]
        weighted = lag_steps[::-1]
        end_re = split_product("hnj,zjh->zhn", back_re, input_one)
        end_im = split_product("hnj,zjh->zhn", back_im, input_one)
        slope_re = split_product("hnj,zjh->zhn", back_re * weighted, input_one)
        slope_im = split_product("hnj,zjh->zhn", back_im * weighted, input_one)
        return (conv_local, end_re, end_im, slope_re, slope_im)

    conv_local, end_re, end_im, slope_re, slope_im = lax.map(
        local_forward, (decay_grp, freq_grp, hre_grp, him_grp, normed_grp)
    )
    end_re = state_merge(end_re)
    end_im = state_merge(end_im)
    slope_re = state_merge(slope_re)
    slope_im = state_merge(slope_im)
    zero_state = jnp.zeros_like(end_re)
    own_span = jnp.full((1,), float(seq_rows), jnp.float32)

    def forward_combine(earlier, later):
        span_one, sre_one, sim_one, dre_one, dim_one = earlier
        span_two, sre_two, sim_two, dre_two, dim_two = later
        magnitude = jnp.exp(-decay_all * span_two)
        fac_re = magnitude * jnp.cos(freq_all * span_two)
        fac_im = magnitude * jnp.sin(freq_all * span_two)
        lift_re = dre_one + span_two * sre_one
        lift_im = dim_one + span_two * sim_one
        new_sre = fac_re * sre_one - fac_im * sim_one + sre_two
        new_sim = fac_re * sim_one + fac_im * sre_one + sim_two
        new_dre = fac_re * lift_re - fac_im * lift_im + dre_two
        new_dim = fac_re * lift_im + fac_im * lift_re + dim_two
        return (span_one + span_two, new_sre, new_sim, new_dre, new_dim)

    zero_span = jnp.zeros((1,), jnp.float32)
    span_in, in_re, in_im, in_dre, in_dim = carried_in(
        (own_span, end_re, end_im, slope_re, slope_im),
        "ctx",
        forward_combine,
        (zero_span, zero_state, zero_state, zero_state, zero_state),
    )

    def cross_forward(inputs):
        decay_one, freq_one, hre_one, him_one, sre_one, sim_one = inputs
        next_re, next_im = powers(decay_one, freq_one, lag_steps + 1.0)
        mix_re = hre_one * sre_one - him_one * sim_one
        mix_im = hre_one * sim_one + him_one * sre_one
        return jnp.einsum("hnt,zhn->zth", next_re, mix_re, precision=HIGH) - jnp.einsum(
            "hnt,zhn->zth", next_im, mix_im, precision=HIGH
        )

    conv_cross = lax.map(
        cross_forward,
        (
            decay_grp,
            freq_grp,
            hre_grp,
            him_grp,
            state_groups(in_re, groups),
            state_groups(in_im, groups),
        ),
    )
    mixed = from_groups(conv_local + conv_cross) + skip_all * normed
    hidden_wide, gelu_pull = jax.vjp(jax.nn.gelu, mixed)
    hidden = hidden_wide.astype(jnp.bfloat16).reshape(seq_count * seq_rows, channels)
    proj = jnp.dot(hidden, weight_all, preferred_element_type=jnp.float32) + bias_all.astype(
        jnp.float32
    )

    def gate_unit(proj_vals):
        return proj_vals[:, :channels] * jax.nn.sigmoid(proj_vals[:, channels:])

    gated, gate_pull = jax.vjp(gate_unit, proj)
    valid_flat = valid.reshape(seq_count * seq_rows, 1)
    block_out = (tokens_wide + (valid_flat * gated).reshape(seq_count, seq_rows, channels)).astype(
        jnp.bfloat16
    )
    cot_wide = cotangent.astype(jnp.float32)
    grad_proj = gate_pull(valid_flat * cot_wide.reshape(seq_count * seq_rows, channels))[0].astype(
        jnp.bfloat16
    )
    grad_weight = jnp.einsum("rk,rm->km", hidden, grad_proj, preferred_element_type=jnp.float32)
    grad_bias = jnp.sum(grad_proj.astype(jnp.float32), axis=0)
    grad_hidden = jnp.einsum("rm,km->rk", grad_proj, weight_all, preferred_element_type=jnp.float32)
    grad_mixed_low = gelu_pull(grad_hidden.reshape(seq_count, seq_rows, channels))[0].astype(
        jnp.bfloat16
    )
    grad_mixed = grad_mixed_low.astype(jnp.float32)
    grad_skip = jnp.sum(grad_mixed * normed, axis=(0, 1))
    grad_mixed_grp = to_groups(grad_mixed_low, groups)

    def local_backward(inputs):
        (
            decay_one,
            freq_one,
            hre_one,
            him_one,
            real_one,
            imag_one,
            input_one,
            grad_one,
            sre_one,
            sim_one,
            dre_one,
            dim_one,
        ) = inputs
        pow_re, pow_im = powers(decay_one, freq_one, lag_steps)
        toeplitz = make_toeplitz(hre_one, him_one, pow_re, pow_im)
        grad_local = split_product("hts,zth->zsh", toeplitz, grad_one)
        outer_prod = jnp.einsum(
            "zth,zsh->hts", grad_one, input_one, preferred_element_type=jnp.float32
        )
        corr = lag_sums(outer_prod)
        one_re = jnp.sum(pow_re * corr[:, None, :], axis=2)
        one_im = jnp.sum(pow_im * corr[:, None, :], axis=2)
        two_re = jnp.sum(pow_re * (corr * lag_steps)[:, None, :], axis=2)
        two_im = jnp.sum(pow_im * (corr * lag_steps)[:, None, :], axis=2)
        next_re, next_im = powers(decay_one, freq_one, lag_steps + 1.0)
        w_re = split_product("hnt,zth->zhn", next_re, grad_one)
        w_im = split_product("hnt,zth->zhn", next_im, grad_one)
        lifted = lag_steps + 1.0
        wl_re = split_product("hnt,zth->zhn", next_re * lifted, grad_one)
        wl_im = split_product("hnt,zth->zhn", next_im * lifted, grad_one)
        one_re = one_re + jnp.sum(w_re * sre_one - w_im * sim_one, axis=0)
        one_im = one_im + jnp.sum(w_re * sim_one + w_im * sre_one, axis=0)
        two_re = two_re + jnp.sum(
            wl_re * sre_one - wl_im * sim_one + w_re * dre_one - w_im * dim_one, axis=0
        )
        two_im = two_im + jnp.sum(
            wl_re * sim_one + wl_im * sre_one + w_re * dim_one + w_im * dre_one, axis=0
        )
        back_re = split_product("hnt,zth->zhn", pow_re, grad_one)
        back_im = split_product("hnt,zth->zhn", pow_im, grad_one)
        scale_one = jnp.sqrt(-jnp.expm1(-2.0 * decay_one))
        slope_scale = jnp.exp(-2.0 * decay_one) / scale_one
        grad_him = -one_im
        grad_decay = -(hre_one * two_re - him_one * two_im) + slope_scale * (
            real_one * one_re + imag_one * grad_him
        )
        grad_freq = -(hre_one * two_im + him_one * two_re)
        return (
            grad_local,
            back_re,
            back_im,
            grad_decay,
            grad_freq,
            scale_one * one_re,
            scale_one * grad_him,
        )

    grad_local, back_re, back_im, grad_decay, grad_freq, grad_real, grad_imag = lax.map(
        local_backward,
        (
            decay_grp,
            freq_grp,
            hre_grp,
            him_grp,
            real_grp,
            imag_grp,
            normed_grp,
            grad_mixed_grp,
            state_groups(in_re, groups),
            state_groups(in_im, groups),
            state_groups(in_dre, groups),
            state_groups(in_dim, groups),
        ),
    )
    back_re = state_merge(back_re)
    back_im = state_merge(back_im)

    def reverse_combine(earlier, later):
        span_far, qre_far, qim_far = earlier
        span_near, qre_near, qim_near = later
        magnitude = jnp.exp(-decay_all * span_near)
        fac_re = magnitude * jnp.cos(freq_all * span_near)
        fac_im = magnitude * jnp.sin(freq_all * span_near)
        new_re = qre_near + fac_re * qre_far - fac_im * qim_far
        new_im = qim_near + fac_re * qim_far + fac_im * qre_far
        return (span_far + span_near, new_re, new_im)

    zero_span = jnp.zeros((1,), jnp.float32)
    span_back, later_re, later_im = carried_in_2(
        (own_span, back_re, back_im), "ctx", reverse_combine, (zero_span, zero_state, zero_state)
    )

    def cross_backward(inputs):
        decay_one, freq_one, hre_one, him_one, qre_one, qim_one = inputs
        tail_re, tail_im = powers(decay_one, freq_one, seq_rows - lag_steps)
        mix_re = hre_one * qre_one - him_one * qim_one
        mix_im = hre_one * qim_one + him_one * qre_one
        return jnp.einsum("hnj,zhn->zjh", tail_re, mix_re, precision=HIGH) - jnp.einsum(
            "hnj,zhn->zjh", tail_im, mix_im, precision=HIGH
        )

    grad_cross = lax.map(
        cross_backward,
        (
            decay_grp,
            freq_grp,
            hre_grp,
            him_grp,
            state_groups(later_re, groups),
            state_groups(later_im, groups),
        ),
    )
    grad_normed = from_groups(grad_local + grad_cross) + skip_all * grad_mixed
    grad_rows, grad_gain, grad_shift = norm_pull(grad_normed)
    tokens_grad = (cot_wide + grad_rows).astype(jnp.bfloat16)
    grad_decay = grad_decay.reshape(channels, -1)
    grad_freq = grad_freq.reshape(channels, -1)
    grad_real = grad_real.reshape(channels, -1)
    grad_imag = grad_imag.reshape(channels, -1)
    partial_owned = (
        lax.psum_scatter(
            grad_weight.astype(jnp.bfloat16), "shard", scatter_dimension=0, tiled=True
        ).astype(jnp.float32),
        lax.psum_scatter(
            grad_bias.astype(jnp.bfloat16), "shard", scatter_dimension=0, tiled=True
        ).astype(jnp.float32),
        lax.psum_scatter(
            grad_decay.astype(jnp.bfloat16), "shard", scatter_dimension=0, tiled=True
        ).astype(jnp.float32),
        lax.psum_scatter(
            grad_freq.astype(jnp.bfloat16), "shard", scatter_dimension=0, tiled=True
        ).astype(jnp.float32),
        lax.psum_scatter(
            grad_real.astype(jnp.bfloat16), "shard", scatter_dimension=0, tiled=True
        ).astype(jnp.float32),
        lax.psum_scatter(
            grad_imag.astype(jnp.bfloat16), "shard", scatter_dimension=0, tiled=True
        ).astype(jnp.float32),
        lax.psum_scatter(
            grad_skip.astype(jnp.bfloat16), "shard", scatter_dimension=0, tiled=True
        ).astype(jnp.float32),
        lax.psum_scatter(
            grad_gain.astype(jnp.bfloat16), "shard", scatter_dimension=0, tiled=True
        ).astype(jnp.float32),
        lax.psum_scatter(
            grad_shift.astype(jnp.bfloat16), "shard", scatter_dimension=0, tiled=True
        ).astype(jnp.float32),
    )
    owned = (
        lax.psum(partial_owned[0].astype(jnp.bfloat16), "ctx").astype(jnp.float32),
        lax.psum(partial_owned[1].astype(jnp.bfloat16), "ctx").astype(jnp.float32),
        lax.psum(partial_owned[2].astype(jnp.bfloat16), "ctx").astype(jnp.float32),
        lax.psum(partial_owned[3].astype(jnp.bfloat16), "ctx").astype(jnp.float32),
        lax.psum(partial_owned[4].astype(jnp.bfloat16), "ctx").astype(jnp.float32),
        lax.psum(partial_owned[5].astype(jnp.bfloat16), "ctx").astype(jnp.float32),
        lax.psum(partial_owned[6].astype(jnp.bfloat16), "ctx").astype(jnp.float32),
        lax.psum(partial_owned[7].astype(jnp.bfloat16), "ctx").astype(jnp.float32),
        lax.psum(partial_owned[8].astype(jnp.bfloat16), "ctx").astype(jnp.float32),
    )
    return (
        block_out,
        tokens_grad,
        owned[0],
        owned[1],
        owned[2],
        owned[3],
        owned[4],
        owned[5],
        owned[6],
        owned[7],
        owned[8],
    )


def solution(mesh):
    in_specs = (
        P("shard", "ctx", None),
        P("shard"),
        P("shard", None),
        P("shard"),
        P("shard", None),
        P("shard", None),
        P("shard", None),
        P("shard", None),
        P("shard"),
        P("shard"),
        P("shard"),
        P("shard", "ctx", None),
    )
    out_specs = (
        P("shard", "ctx", None),
        P("shard", "ctx", None),
        P("shard", None),
        P("shard"),
        P("shard", None),
        P("shard", None),
        P("shard", None),
        P("shard", None),
        P("shard"),
        P("shard"),
        P("shard"),
    )
    return jax.shard_map(
        per_device, mesh=mesh, in_specs=in_specs, out_specs=out_specs, check_vma=False
    )
```

profile of v0, /device:TPU:0, one launch (start us, length us, event | category | flops | bytes accessed | tf_op | source)
XLA Modules:
  0.0 2995.3 jit_solution(9044112479715933264)
XLA Ops:
  14.2 18.3 all-reduce.12
  34.0 15.3 all_gather.55
  49.3 14.2 all_gather.56
  63.5 14.2 all_gather.58
  77.7 14.2 all_gather.57
  95.1 523.4 %while.115 = (s32[]{:T(128)}, f32[16,4,96,32]{2,1,3,0:T(4,128)}, f32[16,4,32,64]{3,1,2,0:T(4,128)}, f32[16,4,32,64]{3,1,2,0:T(4,128)}, f32[16,4,32,64]{3,1,2,0:T...) while((s32[]{:T(128)}, f32[16,4,96,32]{2,1,3,0:T(4,128)}, ...), condition=%wide.region_4.5_spmd.clone.clone.clone, body=%wide.region_2.4_spmd.clone.clone.sunk.clone | while | flops 24828928 | bytes 29552664 | solution.py:180
  96.6 5.8 fusion.378
  129.3 5.8 fusion.378
  162.0 5.8 fusion.378
  194.7 5.8 fusion.378
  227.4 5.8 fusion.378
  292.9 5.8 fusion.378
  325.6 5.8 fusion.378
  358.3 5.8 fusion.378
  587.3 5.8 fusion.378
  628.4 10.0 all-reduce.5
  638.3 8.8 all-gather
  654.9 37.2 %all-gather.13.cloned.1.call-done = f32[4,4,512,64]{2,3,1,0:T(8,128)} async-done(((f32[1,4,512,64]{2,3,1,0:T(8,128)}), f32[4,4,512,64]{2,3,1,0:T(8,128)}) %all-gather.13.cloned.1.call-update) | async-done | bytes 2097168 | tf_op jit(solution)/shard_map/all_gather | solution.py:12
  692.1 37.2 %all-gather.15.cloned.1.call-done = f32[4,4,512,64]{2,3,1,0:T(8,128)} async-done(((f32[1,4,512,64]{2,3,1,0:T(8,128)}), f32[4,4,512,64]{2,3,1,0:T(8,128)}) %all-gather.15.cloned.1.call-update) | async-done | bytes 2097168 | tf_op jit(solution)/shard_map/all_gather | solution.py:12
  729.3 37.0 %all-gather.9.cloned.1.call-done = f32[4,4,512,64]{2,3,1,0:T(8,128)} async-done(((f32[1,4,512,64]{2,3,1,0:T(8,128)}), f32[4,4,512,64]{2,3,1,0:T(8,128)}) %all-gather.9.cloned.1.call-update) | async-done | bytes 2097168 | tf_op jit(solution)/shard_map/all_gather | solution.py:12
  766.3 52.3 %while.119 = (s32[]{:T(128)}, f32[4,512,64]{2,1,0:T(8,128)}, f32[4,512,64]{2,1,0:T(8,128)}, f32[4,512,64]{2,1,0:T(8,128)}, f32[4,512,64]{2,1,0:T(8,128)}, /*inde...) while((s32[]{:T(128)}, f32[4,512,64]{2,1,0:T(8,128)}, ...), condition=%wide.region_6.7_spmd.clone.clone, body=%wide.region_5.6_spmd.clone.sunk.clone | while | flops 3801092 | bytes 15466669 | solution.py:21
  794.8 6.0 fusion.427
  812.7 6.0 fusion.427
  823.5 201.4 %while.116 = (s32[]{:T(128)}, f32[16,4,96,32]{2,1,3,0:T(4,128)S(1)}, f32[16,32,64]{2,1,0:T(8,128)}, f32[16,4,32,64]{3,1,2,0:T(4,128)}, f32[16,32,64]{2,1,0:T(8,1...) while((s32[]{:T(128)}, f32[16,4,96,32]{2,1,3,0:T(4,128)S(1)}, ...), condition=%wide.region_8.9_spmd.clone.clone.clone, body=%wide.region_7.8_spmd.clone.clone.sunk.clone | while | flops 20117600 | bytes 609117 | solution.py:221
  1044.0 1607.5 %while.117 = (s32[]{:T(128)}, f32[16,4,96,32]{2,1,3,0:T(4,128)}, bf16[16,4,32,64]{3,1,2,0:T(4,128)(2,1)}, bf16[16,4,32,64]{3,1,2,0:T(4,128)(2,1)}, bf16[16,32,64...) while((s32[]{:T(128)}, f32[16,4,96,32]{2,1,3,0:T(4,128)}, ...), condition=%wide.region_20.21_spmd.clone.clone.clone, body=%wide.region_9.20_spmd.clone.clone.sunk.clone | while | flops 44635232 | bytes 38760272 | solution.py:320
  1059.0 11.2 rev.46
  1085.1 6.4 fusion.405
  1158.6 11.2 rev.46
  1184.7 6.4 fusion.405
  1258.3 11.2 rev.46
  1284.4 6.4 fusion.405
  1357.9 11.2 rev.46
  1384.0 6.4 fusion.405
  1457.5 11.2 rev.46
  1483.7 6.4 fusion.405
  1557.2 11.2 rev.46
  1583.3 6.4 fusion.405
  1656.8 11.2 rev.46
  1683.0 6.4 fusion.405
  1756.5 11.2 rev.46
  1782.6 6.4 fusion.405
  1856.1 11.2 rev.46
  1882.2 6.4 fusion.405
  1955.8 11.2 rev.46
  1981.9 6.4 fusion.405
  2055.4 11.2 rev.46
  2081.5 6.4 fusion.405
  2155.0 11.2 rev.46
  2181.2 6.4 fusion.405
  2254.7 11.2 rev.46
  2280.8 6.4 fusion.405
  2354.3 11.2 rev.46
  2380.4 6.4 fusion.405
  2454.0 11.2 rev.46
  2480.1 6.4 fusion.405
  2553.6 11.2 rev.46
  2579.7 6.4 fusion.405
  2660.5 9.1 all-reduce.7
  2672.3 8.2 all-gather.19.cloned.1.call-done
  2680.6 28.5 all-gather.21.cloned.1.call-done
  2709.2 27.5 while.114
  2740.3 201.4 %while.118 = (s32[]{:T(128)}, f32[16,4,96,32]{2,1,3,0:T(4,128)S(1)}, f32[16,32,64]{2,1,0:T(8,128)}, f32[16,4,32,64]{3,1,2,0:T(4,128)}, f32[16,32,64]{2,1,0:T(8,1...) while((s32[]{:T(128)}, f32[16,4,96,32]{2,1,3,0:T(4,128)S(1)}, ...), condition=%wide.region_24.25_spmd.clone.clone.clone, body=%wide.region_23.24_spmd.clone.clone.sunk.clone | while | flops 20117600 | bytes 609117 | solution.py:364
  2945.7 16.5 all-reduce.13
  2962.6 15.7 all-reduce.14
  (1366 shorter events, 2328.9 us)
Async XLA Ops:
  7.2 26.8 copy-start.28
  7.2 647.7 %all-gather.11.cloned.1.call-start = ((), (), s32[]{:S(2)}) async-start(), calls=%async_computation.6 | async-start | bytes 2621440 | tf_op jit(solution)/shard_map/all_gather | solution.py:12
  7.3 42.0 %copy-start.29 = (f32[64,64]{1,0:T(8,128)S(1)}, f32[64,64]{1,0:T(8,128)}, u32[]{:S(2)}) copy-start(f32[64,64]{1,0:T(8,128)} %param.30) | copy-start | bytes 49156
  8.6 83.4 %copy-start.1 = (bf16[4,96,512]{1,2,0:T(8,128)(2,1)}, bf16[4,96,512]{1,2,0:T(8,128)(2,1)S(1)}, u32[]{:S(2)}) copy-start(bf16[4,96,512]{1,2,0:T(8,128)(2,1)S(1)} %copy.122) | copy-start | bytes 1179652
  8.6 54.9 %copy-start.30 = (f32[64,64]{1,0:T(8,128)S(1)}, f32[64,64]{1,0:T(8,128)}, u32[]{:S(2)}) copy-start(f32[64,64]{1,0:T(8,128)} %param.31) | copy-start | bytes 49156
  8.6 69.1 %copy-start.31 = (f32[64,64]{1,0:T(8,128)S(1)}, f32[64,64]{1,0:T(8,128)}, u32[]{:S(2)}) copy-start(f32[64,64]{1,0:T(8,128)} %param.29) | copy-start | bytes 49156
  8.9 4.6 copy-start.32
  63.5 31.6 %copy-start.21 = (f32[512,64]{1,0:T(8,128)}, f32[512,64]{1,0:T(8,128)S(1)}, u32[]{:S(2)}) copy-start(f32[512,64]{1,0:T(8,128)S(1)} %all_gather.56) | copy-start | bytes 393220
  77.7 17.4 copy-start.22
  114.0 4.6 copy-start
  146.7 4.6 copy-start
  179.5 4.6 copy-start
  212.2 4.6 copy-start
  244.9 4.6 copy-start
  277.6 4.6 copy-start
  310.3 4.6 copy-start
  343.0 4.6 copy-start
  375.7 4.6 copy-start
  408.4 4.6 copy-start
  441.1 4.6 copy-start
  473.8 4.6 copy-start
  506.6 4.6 copy-start
  539.3 4.6 copy-start
  572.0 4.6 copy-start
  604.7 4.6 copy-start
  618.5 2.6 copy-start.23
  618.5 3.8 copy-start.24
  621.1 71.0 %all-gather.13.cloned.1.call-start = ((), (), s32[]{:S(2)}) async-start(), calls=%async_computation.7 | async-start | bytes 2621440 | tf_op jit(solution)/shard_map/all_gather | solution.py:12
  621.1 2.5 copy-start.25
  622.3 107.0 %all-gather.15.cloned.1.call-start = ((), (), s32[]{:S(2)}) async-start(), calls=%async_computation.8 | async-start | bytes 2621440 | tf_op jit(solution)/shard_map/all_gather | solution.py:12
  622.4 2.5 copy-start.27
  623.6 3.4 copy-start.35
  623.6 14.8 copy-start.34
  623.6 23.6 copy-start.26
  623.6 142.7 %all-gather.9.cloned.1.call-start = ((), (), s32[]{:S(2)}) async-start(), calls=%async_computation.5 | async-start | bytes 2621440 | tf_op jit(solution)/shard_map/all_gather | solution.py:12
  624.8 402.1 %all-gather.17.cloned.1.call-start = ((), (), s32[]{:S(2)}) async-start(), calls=%async_computation.9 | async-start | bytes 1179648 | tf_op jit(solution)/shard_map/all_gather | solution.py:136
  625.6 2055.0 %all-gather.19.cloned.1.call-start = ((), (), s32[]{:S(2)}) async-start(), calls=%async_computation.10 | async-start | bytes 1310720 | tf_op jit(solution)/shard_map/all_gather | solution.py:29
  647.4 118.9 %copy-start.11 = (bf16[4,96,512]{1,2,0:T(8,128)(2,1)}, bf16[4,96,512]{1,2,0:T(8,128)(2,1)S(1)}, u32[]{:S(2)}) copy-start(bf16[4,96,512]{1,2,0:T(8,128)(2,1)S(1)} %copy.141) | copy-start | bytes 1179652
  823.5 201.4 %copy-start.14 = (f32[16,4,96,32]{2,1,3,0:T(4,128)S(1)}, f32[16,4,96,32]{2,1,3,0:T(4,128)}, u32[]{:S(2)}) copy-start(f32[16,4,96,32]{2,1,3,0:T(4,128)} %get-tuple-element.815) | copy-start | bytes 2359300
  1024.9 1.0 copy-start.2
  1025.3 1.6 copy-start.10
  1026.9 0.7 copy-start.17
  1029.4 2.5 copy-start.15
  1031.9 1.5 copy-start.6
  1031.9 1.5 copy-start.8
  1033.4 6.1 copy-start.4
  1033.4 6.1 copy-start.5
  2651.5 4.3 copy-start.7
  2651.5 4.3 copy-start.9
  2651.5 4.3 copy-start.18
  2653.7 55.4 %all-gather.21.cloned.1.call-start = ((), (), s32[]{:S(2)}) async-start(), calls=%async_computation.11 | async-start | bytes 1310720 | tf_op jit(solution)/shard_map/all_gather | solution.py:29
  2655.7 15.1 copy-start.19
  2655.8 288.4 %reduce-scatter.6.cloned.1.call-start = ((), (), s32[]{:S(2)}) async-start(), calls=%async_computation.12 | async-start | bytes 1179648 | tf_op jit(solution)/shard_map/reduce_scatter | solution.py:383
  2657.6 305.0 %reduce-scatter.10.cloned.1.call-start = ((), (), s32[]{:S(2)}) async-start(), calls=%async_computation.15 | async-start | bytes 147456 | tf_op jit(solution)/shard_map/reduce_scatter | solution.py:392
  2658.3 304.2 %reduce-scatter.12.cloned.1.call-start = ((), (), s32[]{:S(2)}) async-start(), calls=%async_computation.16 | async-start | bytes 147456 | tf_op jit(solution)/shard_map/reduce_scatter | solution.py:395
  2658.9 303.7 %reduce-scatter.14.cloned.1.call-start = ((), (), s32[]{:S(2)}) async-start(), calls=%async_computation.17 | async-start | bytes 147456 | tf_op jit(solution)/shard_map/reduce_scatter | solution.py:398
  2659.7 302.9 %reduce-scatter.8.cloned.1.call-start = ((), (), s32[]{:S(2)}) async-start(), calls=%async_computation.14 | async-start | bytes 147456 | tf_op jit(solution)/shard_map/reduce_scatter | solution.py:389
  2672.3 314.5 %all-reduce.17.cloned.1.call-start = ((), (), s32[]{:S(2)}) async-start(), calls=%async_computation.13 | async-start | bytes 262144 | tf_op jit(solution)/shard_map/psum | solution.py:412
  2740.3 201.4 %copy-start.13 = (f32[16,4,96,32]{2,1,3,0:T(4,128)S(1)}, f32[16,4,96,32]{2,1,3,0:T(4,128)}, u32[]{:S(2)}) copy-start(f32[16,4,96,32]{2,1,3,0:T(4,128)} %get-tuple-element.825) | copy-start | bytes 2359300
  2941.7 1.0 copy-start.3
  2941.7 1.2 copy-start.20
  2942.9 0.7 copy-start.33
  2942.9 1.3 copy-start.12
  2942.9 1.4 copy-start.16
Sparse Core Ops, SparseCore 0:
  621.2 33.6 all-gather.10
  656.7 35.2 all-gather.12
  693.9 35.2 all-gather.14
  731.0 35.2 all-gather.8
  767.8 22.0 all-gather.16
  2653.8 26.7 all-gather.18
  2682.4 26.6 all-gather.20
  2711.4 32.3 reduce-scatter.5
  2746.0 28.3 reduce-scatter.9
  2776.6 28.2 reduce-scatter.11
  2807.1 28.2 reduce-scatter.13
  2837.6 28.2 reduce-scatter.7
  2944.3 41.0 all-reduce.16
where the time goes:
time: 3030 us; the launch traced here: 3000 us
  matrix products  1500 us (50%)
  local copies, waits for them, and re-layouts  812 us (27%)
  other arithmetic  355 us (12%)
  waiting for transfers between devices  155 us (5%)
  blocking collectives  136 us (4%)
    dot_general x192, matrix products, split_product(): jnp.einsum(form, rest_part, data, preferred_element_type=jnp.float32)  613 us
    dot_general x192, matrix products, split_product(): jnp.einsum(form, high_part, data, preferred_element_type=jnp.float32)  510 us
    rev x16, local copies, waits for them, and re-layouts, lag_sums(): outer_prod[:, :, ::-1]  180 us
    reshape x32, local copies, waits for them, and re-layouts, lower_toeplitz(): return repeated.reshape(chans, count, 2 * count - 1)[:, :, :count]  177 us
    all_gather x4, waiting for transfers between devices, carried_in(): pieces = jax.tree.map(lambda part: lax.all_gather(part, axis), value)  116 us
    reduce_sum x16, other arithmetic, local_backward(): one_im = jnp.sum(pow_im * corr[:, None, :], axis=2)  102 us
    mul x16, other arithmetic, powers(): return (magnitude * jnp.cos(phase), magnitude * jnp.sin(phase))  93.6 us
    dot_general x16, matrix products, cross_backward(): jnp.einsum('hnj,zhn->zjh', tail_im, mix_im, precision=HIGH)  89.5 us
  transfers between devices with their start and end apart: 13, of which 6 were waited for; matrix products, arithmetic and copies ran while one was open for 17% of the time, Pallas kernels for 0%

commit v1 on v0

v1 whole, which is shorter than its diff:
```python
import functools
import math

import jax
import jax.numpy as jnp
from jax import lax
from jax.experimental import pallas as pl
from jax.experimental.pallas import tpu as pltpu
from jax.sharding import PartitionSpec as P

EPSILON = 1e-05
LANES = 128
BOTH = ("shard", "ctx")
F32 = jnp.float32
BF16 = jnp.bfloat16
VMEM = pl.BlockSpec(memory_space=pltpu.VMEM)
SMEM = pl.BlockSpec(memory_space=pltpu.SMEM)
PARAMS = pltpu.CompilerParams(vmem_limit_bytes=56 * 1024 * 1024)


class Plan:
    def __init__(self, shards, chunks):
        layers = shards // 2
        self.shards, self.chunks = shards, chunks
        self.subs = subs = chunks // layers
        self.order = [
            (core, top * subs + sub)
            for top in range(chunks // subs)
            for core in range(2)
            for sub in range(subs)
        ]
        self.groups = [
            [(2 * z + core) * chunks + c for core, c in self.order] for z in range(layers)
        ]
        members = [(z, core, c) for z in range(layers) for core, c in self.order]

        def here(z, core, c):
            return (2 * z + core) * chunks + c

        def owner(z, core, c, turn):
            place = (z * subs + c % subs + turn) % chunks
            return (2 * (c // subs) + core) * chunks + place

        self.fetch = [(owner(*m, 0), here(*m)) for m in members]
        self.give = [[(here(*m), owner(*m, turn)) for m in members] for turn in range(chunks)]
        self.rotate = [
            [(a, (a + turn) % chunks) for a in range(chunks)] for turn in range(1, chunks)
        ]


def row_stats(rows):
    mean = jnp.mean(rows, axis=-1, keepdims=True)
    centered = rows - mean
    var = jnp.mean(centered * centered, axis=-1, keepdims=True)
    inv = lax.rsqrt(var + EPSILON)
    return centered * inv, inv


def dot(a, b, over):
    return lax.dot_general(a, b, (((over[0],), (over[1],)), ((), ())), preferred_element_type=F32)


def norm_kernel(counts, tokens, out):
    seqs, rows, width = tokens.shape
    blocks, _, chans, _ = out.shape
    pad = LANES - rows
    last = lax.broadcasted_iota(jnp.int32, (pad, width), 0) == pad - 1
    for n in range(seqs):
        xhat, _ = row_stats(tokens[n].astype(F32))
        tail = jnp.where(last, counts[n].astype(F32), 0.0)
        full = jnp.concatenate([xhat, tail], axis=0)
        out[:, n] = full.T.astype(BF16).reshape(blocks, chans, LANES)


def table_kernel(chunks, rows, pack, table, edge, taps):
    chans = pack.shape[0]
    low = lax.broadcasted_iota(jnp.int32, (1, 1, LANES), 2) < LANES // 2
    turn = jnp.where(low, 0.0, math.pi / 2)
    step = 8

    def spread(pair):
        other = pltpu.roll(pair, LANES // 2, 1)
        flag = low[0]
        return jnp.where(flag, pair, other), jnp.where(flag, other, pair)

    def complex_times(values, factor):
        other = pltpu.roll(factor, LANES // 2, 2)
        same = jnp.where(low, factor, other)
        cross = jnp.where(low, -other, factor)
        return values * same + pltpu.roll(values, LANES // 2, 2) * cross

    offsets = lax.broadcasted_iota(jnp.int32, (1, step, 1), 1).astype(F32)
    row_at = lax.broadcasted_iota(jnp.int32, (1, 2 * chunks, 1), 1)
    starts = jnp.where(row_at < chunks, rows * row_at, rows * (row_at - chunks) - LANES).astype(F32)

    def block(at, _):
        here = pl.ds(at * step, step)
        decay, freq = spread(pack[here, 0:LANES])
        real, imag = spread(pack[here, LANES : 2 * LANES])
        decay, freq = decay[:, None, :], freq[:, None, :]

        def power(by):
            return jnp.exp(-decay * by) * jnp.cos(freq * by - turn)

        part = power(offsets)
        table[here, 0:step] = part.astype(BF16)
        size = step
        while size < LANES:
            new = complex_times(part, power(jnp.full((1, 1, 1), float(size), F32)))
            table[here, size : 2 * size] = new.astype(BF16)
            part = jnp.concatenate([part, new], axis=1)
            size *= 2
        edges = power(starts)
        edge[here] = edges
        hat_same = jnp.where(low, real[:, None, :], -real[:, None, :])
        mix = hat_same * edges - imag[:, None, :] * pltpu.roll(edges, LANES // 2, 2)
        mix = jnp.where(row_at == chunks, 0.0, mix).astype(BF16)
        whole = part.astype(BF16)
        for k in range(step):
            taps[at * step + k] = dot(mix[k], whole[k], (1, 1))
        return 0

    lax.fori_loop(0, chans // step, block, 0)


def toeplitz(chunks, rows, taps):
    lane = lax.broadcasted_iota(jnp.int32, (rows, LANES), 1)
    row = lax.broadcasted_iota(jnp.int32, (rows, LANES), 0)
    upper = lane >= row

    def sheared(at):
        wide = jnp.broadcast_to(taps[at : at + 1], (rows, LANES))
        return pltpu.roll(wide, 0, 1, stride=1, stride_axis=0)

    slots = []
    for d in range(chunks):
        below = sheared(chunks + d) if d else 0.0
        slots.append(jnp.where(upper, sheared(d), below).astype(BF16))
    body = jnp.concatenate(slots, axis=1)
    return jnp.concatenate([body, jnp.zeros((LANES - rows, chunks * LANES), BF16)], axis=0)


def place(order, seqs, block, n):
    core, c = order[block]
    return (c * 2 + core) * seqs + n


def forward_kernel(chunks, rows, order, arrived, pack, taps, hidden, mixed, inputs, result, local):
    blocks, seqs, chans, _ = arrived.shape
    local[...] = pack[:, 2 * LANES :]
    total = blocks * seqs
    each = 2 * seqs
    lane = lax.broadcasted_iota(jnp.int32, (chans, LANES), 1).astype(F32)
    gain, shift = pack[:, 257:258], pack[:, 258:259]
    for b in range(blocks):
        for n in range(seqs):
            xhat = arrived[b, n].astype(F32)
            x = jnp.where(lane < xhat[:, LANES - 1 :], xhat * gain + shift, 0.0)
            inputs[pl.ds(place(order, seqs, b, n) * chans, chans), :] = x.astype(BF16).astype(F32)

    def channel(h, _):
        x = inputs[pl.ds(h, total, stride=chans), :]
        weights = toeplitz(chunks, rows, taps[h])
        out = dot(x.astype(BF16), weights, (1, 0))
        parts = []
        for d in range(chunks):
            part = out[0:each, d * LANES : (d + 1) * LANES]
            for c in range(1, d + 1):
                part += out[each * c : each * (c + 1), (d - c) * LANES : (d - c + 1) * LANES]
            parts.append(part)
        mix = jnp.concatenate(parts, axis=0) + local[pl.ds(h, 1), :][:, 0:1] * x
        mixed[h] = mix
        result[pl.ds(h, total, stride=chans), :] = jax.nn.gelu(mix)
        return 0

    lax.fori_loop(0, chans, channel, 0)
    for b in range(blocks):
        for n in range(seqs):
            at = place(order, seqs, b, n) * chans
            hidden[b, n] = result[pl.ds(at, chans), :].astype(BF16)


def glu_kernel(counts, arrived, weights, bias, tokens, cotangent, block_out, leaving, grads):
    seqs, rows, width = tokens.shape
    blocks, _, chans, _ = arrived.shape
    shards, own = weights.shape[0], width // weights.shape[0]
    w = weights[:, 0:own].reshape(width, 2 * width)
    position = lax.broadcasted_iota(jnp.int32, (rows, width), 0)
    sides, outers = [], []
    bias_sum = jnp.zeros((1, 2 * width), F32)
    for n in range(seqs):
        side = arrived[:, n].reshape(width, LANES)
        hidden = side.astype(F32).T.astype(BF16)
        proj = dot(hidden, w, (1, 0)) + bias[...]
        r, q = proj[0:rows, :width], proj[0:rows, width:]
        valid = jnp.where(position < counts[n], 1.0, 0.0)
        open_ = jax.nn.sigmoid(q)
        block_out[n] = (tokens[n].astype(F32) + valid * (r * open_)).astype(BF16)
        e = valid * cotangent[n].astype(F32)
        first = e * open_
        both = jnp.concatenate([first, first * r * (1.0 - open_)], axis=1).astype(BF16)
        bias_sum += jnp.sum(both.astype(F32), axis=0, keepdims=True)
        both = jnp.concatenate([both, jnp.zeros((LANES - rows, 2 * width), BF16)], axis=0)
        back = dot(both, w, (1, 1))
        leaving[:, n] = back.T.astype(BF16).reshape(blocks, chans, LANES)
        sides.append(side)
        outers.append(both)
    outer = dot(jnp.concatenate(sides, axis=1), jnp.concatenate(outers, axis=0), (1, 0))
    grads[:, 0:own] = outer.astype(BF16).reshape(shards, own, 2 * width)
    extra = grads.shape[1] - own
    tail = jnp.broadcast_to(bias_sum, (extra, 2 * width)).astype(BF16)
    for s in range(shards):
        grads[s, own:] = tail


def gelu_slope(x):
    c = math.sqrt(2.0 / math.pi)
    t = jnp.tanh(c * (x + 0.044715 * x * x * x))
    return 0.5 * (1.0 + t) + 0.5 * x * (1.0 - t * t) * (c * (1.0 + 3.0 * 0.044715 * x * x))


def backward_kernel(
    chunks, rows, order, arrived, first, pack, table, edge, taps, mixed,
    leaving, sums, normal, inputs, mirrored, grads, result, masks, local, ones, twos, skips, gains, shifts,
):
    blocks, seqs, chans, _ = arrived.shape
    local[...] = pack[:, 2 * LANES :]
    total = blocks * seqs
    each = 2 * seqs
    lane_row = lax.broadcasted_iota(jnp.int32, (1, LANES), 1).astype(F32)
    lane_all = lax.broadcasted_iota(jnp.int32, (chans, LANES), 1).astype(F32)
    gain_all, shift_all = pack[:, 257:258], pack[:, 258:259]
    square = (LANES, LANES)
    reach = lax.broadcasted_iota(jnp.int32, square, 0) + lax.broadcasted_iota(jnp.int32, square, 1)
    mirror = jnp.where(reach == rows - 1, 1.0, 0.0).astype(BF16)
    for b in range(blocks):
        for n in range(seqs):
            r = place(order, seqs, b, n)
            here = pl.ds(r * chans, chans)
            xhat = first[b, n].astype(F32)
            x = jnp.where(lane_all < xhat[:, LANES - 1 :], xhat * gain_all + shift_all, 0.0).astype(BF16)
            inputs[here, :] = x.astype(F32)
            mirrored[here, :] = dot(x, mirror, (1, 0))
            normal[here, :] = xhat
            grads[here, :] = arrived[b, n].astype(F32)
            masks[r : r + 1, :] = jnp.where(lane_row < xhat[0:1, LANES - 1 :], 1.0, 0.0)
    low = lax.broadcasted_iota(jnp.int32, (1, LANES), 1) < LANES // 2
    lane = lax.broadcasted_iota(jnp.int32, (rows, LANES), 1)
    row = lax.broadcasted_iota(jnp.int32, (rows, LANES), 0)
    upper = lane <= LANES - rows + row
    row_at = lax.broadcasted_iota(jnp.int32, (2 * chunks, 1), 0)
    starts = jnp.where(row_at < chunks, rows * row_at, rows * (row_at - chunks) - LANES).astype(F32)
    lags = starts + lane_row

    def channel(h, _):
        xhat = normal[pl.ds(h, total, stride=chans), :]
        valid = masks[...]
        vectors = local[pl.ds(h, 1), :]
        skip, gain = vectors[:, 0:1], vectors[:, 1:2]
        x = inputs[pl.ds(h, total, stride=chans), :]
        x_mirrored = mirrored[pl.ds(h, total, stride=chans), :].astype(BF16)
        back = grads[pl.ds(h, total, stride=chans), :]
        g = (back * gelu_slope(mixed[h])).astype(BF16).astype(F32)
        weights = toeplitz(chunks, rows, taps[h])
        empty = jnp.zeros((each, LANES), F32)
        ahead = jnp.concatenate(
            [
                jnp.concatenate(
                    [g[each * (c + d) : each * (c + d + 1)] if c + d < chunks else empty for d in range(chunks)],
                    axis=1,
                )
                for c in range(chunks)
            ],
            axis=0,
        ).astype(BF16)
        m = valid * (dot(ahead, weights, (1, 1)) + skip * g)
        result[pl.ds(h, total, stride=chans), :] = gain * m
        here = pl.ds(h, 1)
        skips[here, :] = jnp.sum(g * x, axis=0, keepdims=True)
        gains[here, :] = jnp.sum(m * xhat, axis=0, keepdims=True)
        shifts[here, :] = jnp.sum(m, axis=0, keepdims=True)
        outer = dot(x_mirrored, ahead, (0, 0))
        above, below = [], []
        for d in range(chunks):
            slid = pltpu.roll(
                outer[0:rows, d * LANES : (d + 1) * LANES],
                LANES - rows + 1, 1, stride=1, stride_axis=0,
            )
            above.append(jnp.sum(jnp.where(upper, slid, 0.0), axis=0, keepdims=True))
            if d:
                below.append(jnp.sum(jnp.where(upper, 0.0, slid), axis=0, keepdims=True))
        corr = jnp.concatenate(above + [jnp.zeros((1, LANES), F32)] + below, axis=0)
        both = jnp.concatenate([corr, corr * lags], axis=0).astype(BF16)
        turned = dot(both, table[h], (1, 0))
        factor = edge[h]
        other = pltpu.roll(factor, LANES // 2, 1)
        same = jnp.where(low, factor, other)
        cross = jnp.where(low, -other, factor)
        for k, into in enumerate((ones, twos)):
            part = turned[2 * chunks * k : 2 * chunks * (k + 1)]
            full = part * same + pltpu.roll(part, LANES // 2, 1) * cross
            into[here, :] = jnp.sum(full, axis=0, keepdims=True)
        return 0

    lax.fori_loop(0, chans, channel, 0)
    for b in range(blocks):
        for n in range(seqs):
            at = place(order, seqs, b, n) * chans
            leaving[b, n] = result[pl.ds(at, chans), :].astype(BF16)
    at = lax.broadcasted_iota(jnp.int32, (chans, LANES), 1)
    tail = jnp.zeros((chans, LANES), F32)
    for k, part in enumerate((skips, gains, shifts)):
        tail = jnp.where(at == k, jnp.sum(part[...], axis=1, keepdims=True), tail)
    sums[:, 0:LANES] = ones[...]
    sums[:, LANES : 2 * LANES] = twos[...]
    sums[:, 2 * LANES :] = tail


def final_kernel(arrived, tokens, cotangent, out):
    seqs, rows, width = tokens.shape
    for n in range(seqs):
        d = arrived[:, n].reshape(width, LANES).astype(F32).T[0:rows]
        xhat, inv = row_stats(tokens[n].astype(F32))
        mean = jnp.mean(d, axis=-1, keepdims=True)
        along = jnp.mean(d * xhat, axis=-1, keepdims=True)
        grad = (d - mean - xhat * along) * inv
        out[n] = (cotangent[n].astype(F32) + grad).astype(BF16)


def call(kernel, outs, ins, scratch=()):
    return pl.pallas_call(
        kernel,
        out_shape=[jax.ShapeDtypeStruct(*o) for o in outs],
        in_specs=ins,
        out_specs=[VMEM] * len(outs),
        scratch_shapes=list(scratch),
        compiler_params=PARAMS,
    )


def in_order(received, mine):
    count = len(received)
    twice = jnp.stack(received[::-1] * 2)
    parts = lax.dynamic_slice_in_dim(twice, count - 1 - mine, count, 0).astype(F32)
    return [parts[k] for k in range(count)]


def per_device(
    plan, tokens, lengths, out_weight, out_bias, decay_rate, frequency, coef_real, coef_imag,
    skip, gain, shift, cotangent,
):
    seqs, rows, width = tokens.shape
    chunks, subs = plan.chunks, plan.subs
    blocks = 2 * chunks
    chans = width // blocks
    own, states = decay_rate.shape
    total = blocks * seqs
    mine = lax.axis_index("ctx")
    counts = jnp.clip(lengths - mine * rows, 0, rows).astype(jnp.int32)

    def exchange(buffer):
        return lax.all_to_all(buffer, BOTH, 0, 0, axis_index_groups=plan.groups, tiled=True)

    scale = jnp.sqrt(-jnp.expm1(-2.0 * decay_rate))
    pack = jnp.concatenate(
        [decay_rate, frequency, scale * coef_real, scale * coef_imag]
        + [v[:, None] for v in (skip, gain, shift)]
        + [jnp.zeros((own, LANES - 3), F32)],
        axis=1,
    )
    sub = lax.rem(mine, subs)
    pack = lax.dynamic_slice_in_dim(pack, sub * chans, chans, 0)
    pack = lax.ppermute(pack, BOTH, plan.fetch)
    bias_row = jnp.pad(out_bias[None, :], ((0, 15), (0, 2 * width - out_bias.shape[0])))
    weights = jnp.concatenate([out_weight, bias_row], axis=0).astype(BF16)
    weights = lax.all_gather(weights, "shard")
    bias = weights[:, own, : out_bias.shape[0]].reshape(1, 2 * width).astype(F32)

    wire = ((blocks, seqs, chans, LANES), BF16)
    (first,) = call(norm_kernel, [wire], [SMEM, VMEM])(counts, tokens)
    table, edge, taps = call(
        functools.partial(table_kernel, chunks, rows),
        [
            ((chans, LANES, LANES), BF16),
            ((chans, 2 * chunks, LANES), F32),
            ((chans, 2 * chunks, LANES), F32),
        ],
        [VMEM],
    )(pack)
    first = exchange(first)
    flat = pltpu.VMEM((total * chans, LANES), F32)
    line = pltpu.VMEM((chans, LANES), F32)
    hidden, mixed = call(
        functools.partial(forward_kernel, chunks, rows, plan.order),
        [wire, ((chans, total, LANES), F32)],
        [VMEM] * 3,
        [flat, flat, line],
    )(first, pack, taps)
    hidden = exchange(hidden)
    block_out, back, grads = call(
        glu_kernel,
        [(tokens.shape, BF16), wire, ((plan.shards, own + 16, 2 * width), BF16)],
        [SMEM] + [VMEM] * 5,
    )(counts, hidden, weights, bias, tokens, cotangent)
    back = exchange(back)
    owned = lax.psum_scatter(
        grads.reshape(plan.shards * (own + 16), 2 * width), "shard", scatter_dimension=0, tiled=True
    )
    leaving, sums = call(
        functools.partial(backward_kernel, chunks, rows, plan.order),
        [wire, ((chans, 3 * LANES), F32)],
        [VMEM] * 7,
        [
            flat, flat, flat, flat, flat, pltpu.VMEM((total, LANES), F32),
            line, line, line, line, line, line,
        ],
    )(back, first, pack, table, edge, taps, mixed)
    leaving = exchange(leaving)
    (tokens_grad,) = call(final_kernel, [(tokens.shape, BF16)], [VMEM] * 3)(
        leaving, tokens, cotangent
    )

    parts = in_order([lax.ppermute(sums, BOTH, route) for route in plan.give], mine)
    totals = jnp.concatenate([sum(parts[j::subs][1:], parts[j]) for j in range(subs)], axis=0)
    one_re, one_im, two_re, two_im = (totals[:, k * states : (k + 1) * states] for k in range(4))
    hat_re, hat_im = scale * coef_real, scale * coef_imag
    grad_decay = -(hat_re * two_re - hat_im * two_im) + jnp.exp(-2.0 * decay_rate) / scale * (
        coef_real * one_re - coef_imag * one_im
    )
    grad_freq = -(hat_re * two_im + hat_im * two_re)

    parts = in_order([owned] + [lax.ppermute(owned, "ctx", route) for route in plan.rotate], mine)
    whole = sum(parts[1:], parts[0])
    segment = out_bias.shape[0]
    grad_bias = lax.dynamic_slice_in_dim(whole[own], lax.axis_index("shard") * segment, segment, 0)
    return (
        block_out,
        tokens_grad,
        whole[:own],
        grad_bias,
        grad_decay,
        grad_freq,
        scale * one_re,
        -scale * one_im,
        totals[:, 4 * states],
        totals[:, 4 * states + 1],
        totals[:, 4 * states + 2],
    )


def solution(mesh):
    plan = Plan(mesh.shape["shard"], mesh.shape["ctx"])
    rows = P("shard", "ctx", None)
    matrix = P("shard", None)
    vector = P("shard")
    in_specs = (rows, vector, matrix, vector) + (matrix,) * 4 + (vector,) * 3 + (rows,)
    out_specs = (rows, rows, matrix, vector) + (matrix,) * 4 + (vector,) * 3
    return jax.shard_map(
        functools.partial(per_device, plan),
        mesh=mesh,
        in_specs=in_specs,
        out_specs=out_specs,
        check_vma=False,
    )
```

time: 3030 us -> 192 us (0.06); the launches traced: 3000 us -> 191 us
  matrix products: 1500 us -> 0 us
  local copies, waits for them, and re-layouts: 812 us -> 6.68 us
  other arithmetic: 355 us -> 5.82 us
  waiting for transfers between devices: 155 us -> 24.5 us
  blocking collectives: 136 us -> 12.8 us
  Pallas kernels: 0 us -> 79.3 us
  starting transfers between devices: 0.78 us -> 47.3 us
    dot_general x467 -> x0, matrix products: 1500 us -> none  [the longest x192 613 us: split_product(): jnp.einsum(form, rest_part, data, preferred_element_type=jnp.float32)]
    reshape x66 -> x0, local copies, waits for them, and re-layouts: 304 us -> none  [the longest x32 177 us: lower_toeplitz(): return repeated.reshape(chans, count, 2 * count - 1)[:, :, :count]]
    rev x96 -> x0, local copies, waits for them, and re-layouts: 217 us -> none  [the longest x16 180 us: lag_sums(): outer_prod[:, :, ::-1]]
    all_gather x7 -> x1, waiting for transfers between devices: 152 us -> 0.02 us  [per_device(): weights = lax.all_gather(weights, 'shard')]
    mul x87 -> x2, other arithmetic: 149 us -> 0.76 us  [the longest x1 0.72 us: per_device(): -scale * one_im]
    reduce_sum x38 -> x0, other arithmetic: 132 us -> none  [the longest x16 102 us: local_backward(): one_im = jnp.sum(pow_im * corr[:, None, :], axis=2)]
    another operation x104 -> x2, local copies, waits for them, and re-layouts: 90.2 us -> 0.02 us  [in_order(): twice = jnp.stack(received[::-1] * 2)]
    pallas_call x0 -> x6, Pallas kernels: none -> 79.3 us  [the longest x1 37.6 us: per_device(): call(functools.partial(backward_kernel, chunks, rows, plan.order), [wire,...]
  transfers between devices with their start and end apart: 13 -> 13, of which waited for: 6 -> 3; matrix products, arithmetic and copies ran while one was open for 17% -> 2% of each run, Pallas kernels for 0% -> 38%
where the time goes in v1:
time: 192 us; the launch traced here: 191 us
  Pallas kernels  79.3 us (41%)
  starting transfers between devices  47.3 us (25%)
  waiting for transfers between devices  24.5 us (13%)
  between operations  14.4 us (8%)
  blocking collectives  12.8 us (7%)
  local copies, waits for them, and re-layouts  6.68 us (3%)
  other arithmetic  5.82 us (3%)
    pallas_call x1, Pallas kernels, per_device(): call(functools.partial(backward_kernel, chunks, rows, plan.order), [wire,...  37.6 us
    all_to_all x3, starting transfers between devices, exchange(): lax.all_to_all(buffer, BOTH, 0, 0, axis_index_groups=plan.groups, tiled=T...  32.1 us
    pallas_call x1, Pallas kernels, per_device(): call(functools.partial(forward_kernel, chunks, rows, plan.order), [wire,...  20 us
    all_to_all x1, blocking collectives, exchange(): lax.all_to_all(buffer, BOTH, 0, 0, axis_index_groups=plan.groups, tiled=T...  12.8 us
    pallas_call x1, Pallas kernels, per_device(): call(functools.partial(table_kernel, chunks, rows), [((chans, LANES, LANE...  10.4 us
    ppermute x4, waiting for transfers between devices, per_device(): lax.ppermute(sums, BOTH, route)  9.23 us
    all_to_all x3, waiting for transfers between devices, exchange(): lax.all_to_all(buffer, BOTH, 0, 0, axis_index_groups=plan.groups, tiled=T...  8.37 us
    ppermute x3, starting transfers between devices, per_device(): lax.ppermute(owned, 'ctx', route)  8.26 us
  transfers between devices with their start and end apart: 13, of which 3 were waited for; matrix products, arithmetic and copies ran while one was open for 2% of the time, Pallas kernels for 38%

profile of v1, /device:TPU:0, one launch (start us, length us, event | category | flops | bytes accessed | tf_op | source)
XLA Modules:
  0.0 190.8 jit_solution(1309520933413495083)
XLA Ops:
  7.2 0.0 all-gather.2.cloned.1.call-start
  7.2 1.0 convert_bitcast_fusion
  8.2 0.0 copy-start.10
  8.2 0.0 copy-start.11
  8.2 0.0 copy-start.12
  8.2 0.0 copy-start.6
  8.2 0.0 copy-start.7
  8.3 0.0 copy-start.8
  8.3 0.7 convert_bitcast_fusion.1
  9.0 0.7 pad_maximum_fusion
  9.6 0.0 all-gather.2.cloned.1.call-update
  9.7 1.2 subtract_clamp_fusion.counts
  10.8 2.4 %shard_map.203 = bf16[8,4,64,128]{3,2,1,0:T(8,128)(2,1)} custom-call(s32[4]{0:T(128)} %subtract_clamp_fusion.counts, bf16[4,96,512]{2,1,0:T(8,128)(2,1)} %tokens.5), custom_call_target="tpu_custom_call" | custom-call | tf_op jit(solution)/shard_map/pallas_call | solution.py:380
  13.2 5.2 %all-to-all-start = ((bf16[8,4,64,128]{3,2,1,0:T(8,128)(2,1)}), bf16[8,4,64,128]{3,2,1,0:T(8,128)(2,1)S(1)}, u32[]{:S(2)}, u32[]{:S(2)}) async-start(bf16[8,4,64,128]{3,2,1,0:T(8,128)(2,1)} %shard_map.203), calls=%async_computation | async-start | bytes 1048576 | tf_op jit(solution)/shard_map/all_to_all | solution.py:362
  18.4 0.1 copy.29
  18.5 0.0 copy-done.11
  18.5 0.1 copy.30
  18.6 0.0 copy-done.12
  18.6 0.1 copy.31
  18.8 0.1 concatenate.18
  18.9 0.7 collective-permute-start
  19.6 0.0 collective-permute-done.pack
  19.6 0.0 copy-start.3
  19.6 0.6 copy-done.3
  20.2 10.4 %shard_map.204 = (bf16[64,128,128]{2,1,0:T(8,128)(2,1)}, f32[64,8,128]{2,1,0:T(8,128)}, f32[64,8,128]{2,1,0:T(8,128)}) custom-call(f32[64,384]{1,0:T(8,128)} %copy-done.3), custom_call_target="tpu_custom_call" | custom-call | tf_op jit(solution)/shard_map/pallas_call | solution.py:381
  30.6 0.0 all-to-all-done.arrived.first
  30.6 0.8 copy-done
  31.4 20.0 %shard_map.205 = (bf16[8,4,64,128]{3,2,1,0:T(8,128)(2,1)}, f32[64,32,128]{2,1,0:T(8,128)}) custom-call(bf16[8,4,64,128]{3,2,1,0:T(8,128)(2,1)} %copy-done, f32[64,384]{1,0:T(8,128)} %copy-done.3, f32[64,8,128]{2,1,0:T(8,128)} %get-tuple-element.21.taps), custom_call_target="tpu_custom_call" | custom-call | tf_op jit(solution)/shard_map/pallas_call | solution.py:393
  51.4 19.9 %all-to-all-start.1 = ((bf16[8,4,64,128]{3,2,1,0:T(8,128)(2,1)}), bf16[8,4,64,128]{3,2,1,0:T(8,128)(2,1)S(1)}, u32[]{:S(2)}, u32[]{:S(2)}) async-start(bf16[8,4,64,128]{3,2,1,0:T(8,128)(2,1)} %get-tuple-element.22), calls=%async_computation.1 | async-start | bytes 1048576 | tf_op jit(solution)/shard_map/all_to_all | solution.py:362
  71.3 0.0 reduce-scatter.2.cloned.1.call-start
  71.3 0.0 all-gather.2.cloned.1.call-done.weights
  71.4 1.3 fusion.3.bias
  72.7 8.4 %all-to-all-done.1.arrived = bf16[8,4,64,128]{3,2,1,0:T(8,128)(2,1)S(1)} async-done(((bf16[8,4,64,128]{3,2,1,0:T(8,128)(2,1)}), bf16[8,4,64,128]{3,2,1,0:T(8,128)(2,1)S(1)}, u32[]{:S(2)}, u32[]{:S(2)}) %all-to-all-start.1) | async-done | bytes 524320 | tf_op jit(solution)/shard_map/all_to_all | solution.py:362
  81.0 0.8 copy-done.2
  81.8 5.9 %shard_map.206 = (bf16[4,96,512]{2,1,0:T(8,128)(2,1)}, bf16[8,4,64,128]{3,2,1,0:T(8,128)(2,1)}, bf16[8,80,1024]{2,1,0:T(8,128)(2,1)}) custom-call(s32[4]{0:T(128)} %subtract_clamp_fusion.counts, bf16[8,4,64,128]{3,2,1,0:T(8,128)(2,1)} %copy-done.2, bf16[8,80,1024]{2,1,0:T(8,128)(2,1)} %all-gather.2.cloned.1.call-done.weights, f32[1,1024]{1,0:T(1,128)} %fusion.3.bias, ...), custom_call_target="tpu_custom_call" | custom-call | tf_op jit(solution)/shard_map/pallas_call | solution.py:400
  87.7 0.0 reduce-scatter.2.cloned.1.call-update
  87.8 1.0 copy-done.5
  88.8 12.8 %all_to_all.20.arrived = bf16[8,4,64,128]{3,2,1,0:T(8,128)(2,1)} all-to-all(bf16[8,4,64,128]{3,2,1,0:T(8,128)(2,1)S(1)} %copy-done.5), channel_id=1, replica_groups={{0,4,1,5,2,6,3,7},{8,12,9,13,10,14,11,15},{16,20,17,21,18,22,19,23},{24..., dimensions={0} | all-to-all | bytes 1048576 | tf_op jit(solution)/shard_map/all_to_all | solution.py:362
  101.6 37.6 %shard_map.207 = (bf16[8,4,64,128]{3,2,1,0:T(8,128)(2,1)}, f32[64,384]{1,0:T(8,128)}) custom-call(bf16[8,4,64,128]{3,2,1,0:T(8,128)(2,1)} %all_to_all.20.arrived, bf16[8,4,64,128]{3,2,1,0:T(8,128)(2,1)} %copy-done, f32[64,384]{1,0:T(8,128)} %copy-done.3, bf16[64,128,128]{2,1,0:T(8,128)(2,1)} %get-tuple-element.25.table, ...), custom_call_target="tpu_custom_call" | custom-call | tf_op jit(solution)/shard_map/pallas_call | solution.py:409
  139.2 0.6 collective-permute-start.4
  139.7 1.8 collective-permute-start.5
  141.5 2.3 %collective-permute-start.6 = (f32[64,384]{1,0:T(8,128)}, f32[64,384]{1,0:T(8,128)S(1)}, u32[]{:S(2)}, u32[]{:S(2)}) collective-permute-start(f32[64,384]{1,0:T(8,128)} %get-tuple-element.30), channel_id=1, source_target_pairs={{0,1},{4,5},{1,9},{5,13},{2,17},{6,21},{3,25},{7,29},{8,2},{12,6},... | collective-permute-start | bytes 294920 | tf_op jit(solution)/shard_map/ppermute | solution.py:423
  143.9 1.5 collective-permute-start.7
  145.4 7.0 %all-to-all-start.3 = ((bf16[8,4,64,128]{3,2,1,0:T(8,128)(2,1)}), bf16[8,4,64,128]{3,2,1,0:T(8,128)(2,1)S(1)}, u32[]{:S(2)}, u32[]{:S(2)}) async-start(bf16[8,4,64,128]{3,2,1,0:T(8,128)(2,1)} %get-tuple-element.28), calls=%async_computation.3 | async-start | bytes 1048576 | tf_op jit(solution)/shard_map/all_to_all | solution.py:362
  152.4 9.2 %collective-permute-done.4 = f32[64,384]{1,0:T(8,128)S(1)} collective-permute-done((f32[64,384]{1,0:T(8,128)}, f32[64,384]{1,0:T(8,128)S(1)}, u32[]{:S(2)}, u32[]{:S(2)}) %collective-permute-start.4) | collective-permute-done | bytes 98336 | tf_op jit(solution)/shard_map/ppermute | solution.py:423
  161.7 0.0 collective-permute-done.5
  161.7 0.0 collective-permute-done.6
  161.7 0.0 collective-permute-done.7
  161.9 0.0 reduce-scatter.2.cloned.1.call-done
  161.9 4.5 %collective-permute-start.1 = (bf16[80,1024]{1,0:T(8,128)(2,1)}, bf16[80,1024]{1,0:T(8,128)(2,1)S(1)}, u32[]{:S(2)}, u32[]{:S(2)}) collective-permute-start(bf16[80,1024]{1,0:T(8,128)(2,1)} %reduce-scatter.2.cloned.1.call-done), channel_id=1, source_target_pairs={{0,3},{1,0},{2,1},{3,2},{4,7},{5,4},{6,5},{7,6},{8,11},{9,8},{10,9... | collective-permute-start | bytes 491528 | tf_op jit(solution)/shard_map/ppermute | solution.py:432
  166.4 0.7 negate_multiply_fusion
  167.1 0.7 slice_reduce_fusion
  167.9 0.0 all-to-all-done.3.arrived
  167.9 0.8 copy-done.1
  168.7 3.1 %shard_map.208 = bf16[4,96,512]{2,1,0:T(8,128)(2,1)} custom-call(bf16[8,4,64,128]{3,2,1,0:T(8,128)(2,1)} %copy-done.1, bf16[4,96,512]{2,1,0:T(8,128)(2,1)} %tokens.5, bf16[4,96,512]{2,1,0:T(8,128)(2,1)} %cotangent.3), custom_call_target="tpu_custom_call" | custom-call | tf_op jit(solution)/shard_map/pallas_call | solution.py:419
  171.7 3.8 %collective-permute-start.2 = (bf16[80,1024]{1,0:T(8,128)(2,1)S(1)}, bf16[80,1024]{1,0:T(8,128)(2,1)S(1)}, u32[]{:S(2)}, u32[]{:S(2)}) collective-permute-start(bf16[80,1024]{1,0:T(8,128)(2,1)S(1)} %copy-done.4), channel_id=1, source_target_pairs={{0,2},{1,3},{2,0},{3,1},{4,6},{5,7},{6,4},{7,5},{8,10},{9,11},{10,... | collective-permute-start | bytes 491528 | tf_op jit(solution)/shard_map/ppermute | solution.py:432
  175.5 0.0 collective-permute-start.3
  175.5 0.0 collective-permute-done.1
  175.5 6.8 %collective-permute-done.2 = bf16[80,1024]{1,0:T(8,128)(2,1)S(1)} collective-permute-done((bf16[80,1024]{1,0:T(8,128)(2,1)S(1)}, bf16[80,1024]{1,0:T(8,128)(2,1)S(1)}, u32[]{:S(2)}, u32[]{:S(2)}) %collective-permute-start.2) | collective-permute-done | bytes 163872 | tf_op jit(solution)/shard_map/ppermute | solution.py:432
  182.3 0.0 collective-permute-done.3
  182.5 0.1 dynamic-slice_convert_fusion
  182.6 0.1 slice_add_fusion
  182.7 0.7 slice_bitcast_fusion
  183.4 0.5 fusion.4
  (33 shorter events, 0.3 us)
Async XLA Ops:
  7.2 64.2 %all-gather.2.cloned.1.call-start = ((), (), s32[]{:S(2)}) async-start(), calls=%async_computation.5 | async-start | bytes 1474560 | tf_op jit(solution)/shard_map/all_gather | solution.py:376
  8.2 10.2 %copy-start.10 = (f32[64]{0:T(128)S(1)}, f32[64]{0:T(128)}, u32[]{:S(2)}) copy-start(f32[64]{0:T(128)} %param.20) | copy-start | bytes 772
  8.2 10.3 %copy-start.11 = (f32[64]{0:T(128)S(1)}, f32[64]{0:T(128)}, u32[]{:S(2)}) copy-start(f32[64]{0:T(128)} %param.21) | copy-start | bytes 772
  8.2 10.4 %copy-start.12 = (f32[64]{0:T(128)S(1)}, f32[64]{0:T(128)}, u32[]{:S(2)}) copy-start(f32[64]{0:T(128)} %param.22) | copy-start | bytes 772
  8.2 10.5 %copy-start.6 = (f32[64,64]{1,0:T(8,128)S(1)}, f32[64,64]{1,0:T(8,128)}, u32[]{:S(2)}) copy-start(f32[64,64]{1,0:T(8,128)} %param.16) | copy-start | bytes 49156
  8.2 10.5 %copy-start.7 = (f32[64,64]{1,0:T(8,128)S(1)}, f32[64,64]{1,0:T(8,128)}, u32[]{:S(2)}) copy-start(f32[64,64]{1,0:T(8,128)} %param.19) | copy-start | bytes 49156
  8.3 10.5 %copy-start.8 = (f32[64,64]{1,0:T(8,128)S(1)}, f32[64,64]{1,0:T(8,128)}, u32[]{:S(2)}) copy-start(f32[64,64]{1,0:T(8,128)} %param.18) | copy-start | bytes 49156
  9.0 9.8 %copy-start.9 = (f32[64,64]{1,0:T(8,128)S(1)}, f32[64,64]{1,0:T(8,128)}, u32[]{:S(2)}) copy-start(f32[64,64]{1,0:T(8,128)} %param.17) | copy-start | bytes 49156
  13.2 17.4 %all-to-all-start = ((bf16[8,4,64,128]{3,2,1,0:T(8,128)(2,1)}), bf16[8,4,64,128]{3,2,1,0:T(8,128)(2,1)S(1)}, u32[]{:S(2)}, u32[]{:S(2)}) async-start(bf16[8,4,64,128]{3,2,1,0:T(8,128)(2,1)} %shard_map.203), calls=%async_computation | async-start | bytes 1048576 | tf_op jit(solution)/shard_map/all_to_all | solution.py:362
  18.9 0.7 collective-permute-start
  19.6 0.6 copy-start.3
  30.6 0.8 copy-start
  51.4 29.6 %all-to-all-start.1 = ((bf16[8,4,64,128]{3,2,1,0:T(8,128)(2,1)}), bf16[8,4,64,128]{3,2,1,0:T(8,128)(2,1)S(1)}, u32[]{:S(2)}, u32[]{:S(2)}) async-start(bf16[8,4,64,128]{3,2,1,0:T(8,128)(2,1)} %get-tuple-element.22), calls=%async_computation.1 | async-start | bytes 1048576 | tf_op jit(solution)/shard_map/all_to_all | solution.py:362
  71.3 90.6 %reduce-scatter.2.cloned.1.call-start = ((), (), s32[]{:S(2)}) async-start(), calls=%async_computation.6 | async-start | bytes 1474560 | tf_op jit(solution)/shard_map/reduce_scatter | solution.py:406
  81.0 0.8 copy-start.2
  87.7 1.0 copy-start.5
  139.2 22.5 %collective-permute-start.4 = (f32[64,384]{1,0:T(8,128)}, f32[64,384]{1,0:T(8,128)S(1)}, u32[]{:S(2)}, u32[]{:S(2)}) collective-permute-start(f32[64,384]{1,0:T(8,128)} %get-tuple-element.30), channel_id=1, source_target_pairs={{0,3},{4,7},{1,11},{5,15},{2,19},{6,23},{3,27},{7,31},{8,0},{12,4}... | collective-permute-start | bytes 294920 | tf_op jit(solution)/shard_map/ppermute | solution.py:423
  139.7 21.9 %collective-permute-start.5 = (f32[64,384]{1,0:T(8,128)}, f32[64,384]{1,0:T(8,128)S(1)}, u32[]{:S(2)}, u32[]{:S(2)}) collective-permute-start(f32[64,384]{1,0:T(8,128)} %get-tuple-element.30), channel_id=1, source_target_pairs={{0,2},{4,6},{1,10},{5,14},{2,18},{6,22},{3,26},{7,30},{8,3},{12,7}... | collective-permute-start | bytes 294920 | tf_op jit(solution)/shard_map/ppermute | solution.py:423
  141.5 20.2 %collective-permute-start.6 = (f32[64,384]{1,0:T(8,128)}, f32[64,384]{1,0:T(8,128)S(1)}, u32[]{:S(2)}, u32[]{:S(2)}) collective-permute-start(f32[64,384]{1,0:T(8,128)} %get-tuple-element.30), channel_id=1, source_target_pairs={{0,1},{4,5},{1,9},{5,13},{2,17},{6,21},{3,25},{7,29},{8,2},{12,6},... | collective-permute-start | bytes 294920 | tf_op jit(solution)/shard_map/ppermute | solution.py:423
  143.9 17.9 %collective-permute-start.7 = (f32[64,384]{1,0:T(8,128)}, f32[64,384]{1,0:T(8,128)S(1)}, u32[]{:S(2)}, u32[]{:S(2)}) collective-permute-start(f32[64,384]{1,0:T(8,128)} %get-tuple-element.30), channel_id=1, source_target_pairs={{0,0},{4,4},{1,8},{5,12},{2,16},{6,20},{3,24},{7,28},{8,1},{12,5},... | collective-permute-start | bytes 294920 | tf_op jit(solution)/shard_map/ppermute | solution.py:423
  145.4 22.5 %all-to-all-start.3 = ((bf16[8,4,64,128]{3,2,1,0:T(8,128)(2,1)}), bf16[8,4,64,128]{3,2,1,0:T(8,128)(2,1)S(1)}, u32[]{:S(2)}, u32[]{:S(2)}) async-start(bf16[8,4,64,128]{3,2,1,0:T(8,128)(2,1)} %get-tuple-element.28), calls=%async_computation.3 | async-start | bytes 1048576 | tf_op jit(solution)/shard_map/all_to_all | solution.py:362
  161.9 9.9 %copy-start.4 = (bf16[80,1024]{1,0:T(8,128)(2,1)S(1)}, bf16[80,1024]{1,0:T(8,128)(2,1)}, u32[]{:S(2)}) copy-start(bf16[80,1024]{1,0:T(8,128)(2,1)} %reduce-scatter.2.cloned.1.call-done) | copy-start | bytes 491524
  161.9 13.6 %collective-permute-start.1 = (bf16[80,1024]{1,0:T(8,128)(2,1)}, bf16[80,1024]{1,0:T(8,128)(2,1)S(1)}, u32[]{:S(2)}, u32[]{:S(2)}) collective-permute-start(bf16[80,1024]{1,0:T(8,128)(2,1)} %reduce-scatter.2.cloned.1.call-done), channel_id=1, source_target_pairs={{0,3},{1,0},{2,1},{3,2},{4,7},{5,4},{6,5},{7,6},{8,11},{9,8},{10,9... | collective-permute-start | bytes 491528 | tf_op jit(solution)/shard_map/ppermute | solution.py:432
  167.9 0.8 copy-start.1
  171.7 10.6 %collective-permute-start.2 = (bf16[80,1024]{1,0:T(8,128)(2,1)S(1)}, bf16[80,1024]{1,0:T(8,128)(2,1)S(1)}, u32[]{:S(2)}, u32[]{:S(2)}) collective-permute-start(bf16[80,1024]{1,0:T(8,128)(2,1)S(1)} %copy-done.4), channel_id=1, source_target_pairs={{0,2},{1,3},{2,0},{3,1},{4,6},{5,7},{6,4},{7,5},{8,10},{9,11},{10,... | collective-permute-start | bytes 491528 | tf_op jit(solution)/shard_map/ppermute | solution.py:432
  175.5 6.8 %collective-permute-start.3 = (bf16[80,1024]{1,0:T(8,128)(2,1)S(1)}, bf16[80,1024]{1,0:T(8,128)(2,1)S(1)}, u32[]{:S(2)}, u32[]{:S(2)}) collective-permute-start(bf16[80,1024]{1,0:T(8,128)(2,1)S(1)} %copy-done.4), channel_id=1, source_target_pairs={{0,1},{1,2},{2,3},{3,0},{4,5},{5,6},{6,7},{7,4},{8,9},{9,10},{10,1... | collective-permute-start | bytes 491528 | tf_op jit(solution)/shard_map/ppermute | solution.py:432
Sparse Core Ops, SparseCore 0:
  10.2 31.2 all-gather.1
  87.9 33.9 reduce-scatter.1

commit v2 on v1

v2 whole, which is shorter than its diff:
```python
import functools
import math

import jax
import jax.numpy as jnp
from jax import lax
from jax.experimental import pallas as pl
from jax.experimental.pallas import tpu as pltpu
from jax.sharding import PartitionSpec as P

EPSILON = 1e-05
LANES = 128
GROUP = 8
COST = (2, 8, 10, 6, 1, 3, 2, 8)
BOTH = ("shard", "ctx")
F32 = jnp.float32
BF16 = jnp.bfloat16
VMEM = pl.BlockSpec(memory_space=pltpu.VMEM)
SMEM = pl.BlockSpec(memory_space=pltpu.SMEM)
HBM = pl.BlockSpec(memory_space=pltpu.HBM)
PARAMS = pltpu.CompilerParams(vmem_limit_bytes=20 * 1024 * 1024)


class Plan:
    def __init__(self, shards, chunks):
        layers = shards // 2
        self.shards, self.chunks = shards, chunks
        self.subs = subs = chunks // layers
        self.order = [
            (core, top * subs + sub)
            for top in range(chunks // subs)
            for core in range(2)
            for sub in range(subs)
        ]
        self.groups = [
            [(2 * z + core) * chunks + c for core, c in self.order] for z in range(layers)
        ]
        members = [(z, core, c) for z in range(layers) for core, c in self.order]

        def here(z, core, c):
            return (2 * z + core) * chunks + c

        def owner(z, core, c, turn):
            place = (z * subs + c % subs + turn) % chunks
            return (2 * (c // subs) + core) * chunks + place

        self.fetch = [(owner(*m, 0), here(*m)) for m in members]
        self.give = [[(here(*m), owner(*m, turn)) for m in members] for turn in range(chunks)]
        self.rotate = [
            [(a, (a + turn) % chunks) for a in range(chunks)] for turn in range(1, chunks)
        ]
        self.layers = layers
        self.climb = [
            [(s, (s + 2 * turn) % shards) for s in range(shards)] for turn in range(1, layers)
        ]
        self.across = [(s, s ^ 1) for s in range(shards)]


def row_stats(rows):
    mean = jnp.mean(rows, axis=-1, keepdims=True)
    centered = rows - mean
    var = jnp.mean(centered * centered, axis=-1, keepdims=True)
    inv = lax.rsqrt(var + EPSILON)
    return centered * inv, inv


def dot(a, b, over):
    return lax.dot_general(a, b, (((over[0],), (over[1],)), ((), ())), preferred_element_type=F32)


def pack_kernel(decay, freq, real, imag, skip, gain, shift, weight, bias, pack, scales, piece):
    own, states = decay.shape
    wide = weight.shape[1]
    rate = decay[...]
    square = rate * rate
    scale = jnp.sqrt(2.0 * rate * jnp.exp(-rate) * (1.0 + square / 6.0 * (1.0 + square / 20.0)))
    scales[...] = scale
    pack[:, 0:LANES] = jnp.concatenate([rate, freq[...]], axis=1)
    pack[:, LANES : 2 * LANES] = jnp.concatenate([scale * real[...], scale * imag[...]], axis=1)
    lane = lax.broadcasted_iota(jnp.int32, (own, LANES), 1)
    diagonal = lax.broadcasted_iota(jnp.int32, (own, own), 0) == lax.broadcasted_iota(jnp.int32, (own, own), 1)
    tail = jnp.zeros((own, LANES), F32)
    for k, vector in enumerate((skip, gain, shift)):
        column = jnp.sum(jnp.where(diagonal, vector[...], 0.0), axis=1, keepdims=True)
        tail = jnp.where(lane == k, column, tail)
    pack[:, 2 * LANES :] = tail
    piece[0:own] = weight[...].astype(BF16)
    segment = lax.broadcasted_iota(jnp.int32, (1, wide), 1) // bias.shape[1]
    repeated = jnp.concatenate([bias[...]] * (wide // bias.shape[1]), axis=1)
    row = jnp.where(segment == lax.axis_index("shard"), repeated, 0.0)
    piece[own:] = jnp.broadcast_to(row, (piece.shape[0] - own, wide)).astype(BF16)


def valid_count(lengths, n, rows):
    return jnp.clip(lengths[n] - lax.axis_index("ctx") * rows, 0, rows)


def norm_kernel(lengths, tokens, out):
    seqs, rows, width = tokens.shape
    blocks, _, chans, _ = out.shape
    pad = LANES - rows
    last = lax.broadcasted_iota(jnp.int32, (pad, width), 0) == pad - 1
    for n in range(seqs):
        xhat, _ = row_stats(tokens[n].astype(F32))
        tail = jnp.where(last, valid_count(lengths, n, rows).astype(F32), 0.0)
        full = jnp.concatenate([xhat, tail], axis=0)
        out[:, n] = full.T.astype(BF16).reshape(blocks, chans, LANES)


def swap(values):
    return pltpu.roll(values, LANES // 2, values.ndim - 1)


def table_kernel(rows, pack, table, lines, firsts):
    chans = pack.shape[0]
    low2 = lax.broadcasted_iota(jnp.int32, (1, LANES), 1) < LANES // 2
    low3 = low2[None]
    angle = jnp.where(low2, 0.0, math.pi / 2)
    step = 8
    offsets = lax.broadcasted_iota(jnp.int32, (1, step, 1), 1).astype(F32)

    def spread(pair):
        other = swap(pair)
        return jnp.where(low2, pair, other), jnp.where(low2, other, pair)

    def factors(power):
        other = swap(power)
        return jnp.where(low2, power, other), jnp.where(low2, -other, power)

    def block(at, _):
        here = pl.ds(pl.multiple_of(at * step, step), step)
        decay, freq = spread(pack[here, 0:LANES])
        real, imag = spread(pack[here, LANES : 2 * LANES])

        def power(by):
            return jnp.exp(-decay * by) * jnp.cos(freq * by - angle)

        part = jnp.exp(-decay[:, None, :] * offsets) * jnp.cos(freq[:, None, :] * offsets - angle[None])
        table[here, 0:step] = part.astype(BF16)
        size = step
        while size < LANES:
            same, cross = factors(power(float(size)))
            new = part * same[:, None, :] + swap(part) * cross[:, None, :]
            table[here, size : 2 * size] = new.astype(BF16)
            part = jnp.concatenate([part, new], axis=1)
            size *= 2
        real = jnp.where(low2, real, -real)
        whole = part.astype(BF16)
        hat = jnp.where(low2, real, -imag).astype(BF16)
        for k in range(step):
            row = jnp.broadcast_to(hat[k : k + 1], (step, LANES))
            lines[at * step + k, 0:1] = dot(row, whole[k], (1, 1))[0:1]
        one = power(1.0)
        same, cross = factors(one)
        firsts[0, here] = same
        firsts[1, here] = cross
        chunk_same, chunk_cross = factors(power(float(rows)))
        hat_re = jnp.where(low2, real, -real)
        turn_re = hat_re * same - imag * jnp.where(low2, -cross, cross)
        turn_im = hat_re * jnp.where(low2, -cross, cross) + imag * same
        for k, line in enumerate((chunk_same, chunk_cross, jnp.where(low2, turn_re, -turn_re), -turn_im)):
            lines[here, k + 1 : k + 2] = line[:, None, :]
        return 0

    lax.fori_loop(0, chans // step, block, 0)


def upper_half(rows):
    square = (rows, LANES)
    return lax.broadcasted_iota(jnp.int32, square, 1) >= lax.broadcasted_iota(jnp.int32, square, 0)


def toeplitz(upper, taps):
    slid = pltpu.roll(jnp.broadcast_to(taps, upper.shape), 0, 1, stride=1, stride_axis=0)
    body = jnp.where(upper, slid, 0.0).astype(BF16)
    return jnp.concatenate([body, jnp.zeros((LANES - upper.shape[0], LANES), BF16)], axis=0)


def mirror_matrix(rows):
    square = (LANES, LANES)
    reach = lax.broadcasted_iota(jnp.int32, square, 0) + lax.broadcasted_iota(jnp.int32, square, 1)
    return jnp.where(reach == rows - 1, 1.0, 0.0).astype(BF16)


def place(order, seqs, block, n):
    core, c = order[block]
    return (c * 2 + core) * seqs + n


def forward_kernel(
    chunks, rows, order, arrived, pack, far_table, lines, hidden, kept, inputs, mirrored, mixed, table, sem,
):
    fetch = pltpu.make_async_copy(far_table, table, sem)
    fetch.start()
    blocks, seqs, chans, _ = arrived.shape
    total = blocks * seqs
    each = 2 * seqs
    lane = lax.broadcasted_iota(jnp.int32, (1, LANES), 1).astype(F32)
    gain, shift = pack[:, 257:258], pack[:, 258:259]
    mirror = mirror_matrix(rows)
    upper = upper_half(rows)
    for b in range(blocks):
        for n in range(seqs):
            here = pl.ds(place(order, seqs, b, n) * chans, chans)
            xhat = arrived[b, n].astype(F32)
            x = jnp.where(lane < xhat[0:1, LANES - 1 :], xhat * gain + shift, 0.0).astype(BF16)
            inputs[here, :] = x.astype(F32)
            mirrored[here, :] = dot(x, mirror, (1, 0))

    def group(at, _):
        members = range(GROUP)
        mine = [pl.ds(at * GROUP + k, total, stride=chans) for k in members]
        line = [lines[at * GROUP + k] for k in members]
        ends = [dot(mirrored[mine[k], :].astype(BF16), table[at * GROUP + k], (1, 0)) for k in members]
        local = [
            dot(inputs[mine[k], :].astype(BF16), toeplitz(upper, line[k][0:1]), (1, 0)) for k in members
        ]
        for k in members:
            state = ends[k][0:each]
            carried = [jnp.zeros((each, LANES), F32)]
            for c in range(1, chunks):
                carried.append(state * line[k][3:4] + swap(state) * line[k][4:5])
                if c < chunks - 1:
                    state = state * line[k][1:2] + swap(state) * line[k][2:3]
                    state += ends[k][each * c : each * (c + 1)]
            ends[k] = jnp.concatenate(carried, axis=0).astype(BF16)
        for k in members:
            mixed[mine[k], :] = local[k] + dot(ends[k], table[at * GROUP + k], (1, 1))
        return 0

    fetch.wait()
    lax.fori_loop(0, chans // GROUP, group, 0)
    skip = pack[:, 256:257]
    for b in range(blocks):
        for n in range(seqs):
            here = pl.ds(place(order, seqs, b, n) * chans, chans)
            mix = mixed[here, :] + skip * inputs[here, :]
            kept[here, :] = mix.astype(BF16)
            hidden[b, n] = jax.nn.gelu(mix).astype(BF16)


def weight_kernel(plan, *refs):
    pieces, (w, bias) = refs[:-2], refs[-2:]
    layers = plan.layers
    width = w.shape[0]
    own = width // plan.shards
    shard = lax.axis_index("shard")
    layer, core = shard // 2, lax.rem(shard, 2)
    total = jnp.zeros((1, 2 * width), F32)
    for side in range(2):
        for turn in range(layers):
            piece = pieces[side * layers + turn]
            home = 2 * lax.rem(layer + layers - turn, layers) + lax.rem(core + side, 2)
            w[pl.ds(pl.multiple_of(home * own, own), own), :] = piece[0:own]
            total += piece[own : own + 1].astype(F32)
    bias[...] = total


def glu_kernel(lengths, arrived, tokens, cotangent, w, bias, block_out, leaving, outers):
    seqs, rows, width = tokens.shape
    blocks, _, chans, _ = arrived.shape
    position = lax.broadcasted_iota(jnp.int32, (rows, width), 0)
    for n in range(seqs):
        hidden = arrived[:, n].reshape(width, LANES).astype(F32).T.astype(BF16)
        proj = dot(hidden, w[...], (1, 0)) + bias[...]
        r, q = proj[0:rows, :width], proj[0:rows, width:]
        valid = jnp.where(position < valid_count(lengths, n, rows), 1.0, 0.0)
        open_ = jax.nn.sigmoid(q)
        block_out[n] = (tokens[n].astype(F32) + valid * (r * open_)).astype(BF16)
        e = valid * cotangent[n].astype(F32)
        first = e * open_
        both = jnp.concatenate([first, first * r * (1.0 - open_)], axis=1).astype(BF16)
        both = jnp.concatenate([both, jnp.zeros((LANES - rows, 2 * width), BF16)], axis=0)
        back = dot(both, w[...], (1, 1))
        leaving[:, n] = back.T.astype(BF16).reshape(blocks, chans, LANES)
        outers[pl.ds(n * LANES, LANES), :] = both


def outer_kernel(plan, arrived, outers, kept, sent):
    blocks, seqs, chans, _ = arrived.shape
    layers, subs = plan.layers, plan.subs
    own = chans * subs
    wide = outers.shape[1]
    core = lax.rem(lax.axis_index("shard"), 2)
    outer = outers[...]
    bias = jnp.sum(outer.astype(F32), axis=0, keepdims=True)
    tail = jnp.broadcast_to(bias, (kept.shape[1] - own, wide)).astype(BF16)
    for side, out in enumerate((sent, kept)):
        which = lax.rem(core + 1 - side, 2)
        left = jnp.concatenate(
            [
                jnp.concatenate([arrived[(2 * z + which) * subs + sub, n] for n in range(seqs)], axis=1)
                for z in range(layers)
                for sub in range(subs)
            ],
            axis=0,
        )
        out[:, 0:own] = dot(left, outer, (1, 0)).astype(BF16).reshape(layers, own, wide)
        for z in range(layers):
            out[z, own:] = tail


def gelu_slope(x):
    c = math.sqrt(2.0 / math.pi)
    t = jnp.tanh(c * (x + 0.044715 * x * x * x))
    return 0.5 * (1.0 + t) + 0.5 * x * (1.0 - t * t) * (c * (1.0 + 3.0 * 0.044715 * x * x))


def backward_kernel(
    chunks, rows, order, arrived, first, pack, far_table, lines, mixed,
    leaving, kept, tallies, grads, local, cross, table, sem,
):
    fetch = pltpu.make_async_copy(far_table, table, sem)
    fetch.start()
    blocks, seqs, chans, _ = arrived.shape
    total = blocks * seqs
    each = 2 * seqs
    lane = lax.broadcasted_iota(jnp.int32, (1, LANES), 1).astype(F32)
    skip, gain = pack[:, 256:257], pack[:, 257:258]
    mirror = mirror_matrix(rows)
    upper = upper_half(rows)
    for b in range(blocks):
        for n in range(seqs):
            here = pl.ds(place(order, seqs, b, n) * chans, chans)
            g = (arrived[b, n].astype(F32) * gelu_slope(mixed[here, :].astype(F32))).astype(BF16)
            kept[here, :] = g
            grads[here, :] = g.astype(F32)

    def group(at, _):
        members = range(GROUP)
        which = [at * GROUP + k for k in members]
        mine = [pl.ds(h, total, stride=chans) for h in which]
        line = [lines[h] for h in which]
        ends = [dot(grads[mine[k], :].astype(BF16), table[which[k]], (1, 0)) for k in members]
        for k in members:
            g = grads[mine[k], :].astype(BF16)
            local[mine[k], :] = dot(g, toeplitz(upper, line[k][0:1]), (1, 1))
        for k in members:
            parts = [jnp.zeros((each, LANES), F32)]
            state = ends[k][each * (chunks - 1) :]
            for c in range(chunks - 2, -1, -1):
                parts.append(state * line[k][3:4] + swap(state) * line[k][4:5])
                if c:
                    state = state * line[k][1:2] + swap(state) * line[k][2:3]
                    state += ends[k][each * c : each * (c + 1)]
            ends[k] = jnp.concatenate(parts[::-1], axis=0).astype(BF16)
        for k in members:
            cross[mine[k], :] = dot(ends[k], table[which[k]], (1, 1))
        return 0

    fetch.wait()
    lax.fori_loop(0, chans // GROUP, group, 0)
    gains = shifts = jnp.zeros((chans, LANES), F32)
    for b in range(blocks):
        for n in range(seqs):
            here = pl.ds(place(order, seqs, b, n) * chans, chans)
            grad = local[here, :] + skip * grads[here, :]
            grad += dot(cross[here, :].astype(BF16), mirror, (1, 0))
            xhat = first[b, n].astype(F32)
            m = jnp.where(lane < xhat[0:1, LANES - 1 :], grad, 0.0)
            gains += m * xhat
            shifts += m
            leaving[b, n] = (gain * m).astype(BF16)
    tallies[0] = gains
    tallies[1] = shifts


def moment_kernel(
    chunks, rows, order, first, pack, table, lines, firsts, kept, tallies, sums, mirrored, grads,
    cross_one_a, cross_one_b, cross_two_a, cross_two_b, local_one, local_two,
):
    blocks, seqs, chans, _ = first.shape
    total = blocks * seqs
    each = 2 * seqs
    lane = lax.broadcasted_iota(jnp.int32, (1, LANES), 1).astype(F32)
    gain, shift = pack[:, 257:258], pack[:, 258:259]
    mirror = mirror_matrix(rows)
    skips = jnp.zeros((chans, LANES), F32)
    for b in range(blocks):
        for n in range(seqs):
            here = pl.ds(place(order, seqs, b, n) * chans, chans)
            xhat = first[b, n].astype(F32)
            x = jnp.where(lane < xhat[0:1, LANES - 1 :], xhat * gain + shift, 0.0).astype(BF16)
            mirrored[here, :] = dot(x, mirror, (1, 0))
            g = kept[here, :].astype(F32)
            grads[here, :] = g
            skips += g * x.astype(F32)
    square = (rows, LANES)
    behind = lax.broadcasted_iota(jnp.int32, square, 1) <= (
        LANES - rows + lax.broadcasted_iota(jnp.int32, square, 0)
    )

    def group(place_at, _):
        members = range(GROUP)
        which = [place_at * GROUP + k for k in members]
        mine = [pl.ds(h, total, stride=chans) for h in which]
        line = [lines[h] for h in which]
        ends, outer, pairs = [], [], []
        for k in members:
            x_back, g = mirrored[mine[k], :], grads[mine[k], :]
            stack = jnp.concatenate([x_back, g, x_back * lane, g * lane], axis=0).astype(BF16)
            ends.append(dot(stack, table[which[k]], (1, 0)))
        for k in members:
            g = grads[mine[k], :].astype(BF16)
            outer.append(dot(mirrored[mine[k], :].astype(BF16), g, (0, 0)))
        for k in members:
            swapped = swap(ends[k])

            def at(kind, c, of=ends[k]):
                start = kind * total + each * c
                return of[start : start + each]

            def onward(state):
                return state * line[k][1:2] + swap(state) * line[k][2:3]

            one_a = one_b = two_a = two_b = jnp.zeros((each, LANES), F32)
            state, slope = at(0, 0), at(2, 0)
            for c in range(1, chunks):
                both = state + slope
                one_a += state * at(1, c)
                one_b += state * at(1, c, swapped)
                two_a += both * at(1, c) + state * at(3, c)
                two_b += both * at(1, c, swapped) + state * at(3, c, swapped)
                if c < chunks - 1:
                    slope = onward(slope + float(rows) * state) + at(2, c)
                    state = onward(state) + at(0, c)
            for into, value in (
                (cross_one_a, one_a), (cross_one_b, one_b), (cross_two_a, two_a), (cross_two_b, two_b),
            ):
                into[pl.ds(which[k], 1), :] = jnp.sum(value, axis=0, keepdims=True)
            slid = pltpu.roll(outer[k][0:rows], LANES - rows + 1, 1, stride=1, stride_axis=0)
            corr = jnp.sum(jnp.where(behind, slid, 0.0), axis=0, keepdims=True)
            pair = jnp.concatenate([corr, corr * lane, jnp.zeros((6, LANES), F32)], axis=0)
            pairs.append(pair.astype(BF16))
        for k in members:
            turned = dot(pairs[k], table[which[k]], (1, 0))
            local_one[pl.ds(which[k], 1), :] = turned[0:1]
            local_two[pl.ds(which[k], 1), :] = turned[1:2]
        return 0

    lax.fori_loop(0, chans // GROUP, group, 0)
    low = lax.broadcasted_iota(jnp.int32, (1, LANES), 1) < LANES // 2
    for k, (a, b, near) in enumerate(
        ((cross_one_a, cross_one_b, local_one), (cross_two_a, cross_two_b, local_two))
    ):
        far = jnp.where(low, a[...] - swap(a[...]), b[...] + swap(b[...]))
        moment = far * firsts[0] + swap(far) * firsts[1] + near[...]
        sums[0:chans, k * LANES : (k + 1) * LANES] = moment.astype(BF16)
    diagonal = lax.broadcasted_iota(jnp.int32, (chans, 2 * LANES), 0) == lax.broadcasted_iota(
        jnp.int32, (chans, 2 * LANES), 1
    )
    row = lax.broadcasted_iota(jnp.int32, (16, 2 * LANES), 0)
    tail = jnp.zeros((16, 2 * LANES), F32)
    for k, part in enumerate((skips, tallies[0], tallies[1])):
        column = jnp.sum(part, axis=1, keepdims=True)
        line = jnp.sum(jnp.where(diagonal, column, 0.0), axis=0, keepdims=True)
        tail = jnp.where(row == k, line, tail)
    sums[chans:, :] = tail.astype(BF16)


def share_kernel(layers, kept, came, *outs):
    layer = lax.axis_index("shard") // 2
    for turn, out in enumerate(outs):
        at = lax.rem(layer + turn, layers)
        out[...] = (kept[at].astype(F32) + came[at].astype(F32)).astype(BF16)


def add_kernel(*refs):
    total = refs[0][...].astype(F32)
    for ref in refs[1:-1]:
        total += ref[...].astype(F32)
    refs[-1][...] = total.astype(BF16)


def ordered(parts, slots):
    count = len(parts)
    mine = lax.axis_index("ctx")
    for turn, part in enumerate(parts):
        slots[lax.rem(mine + count - turn, count)] = part[...]


def owner_kernel(chunks, *refs):
    parts, (grad, bias, slots) = refs[:chunks], refs[chunks:]
    own, segment = grad.shape[0], bias.shape[1]
    ordered(parts, slots)
    total = slots[0].astype(F32)
    for k in range(1, chunks):
        total += slots[k].astype(F32)
    grad[...] = total[0:own]
    shard = lax.axis_index("shard")
    row = jnp.zeros((1, segment), F32)
    for s in range(total.shape[1] // segment):
        row = jnp.where(shard == s, total[own : own + 1, s * segment : (s + 1) * segment], row)
    bias[...] = row


def state_kernel(chunks, subs, *refs):
    parts, (decay, scale_in, real, imag), outs = refs[:chunks], refs[chunks : chunks + 4], refs[chunks + 4 :]
    grad_decay, grad_freq, grad_real, grad_imag, *vectors, slots = outs
    ordered(parts, slots)
    own, states = decay.shape
    chans = own // subs
    sums = []
    for sub in range(subs):
        total = slots[sub].astype(F32)
        for k in range(sub + subs, chunks, subs):
            total += slots[k].astype(F32)
        sums.append(total)
    moments = jnp.concatenate([t[0:chans] for t in sums], axis=0)
    one_re, one_im, two_re, two_im = (moments[:, k * states : (k + 1) * states] for k in range(4))
    scale = scale_in[...]
    hat_re, hat_im = scale * real[...], scale * imag[...]
    grad_decay[...] = -(hat_re * two_re - hat_im * two_im) + jnp.exp(-2.0 * decay[...]) / scale * (
        real[...] * one_re - imag[...] * one_im
    )
    grad_freq[...] = -(hat_re * two_im + hat_im * two_re)
    grad_real[...] = scale * one_re
    grad_imag[...] = -scale * one_im
    for k, vector in enumerate(vectors):
        lines = [t[chans + k : chans + k + 1, 0:chans] for t in sums]
        vector[...] = jnp.concatenate(lines, axis=1) if subs > 1 else lines[0]


def final_kernel(arrived, tokens, cotangent, out):
    seqs, rows, width = tokens.shape
    for n in range(seqs):
        d = arrived[:, n].reshape(width, LANES).astype(F32).T[0:rows]
        xhat, inv = row_stats(tokens[n].astype(F32))
        mean = jnp.mean(d, axis=-1, keepdims=True)
        along = jnp.mean(d * xhat, axis=-1, keepdims=True)
        grad = (d - mean - xhat * along) * inv
        out[n] = (cotangent[n].astype(F32) + grad).astype(BF16)


def call(kernel, micros, outs, ins, scratch=()):
    return pl.pallas_call(
        kernel,
        out_shape=[(pltpu.HBM if len(o) > 2 else jax.ShapeDtypeStruct)(*o[:2]) for o in outs],
        in_specs=ins,
        out_specs=[VMEM] * len(outs),
        scratch_shapes=list(scratch),
        compiler_params=PARAMS,
        cost_estimate=pl.CostEstimate(
            flops=int(micros * 1e9), bytes_accessed=int(micros * 3.5e6), transcendentals=0
        ),
    )


def in_hbm(*arrays):
    return [pltpu.with_memory_space_constraint(a, pltpu.HBM) for a in arrays]


def per_device(
    plan, tokens, lengths, out_weight, out_bias, decay_rate, frequency, coef_real, coef_imag,
    skip, gain, shift, cotangent,
):
    seqs, rows, width = tokens.shape
    chunks, subs = plan.chunks, plan.subs
    blocks = 2 * chunks
    chans = width // blocks
    own, states = decay_rate.shape
    total = blocks * seqs
    mine, shard = lax.axis_index("ctx"), lax.axis_index("shard")
    layer = shard // 2

    def exchange(buffer):
        return lax.all_to_all(buffer, BOTH, 0, 0, axis_index_groups=plan.groups, tiled=True)

    segment = out_bias.shape[0]
    pack, scale, piece = call(
        pack_kernel,
        2,
        [((own, 3 * LANES), F32), ((own, states), F32), ((own + 16, 2 * width), BF16)],
        [VMEM] * 9,
    )(
        *in_hbm(
            decay_rate, frequency, coef_real, coef_imag,
            skip[None], gain[None], shift[None], out_weight, out_bias[None],
        )
    )
    if subs > 1:
        pack = lax.dynamic_slice_in_dim(pack, lax.rem(mine, subs) * chans, chans, 0)
    pack = lax.ppermute(pack, BOTH, plan.fetch)

    wire = ((blocks, seqs, chans, LANES), BF16)
    (first,) = call(norm_kernel, COST[0], [wire], [SMEM, VMEM])(lengths, tokens)
    first = exchange(first)
    piece, pack = lax.optimization_barrier((piece, pack))
    near = [piece] + [lax.ppermute(piece, "shard", route) for route in plan.climb]
    table_type = ((chans, LANES, LANES), BF16, 1)
    table, lines, firsts = call(
        functools.partial(table_kernel, rows),
        COST[1],
        [table_type, ((chans, 8, LANES), F32), ((2, chans, LANES), F32)],
        [VMEM],
    )(pack)
    buffer = pltpu.VMEM((total * chans, LANES), F32)
    line = pltpu.VMEM((chans, LANES), F32)
    fetched = [pltpu.VMEM(*table_type[:2]), pltpu.SemaphoreType.DMA]
    low = ((total * chans, LANES), BF16)
    hidden, mixed = call(
        functools.partial(forward_kernel, chunks, rows, plan.order),
        COST[2],
        [wire, low],
        [VMEM, VMEM, HBM, VMEM],
        [buffer, buffer, buffer] + fetched,
    )(first, pack, table, lines)
    hidden, near = lax.optimization_barrier((hidden, near))
    across = [lax.ppermute(p, "shard", plan.across) for p in near]
    hidden = exchange(hidden)
    weight, bias = call(
        functools.partial(weight_kernel, plan),
        2,
        [((width, 2 * width), BF16), ((1, 2 * width), F32)],
        [VMEM] * (2 * plan.layers),
    )(*near, *across)
    half = ((plan.layers, own + 16, 2 * width), BF16)
    block_out, back, outers = call(
        glu_kernel,
        COST[3],
        [(tokens.shape, BF16), wire, ((seqs * LANES, 2 * width), BF16)],
        [SMEM] + [VMEM] * 5,
    )(lengths, hidden, tokens, cotangent, weight, bias)
    back = exchange(back)
    kept, sent = call(functools.partial(outer_kernel, plan), 2, [half, half], [VMEM] * 2)(hidden, outers)

    came = lax.ppermute(sent, "shard", plan.across)
    slab = ((own + 16, 2 * width), BF16)
    shares = call(
        functools.partial(share_kernel, plan.layers), COST[6], [slab] * plan.layers, [VMEM] * 2
    )(kept, came)
    back, shares = lax.optimization_barrier((back, shares))
    climbed = [lax.ppermute(v, "shard", route) for v, route in zip(shares[1:], plan.climb)]
    leaving, local_grads, tallies = call(
        functools.partial(backward_kernel, chunks, rows, plan.order),
        COST[4],
        [wire, low, ((2, chans, LANES), F32)],
        [VMEM, VMEM, VMEM, HBM, VMEM, VMEM],
        [buffer, buffer, buffer] + fetched,
    )(back, first, pack, table, lines, mixed)
    (owned,) = call(add_kernel, 1, [slab], [VMEM] * plan.layers)(shares[0], *climbed)
    tallies, owned = lax.optimization_barrier((tallies, owned))
    state = (chans + 16, 2 * LANES)
    (sums,) = call(
        functools.partial(moment_kernel, chunks, rows, plan.order),
        COST[7],
        [(state, BF16)],
        [VMEM] * 7,
        [buffer, buffer] + [line] * 6,
    )(first, pack, table, lines, firsts, local_grads, tallies)
    leaving = exchange(leaving)
    (tokens_grad,) = call(final_kernel, COST[5], [(tokens.shape, BF16)], [VMEM] * 3)(
        leaving, tokens, cotangent
    )

    parts = [lax.ppermute(sums, BOTH, route) for route in plan.give]
    wholes = [owned] + [lax.ppermute(owned, "ctx", route) for route in plan.rotate]
    tokens_grad, parts, wholes = lax.optimization_barrier((tokens_grad, parts, wholes))
    grad_weight, grad_bias = call(
        functools.partial(owner_kernel, chunks),
        2,
        [(out_weight.shape, F32), ((1, segment), F32)],
        [VMEM] * chunks,
        [pltpu.VMEM((chunks,) + slab[0], BF16)],
    )(*wholes)
    matrix, vector = ((own, states), F32), ((1, own), F32)
    grads = call(
        functools.partial(state_kernel, chunks, subs),
        2,
        [matrix] * 4 + [vector] * 3,
        [VMEM] * (chunks + 4),
        [pltpu.VMEM((chunks,) + state, BF16)],
    )(*parts, decay_rate, scale, coef_real, coef_imag)
    return (
        block_out,
        tokens_grad,
        grad_weight,
        grad_bias[0],
        *grads[:4],
        *(v[0] for v in grads[4:]),
    )


def solution(mesh):
    plan = Plan(mesh.shape["shard"], mesh.shape["ctx"])
    rows = P("shard", "ctx", None)
    matrix = P("shard", None)
    vector = P("shard")
    in_specs = (rows, vector, matrix, vector) + (matrix,) * 4 + (vector,) * 3 + (rows,)
    out_specs = (rows, rows, matrix, vector) + (matrix,) * 4 + (vector,) * 3
    return jax.shard_map(
        functools.partial(per_device, plan),
        mesh=mesh,
        in_specs=in_specs,
        out_specs=out_specs,
        check_vma=False,
    )
```

time: 192 us -> 120 us (0.62)
  Pallas kernels: 79.3 us -> 41.7 us
  between operations: 14.4 us -> 0.96 us
  blocking collectives: 12.8 us -> 0 us
  local copies, waits for them, and re-layouts: 6.68 us -> 17.4 us
  waiting for transfers between devices: 24.5 us -> 15.5 us
  other arithmetic: 5.82 us -> 0 us
  starting transfers between devices: 47.3 us -> 44.1 us
    pallas_call x6 -> x14, Pallas kernels: 79.3 us -> 41.7 us  [the longest x1 7.79 us: per_device(): call(functools.partial(forward_kernel, chunks, rows, plan.order), COST[2]...]
    unnamed x40 -> x64, local copies, waits for them, and re-layouts: 4.27 us -> 17.4 us
    all_to_all x1 -> x0, blocking collectives: 12.8 us -> none  [exchange(): lax.all_to_all(buffer, BOTH, 0, 0, axis_index_groups=plan.groups, tiled=T...]
    all_to_all x3 -> x4, starting transfers between devices: 32.1 us -> 21 us  [exchange(): lax.all_to_all(buffer, BOTH, 0, 0, axis_index_groups=plan.groups, tiled=T...]
    ppermute x4 -> x15, waiting for transfers between devices: 9.23 us -> 1.35 us  [the longest x4 1.32 us: per_device(): across = [lax.ppermute(p, 'shard', plan.across) for p in near]]
    ppermute x4 -> x15, starting transfers between devices: 6.24 us -> 13.9 us  [the longest x3 5.28 us: per_device(): lax.ppermute(v, 'shard', route)]
    ppermute x3, waiting for transfers between devices: 6.79 us -> 4.04 us  [per_device(): lax.ppermute(owned, 'ctx', route)]
    all_to_all x3 -> x4, waiting for transfers between devices: 8.37 us -> 10.1 us  [exchange(): lax.all_to_all(buffer, BOTH, 0, 0, axis_index_groups=plan.groups, tiled=T...]
  transfers between devices with their start and end apart: 13 -> 23, of which waited for: 3 -> 8; matrix products, arithmetic and copies ran while one was open for 2% -> 0% of each run, Pallas kernels for 38% -> 28%
where the time goes in v2:
time: 120 us
  starting transfers between devices  44.1 us (37%)
  Pallas kernels  41.7 us (35%)
  local copies, waits for them, and re-layouts  17.4 us (14%)
  waiting for transfers between devices  15.5 us (13%)
    all_to_all x4, starting transfers between devices, exchange(): lax.all_to_all(buffer, BOTH, 0, 0, axis_index_groups=plan.groups, tiled=T...  21 us
    unnamed x64, local copies, waits for them, and re-layouts  17.4 us
    all_to_all x4, waiting for transfers between devices, exchange(): lax.all_to_all(buffer, BOTH, 0, 0, axis_index_groups=plan.groups, tiled=T...  10.1 us
    ppermute x3, starting transfers between devices, per_device(): lax.ppermute(owned, 'ctx', route)  8.54 us
    pallas_call x1, Pallas kernels, per_device(): call(functools.partial(forward_kernel, chunks, rows, plan.order), COST[2]...  7.79 us
    pallas_call x1, Pallas kernels, per_device(): call(functools.partial(table_kernel, rows), COST[1], [table_type, ((chans...  7.2 us
    pallas_call x1, Pallas kernels, per_device(): call(functools.partial(backward_kernel, chunks, rows, plan.order), COST[4...  6.6 us
    pallas_call x1, Pallas kernels, per_device(): call(functools.partial(moment_kernel, chunks, rows, plan.order), COST[7],...  5.86 us
  transfers between devices with their start and end apart: 23, of which 8 were waited for; matrix products, arithmetic and copies ran while one was open for 0% of the time, Pallas kernels for 28%

profile of v2, /device:TPU:0, one launch (start us, length us, event | category | flops | bytes accessed | tf_op | source)
XLA Modules:
  0.0 119.6 jit_solution(9335588013385647187)
XLA Ops:
  0.6 0.0 copy-start.9
  0.7 1.2 %shard_map.204 = (f32[64,384]{1,0:T(8,128)S(1)}, f32[64,64]{1,0:T(8,128)S(1)}, bf16[80,1024]{1,0:T(8,128)(2,1)S(1)}) custom-call(f32[64,64]{1,0:T(8,128)} %refs_4_.1, f32[64,64]{1,0:T(8,128)} %freq.1, f32[64,64]{1,0:T(8,128)} %refs_6_.1, f32[64,64]{1,0:T(8,128)} %refs_7_.1, f32[1,64]{1,0:T(1,128)} %bitcast.8, f32[1,64]{1,0:T(1,128)} %bitcast.9, ...), custom_call_target="tpu_custom_call" | custom-call | flops 2000000000 | bytes 7000000 | tf_op jit(solution)/shard_map/pallas_call | solution.py:570
  1.9 0.0 copy-start.28
  1.9 0.7 collective-permute-start
  2.6 1.9 %shard_map.203 = bf16[8,4,64,128]{3,2,1,0:T(8,128)(2,1)} custom-call(s32[4]{0:T(128)S(1)} %copy-done.21, bf16[4,96,512]{2,1,0:T(8,128)(2,1)S(1)} %copy-done.9), custom_call_target="tpu_custom_call" | custom-call | flops 2000000000 | bytes 7000000 | tf_op jit(solution)/shard_map/pallas_call | solution.py:586
  4.5 9.9 %all-to-all-start = ((bf16[8,4,64,128]{3,2,1,0:T(8,128)(2,1)}), bf16[8,4,64,128]{3,2,1,0:T(8,128)(2,1)S(1)}, u32[]{:S(2)}, u32[]{:S(2)}) async-start(bf16[8,4,64,128]{3,2,1,0:T(8,128)(2,1)} %shard_map.203), calls=%async_computation | async-start | bytes 1048576 | tf_op jit(solution)/shard_map/all_to_all | solution.py:567
  14.4 2.7 %collective-permute-start.3 = (bf16[80,1024]{1,0:T(8,128)(2,1)S(1)}, bf16[80,1024]{1,0:T(8,128)(2,1)S(1)}, u32[]{:S(2)}, u32[]{:S(2)}) collective-permute-start(bf16[80,1024]{1,0:T(8,128)(2,1)S(1)} %get-tuple-element.73.refs_0_), channel_id=1, source_target_pairs={{0,24},{4,28},{8,0},{12,4},{16,8},{20,12},{24,16},{28,20},{1,25},{... | collective-permute-start | bytes 491528 | tf_op jit(solution)/shard_map/ppermute | solution.py:589
  17.2 0.6 collective-permute-start.1
  17.7 7.2 %shard_map.205 = (bf16[64,128,128]{2,1,0:T(8,128)(2,1)}, f32[64,8,128]{2,1,0:T(8,128)S(1)}, f32[2,64,128]{2,1,0:T(8,128)S(1)}) custom-call(f32[64,384]{1,0:T(8,128)S(1)} %collective-permute-done.pack), custom_call_target="tpu_custom_call" | custom-call | flops 8000000000 | bytes 28000000 | tf_op jit(solution)/shard_map/pallas_call | solution.py:591
  25.0 1.6 %copy-done = bf16[64,128,128]{2,1,0:T(8,128)(2,1)S(1)} copy-done((bf16[64,128,128]{2,1,0:T(8,128)(2,1)S(1)}, bf16[64,128,128]{2,1,0:T(8,128)(2,1)}, u32[]{:S(2)}) %copy-start) | copy-done | bytes 2097176
  26.6 7.8 %shard_map.206 = (bf16[8,4,64,128]{3,2,1,0:T(8,128)(2,1)}, bf16[2048,128]{1,0:T(8,128)(2,1)S(1)}) custom-call(bf16[8,4,64,128]{3,2,1,0:T(8,128)(2,1)S(1)} %all-to-all-done.arrived.first, f32[64,384]{1,0:T(8,128)S(1)} %collective-permute-done.pack, bf16[64,128,128]{2,1,0:T(8,128)(2,1)S(1)} %copy-done, f32[64,8,128]{2,1,0:T(8,128)S(1)} %get-tuple-element.69.lines), custom_call_target="tpu_custom_call" | custom-call | flops 10000000000 | bytes 35000000 | tf_op jit(solution)/shard_map/pallas_call | solution.py:601
  34.4 0.8 copy-done.2
  35.2 4.1 %all-to-all-start.1 = ((bf16[8,4,64,128]{3,2,1,0:T(8,128)(2,1)}), bf16[8,4,64,128]{3,2,1,0:T(8,128)(2,1)S(1)}, u32[]{:S(2)}, u32[]{:S(2)}) async-start(bf16[8,4,64,128]{3,2,1,0:T(8,128)(2,1)} %get-tuple-element.72), calls=%async_computation.1 | async-start | bytes 1048576 | tf_op jit(solution)/shard_map/all_to_all | solution.py:567
  39.3 0.5 collective-permute-start.4
  39.8 0.1 collective-permute-start.5
  39.9 0.4 collective-permute-start.6
  40.3 0.1 collective-permute-start.7
  40.4 0.4 collective-permute-done.4.refs_4_
  40.8 0.4 collective-permute-done.5.refs_5_
  41.2 0.2 collective-permute-done.6.refs_6_
  41.5 0.3 collective-permute-done.7.refs_7_
  41.7 0.1 shard_map.207
  41.8 1.0 copy-done.22
  42.8 6.2 %all-to-all-done.1.arrived = bf16[8,4,64,128]{3,2,1,0:T(8,128)(2,1)S(1)} async-done(((bf16[8,4,64,128]{3,2,1,0:T(8,128)(2,1)}), bf16[8,4,64,128]{3,2,1,0:T(8,128)(2,1)S(1)}, u32[]{:S(2)}, u32[]{:S(2)}) %all-to-all-start.1) | async-done | bytes 524320 | tf_op jit(solution)/shard_map/all_to_all | solution.py:567
  49.1 1.2 %copy-done.23 = bf16[512,1024]{1,0:T(8,128)(2,1)S(1)} copy-done((bf16[512,1024]{1,0:T(8,128)(2,1)S(1)}, bf16[512,1024]{1,0:T(8,128)(2,1)}, u32[]{:S(2)}) %copy-start.23) | copy-done | bytes 1048600
  50.3 3.9 %shard_map.208 = (bf16[4,96,512]{2,1,0:T(8,128)(2,1)}, bf16[8,4,64,128]{3,2,1,0:T(8,128)(2,1)}, bf16[512,1024]{1,0:T(8,128)(2,1)S(1)}) custom-call(s32[4]{0:T(128)S(1)} %copy-done.21, bf16[8,4,64,128]{3,2,1,0:T(8,128)(2,1)S(1)} %all-to-all-done.1.arrived, bf16[4,96,512]{2,1,0:T(8,128)(2,1)S(1)} %copy-done.9, bf16[4,96,512]{2,1,0:T(8,128)(2,1)S(1)} %copy-done.11, ...), custom_call_target="tpu_custom_call" | custom-call | flops 6000000000 | bytes 21000000 | tf_op jit(solution)/shard_map/pallas_call | solution.py:618
  54.2 0.7 shard_map.209
  55.0 0.8 copy-done.26
  55.8 3.5 %all-to-all-start.2 = ((bf16[8,4,64,128]{3,2,1,0:T(8,128)(2,1)}), bf16[8,4,64,128]{3,2,1,0:T(8,128)(2,1)S(1)}, u32[]{:S(2)}, u32[]{:S(2)}) async-start(bf16[8,4,64,128]{3,2,1,0:T(8,128)(2,1)} %get-tuple-element.80), calls=%async_computation.2 | async-start | bytes 1048576 | tf_op jit(solution)/shard_map/all_to_all | solution.py:567
  59.3 0.8 copy-done.5
  60.2 1.1 copy-done.6
  61.3 1.1 copy-done.27
  62.3 0.2 shard_map.210
  62.5 0.6 copy-done.13
  63.2 0.7 copy-done.14
  63.8 0.7 copy-done.15
  64.5 0.7 copy-done.24
  65.1 3.9 %all-to-all-done.2.arrived = bf16[8,4,64,128]{3,2,1,0:T(8,128)(2,1)S(1)} async-done(((bf16[8,4,64,128]{3,2,1,0:T(8,128)(2,1)}), bf16[8,4,64,128]{3,2,1,0:T(8,128)(2,1)S(1)}, u32[]{:S(2)}, u32[]{:S(2)}) %all-to-all-start.2) | async-done | bytes 524320 | tf_op jit(solution)/shard_map/all_to_all | solution.py:567
  69.0 2.9 %collective-permute-start.9 = (bf16[80,1024]{1,0:T(8,128)(2,1)}, bf16[80,1024]{1,0:T(8,128)(2,1)}, u32[]{:S(2)}, u32[]{:S(2)}) collective-permute-start(bf16[80,1024]{1,0:T(8,128)(2,1)} %copy-done.15), channel_id=1, source_target_pairs={{0,8},{4,12},{8,16},{12,20},{16,24},{20,28},{24,0},{28,4},{1,9},{5... | collective-permute-start | bytes 491528 | tf_op jit(solution)/shard_map/ppermute | solution.py:633
  71.9 0.9 collective-permute-start.10
  72.8 1.5 %collective-permute-start.11 = (bf16[80,1024]{1,0:T(8,128)(2,1)}, bf16[80,1024]{1,0:T(8,128)(2,1)}, u32[]{:S(2)}, u32[]{:S(2)}) collective-permute-start(bf16[80,1024]{1,0:T(8,128)(2,1)} %copy-done.13), channel_id=1, source_target_pairs={{0,24},{4,28},{8,0},{12,4},{16,8},{20,12},{24,16},{28,20},{1,25},{... | collective-permute-start | bytes 491528 | tf_op jit(solution)/shard_map/ppermute | solution.py:633
  74.3 1.0 copy-done.3
  75.3 6.6 %shard_map.211 = (bf16[8,4,64,128]{3,2,1,0:T(8,128)(2,1)S(1)}, bf16[2048,128]{1,0:T(8,128)(2,1)S(1)}, f32[2,64,128]{2,1,0:T(8,128)S(1)}) custom-call(bf16[8,4,64,128]{3,2,1,0:T(8,128)(2,1)S(1)} %all-to-all-done.2.arrived, bf16[8,4,64,128]{3,2,1,0:T(8,128)(2,1)S(1)} %all-to-all-done.arrived.first, f32[64,384]{1,0:T(8,128)S(1)} %collective-permute-done.pack, ...), custom_call_target="tpu_custom_call" | custom-call | flops 1000000000 | bytes 3500000 | tf_op jit(solution)/shard_map/pallas_call | solution.py:634
  81.9 0.8 copy-done.4
  82.7 0.8 copy-done.7
  83.5 0.6 copy-done.16
  84.2 3.5 %all-to-all-start.3 = ((bf16[8,4,64,128]{3,2,1,0:T(8,128)(2,1)}), bf16[8,4,64,128]{3,2,1,0:T(8,128)(2,1)S(1)}, u32[]{:S(2)}, u32[]{:S(2)}) async-start(bf16[8,4,64,128]{3,2,1,0:T(8,128)(2,1)} %copy-done.4), calls=%async_computation.3 | async-start | bytes 1048576 | tf_op jit(solution)/shard_map/all_to_all | solution.py:567
  87.7 0.0 copy-start.25
  87.7 1.0 copy-done.25
  88.7 1.9 %shard_map.213.refs_0_ = bf16[80,1024]{1,0:T(8,128)(2,1)} custom-call(bf16[80,1024]{1,0:T(8,128)(2,1)S(1)} %copy-done.25, bf16[80,1024]{1,0:T(8,128)(2,1)} %collective-permute-done.9.refs_1_, bf16[80,1024]{1,0:T(8,128)(2,1)} %collective-permute-done.10.refs_2_, bf16[80,1024]{1,0:T(8,128)(2,1)} %collective-permute-done.11.refs_3_), custom_call_target="tpu_custom_call" | custom-call | flops 1000000000 | bytes 3500000 | tf_op jit(solution)/shard_map/pallas_call | solution.py:641
  90.5 5.9 %shard_map.214 = bf16[80,256]{1,0:T(8,128)(2,1)S(1)} custom-call(bf16[8,4,64,128]{3,2,1,0:T(8,128)(2,1)S(1)} %all-to-all-done.arrived.first, f32[64,384]{1,0:T(8,128)S(1)} %collective-permute-done.pack, bf16[64,128,128]{2,1,0:T(8,128)(2,1)S(1)} %copy-done.1, f32[64,8,128]{2,1,0:T(8,128)S(1)} %get-tuple-element.69.lines, f32[2,64,128]{2,1,0:T(8,128)S(1)} %copy-done.31, ...), custom_call_target="tpu_custom_call" | custom-call | flops 8000000000 | bytes 28000000 | tf_op jit(solution)/shard_map/pallas_call | solution.py:644
  96.4 2.9 %collective-permute-start.15 = (bf16[80,256]{1,0:T(8,128)(2,1)S(1)}, bf16[80,256]{1,0:T(8,128)(2,1)S(1)}, u32[]{:S(2)}, u32[]{:S(2)}) collective-permute-start(bf16[80,256]{1,0:T(8,128)(2,1)S(1)} %shard_map.214), channel_id=1, source_target_pairs={{0,3},{4,7},{1,11},{5,15},{2,19},{6,23},{3,27},{7,31},{8,0},{12,4}... | collective-permute-start | bytes 122888 | tf_op jit(solution)/shard_map/ppermute | solution.py:656
  99.3 0.6 collective-permute-start.14
  99.9 0.1 collective-permute-start.13
  100.0 0.7 collective-permute-start.12
  100.6 7.4 %collective-permute-start.18 = (bf16[80,1024]{1,0:T(8,128)(2,1)}, bf16[80,1024]{1,0:T(8,128)(2,1)S(1)}, u32[]{:S(2)}, u32[]{:S(2)}) collective-permute-start(bf16[80,1024]{1,0:T(8,128)(2,1)} %shard_map.213.refs_0_), channel_id=1, source_target_pairs={{0,3},{1,0},{2,1},{3,2},{4,7},{5,4},{6,5},{7,6},{8,11},{9,8},{10,9... | collective-permute-start | bytes 491528 | tf_op jit(solution)/shard_map/ppermute | solution.py:657
  108.0 1.2 collective-permute-start.16
  109.2 1.0 copy-done.10
  110.2 1.0 copy-done.12
  111.2 1.8 %shard_map.212 = bf16[4,96,512]{2,1,0:T(8,128)(2,1)} custom-call(bf16[8,4,64,128]{3,2,1,0:T(8,128)(2,1)S(1)} %all-to-all-done.3.arrived, bf16[4,96,512]{2,1,0:T(8,128)(2,1)S(1)} %copy-done.10, bf16[4,96,512]{2,1,0:T(8,128)(2,1)S(1)} %copy-done.12), custom_call_target="tpu_custom_call" | custom-call | flops 3000000000 | bytes 10500000 | tf_op jit(solution)/shard_map/pallas_call | solution.py:652
  113.0 0.9 collective-permute-done.18.refs_3_
  113.9 3.1 %collective-permute-done.17.refs_2_ = bf16[80,1024]{1,0:T(8,128)(2,1)S(1)} collective-permute-done((bf16[80,1024]{1,0:T(8,128)(2,1)}, bf16[80,1024]{1,0:T(8,128)(2,1)S(1)}, u32[]{:S(2)}, u32[]{:S(2)}) %collective-permute-start.17) | collective-permute-done | bytes 163872 | tf_op jit(solution)/shard_map/ppermute | solution.py:657
  117.1 1.8 %shard_map.215 = (f32[64,1024]{1,0:T(8,128)}, f32[1,128]{1,0:T(1,128)}) custom-call(bf16[80,1024]{1,0:T(8,128)(2,1)} %shard_map.213.refs_0_, bf16[80,1024]{1,0:T(8,128)(2,1)S(1)} %collective-permute-done.16.refs_1_, bf16[80,1024]{1,0:T(8,128)(2,1)S(1)} %collective-permute-done.17.refs_2_, bf16[80,1024]{1,0:T(8,128)(2,1)S(1)} %collective-permute-done.18.refs_3_), custom_call_target="tpu_custom_call" | custom-call | flops 2000000000 | bytes 7000000 | tf_op jit(solution)/shard_map/pallas_call | solution.py:659
  118.9 0.8 shard_map.216
  (60 shorter events, 0.1 us)
Async XLA Ops:
  0.6 1.9 %copy-start.9 = (bf16[4,96,512]{2,1,0:T(8,128)(2,1)S(1)}, bf16[4,96,512]{2,1,0:T(8,128)(2,1)}, u32[]{:S(2)}) copy-start(bf16[4,96,512]{2,1,0:T(8,128)(2,1)} %tokens.5) | copy-start | bytes 1179652
  0.7 1.9 %copy-start.21 = (s32[4]{0:T(128)S(1)}, s32[4]{0:T(128)}, u32[]{:S(2)}) copy-start(s32[4]{0:T(128)} %lengths.3) | copy-start | bytes 52
  1.9 2.6 %copy-start.28 = (f32[64,64]{1,0:T(8,128)}, f32[64,64]{1,0:T(8,128)S(1)}, u32[]{:S(2)}) copy-start(f32[64,64]{1,0:T(8,128)S(1)} %get-tuple-element.111.refs_5_) | copy-start | bytes 49156
  1.9 12.5 %collective-permute-start = (f32[64,384]{1,0:T(8,128)S(1)}, f32[64,384]{1,0:T(8,128)S(1)}, u32[]{:S(2)}, u32[]{:S(2)}) collective-permute-start(f32[64,384]{1,0:T(8,128)S(1)} %get-tuple-element.66), channel_id=1, source_target_pairs={{0,0},{4,4},{8,1},{12,5},{16,2},{20,6},{24,3},{28,7},{1,8},{5,12},... | collective-permute-start | bytes 294920 | tf_op jit(solution)/shard_map/ppermute | solution.py:583
  4.5 20.5 %all-to-all-start = ((bf16[8,4,64,128]{3,2,1,0:T(8,128)(2,1)}), bf16[8,4,64,128]{3,2,1,0:T(8,128)(2,1)S(1)}, u32[]{:S(2)}, u32[]{:S(2)}) async-start(bf16[8,4,64,128]{3,2,1,0:T(8,128)(2,1)} %shard_map.203), calls=%async_computation | async-start | bytes 1048576 | tf_op jit(solution)/shard_map/all_to_all | solution.py:567
  14.4 20.7 %collective-permute-start.3 = (bf16[80,1024]{1,0:T(8,128)(2,1)S(1)}, bf16[80,1024]{1,0:T(8,128)(2,1)S(1)}, u32[]{:S(2)}, u32[]{:S(2)}) collective-permute-start(bf16[80,1024]{1,0:T(8,128)(2,1)S(1)} %get-tuple-element.73.refs_0_), channel_id=1, source_target_pairs={{0,24},{4,28},{8,0},{12,4},{16,8},{20,12},{24,16},{28,20},{1,25},{... | collective-permute-start | bytes 491528 | tf_op jit(solution)/shard_map/ppermute | solution.py:589
  17.2 18.0 %collective-permute-start.2 = (bf16[80,1024]{1,0:T(8,128)(2,1)S(1)}, bf16[80,1024]{1,0:T(8,128)(2,1)S(1)}, u32[]{:S(2)}, u32[]{:S(2)}) collective-permute-start(bf16[80,1024]{1,0:T(8,128)(2,1)S(1)} %get-tuple-element.73.refs_0_), channel_id=1, source_target_pairs={{0,16},{4,20},{8,24},{12,28},{16,0},{20,4},{24,8},{28,12},{1,17},{... | collective-permute-start | bytes 491528 | tf_op jit(solution)/shard_map/ppermute | solution.py:589
  17.2 18.0 %collective-permute-start.1 = (bf16[80,1024]{1,0:T(8,128)(2,1)S(1)}, bf16[80,1024]{1,0:T(8,128)(2,1)S(1)}, u32[]{:S(2)}, u32[]{:S(2)}) collective-permute-start(bf16[80,1024]{1,0:T(8,128)(2,1)S(1)} %get-tuple-element.73.refs_0_), channel_id=1, source_target_pairs={{0,8},{4,12},{8,16},{12,20},{16,24},{20,28},{24,0},{28,4},{1,9},{5... | collective-permute-start | bytes 491528 | tf_op jit(solution)/shard_map/ppermute | solution.py:589
  24.9 9.4 %copy-start.30 = (f32[2,64,128]{2,1,0:T(8,128)}, f32[2,64,128]{2,1,0:T(8,128)S(1)}, u32[]{:S(2)}) copy-start(f32[2,64,128]{2,1,0:T(8,128)S(1)} %get-tuple-element.91.firsts) | copy-start | bytes 196612
  25.0 1.6 %copy-start = (bf16[64,128,128]{2,1,0:T(8,128)(2,1)S(1)}, bf16[64,128,128]{2,1,0:T(8,128)(2,1)}, u32[]{:S(2)}) copy-start(bf16[64,128,128]{2,1,0:T(8,128)(2,1)} %get-tuple-element.68.far_table.table) | copy-start | bytes 6291460
  34.4 0.8 copy-start.2
  35.2 13.9 %all-to-all-start.1 = ((bf16[8,4,64,128]{3,2,1,0:T(8,128)(2,1)}), bf16[8,4,64,128]{3,2,1,0:T(8,128)(2,1)S(1)}, u32[]{:S(2)}, u32[]{:S(2)}) async-start(bf16[8,4,64,128]{3,2,1,0:T(8,128)(2,1)} %get-tuple-element.72), calls=%async_computation.1 | async-start | bytes 1048576 | tf_op jit(solution)/shard_map/all_to_all | solution.py:567
  39.3 9.7 %copy-start.11 = (bf16[4,96,512]{2,1,0:T(8,128)(2,1)S(1)}, bf16[4,96,512]{2,1,0:T(8,128)(2,1)}, u32[]{:S(2)}) copy-start(bf16[4,96,512]{2,1,0:T(8,128)(2,1)} %cotangent.3) | copy-start | bytes 1179652
  39.3 1.5 %collective-permute-start.4 = (bf16[80,1024]{1,0:T(8,128)(2,1)S(1)}, bf16[80,1024]{1,0:T(8,128)(2,1)S(1)}, u32[]{:S(2)}, u32[]{:S(2)}) collective-permute-start(bf16[80,1024]{1,0:T(8,128)(2,1)S(1)} %get-tuple-element.73.refs_0_), channel_id=1, source_target_pairs={{0,4},{4,0},{8,12},{12,8},{16,20},{20,16},{24,28},{28,24},{1,5},{5... | collective-permute-start | bytes 491528 | tf_op jit(solution)/shard_map/ppermute | solution.py:609
  39.8 1.4 %collective-permute-start.5 = (bf16[80,1024]{1,0:T(8,128)(2,1)S(1)}, bf16[80,1024]{1,0:T(8,128)(2,1)S(1)}, u32[]{:S(2)}, u32[]{:S(2)}) collective-permute-start(bf16[80,1024]{1,0:T(8,128)(2,1)S(1)} %collective-permute-done.1.refs_1_), channel_id=1, source_target_pairs={{0,4},{4,0},{8,12},{12,8},{16,20},{20,16},{24,28},{28,24},{1,5},{5... | collective-permute-start | bytes 491528 | tf_op jit(solution)/shard_map/ppermute | solution.py:609
  39.9 1.6 %collective-permute-start.6 = (bf16[80,1024]{1,0:T(8,128)(2,1)S(1)}, bf16[80,1024]{1,0:T(8,128)(2,1)S(1)}, u32[]{:S(2)}, u32[]{:S(2)}) collective-permute-start(bf16[80,1024]{1,0:T(8,128)(2,1)S(1)} %collective-permute-done.2.refs_2_), channel_id=1, source_target_pairs={{0,4},{4,0},{8,12},{12,8},{16,20},{20,16},{24,28},{28,24},{1,5},{5... | collective-permute-start | bytes 491528 | tf_op jit(solution)/shard_map/ppermute | solution.py:609
  40.3 1.4 %collective-permute-start.7 = (bf16[80,1024]{1,0:T(8,128)(2,1)S(1)}, bf16[80,1024]{1,0:T(8,128)(2,1)S(1)}, u32[]{:S(2)}, u32[]{:S(2)}) collective-permute-start(bf16[80,1024]{1,0:T(8,128)(2,1)S(1)} %collective-permute-done.3.refs_3_), channel_id=1, source_target_pairs={{0,4},{4,0},{8,12},{12,8},{16,20},{20,16},{24,28},{28,24},{1,5},{5... | collective-permute-start | bytes 491528 | tf_op jit(solution)/shard_map/ppermute | solution.py:609
  41.8 1.0 copy-start.22
  49.1 1.2 %copy-start.23 = (bf16[512,1024]{1,0:T(8,128)(2,1)S(1)}, bf16[512,1024]{1,0:T(8,128)(2,1)}, u32[]{:S(2)}) copy-start(bf16[512,1024]{1,0:T(8,128)(2,1)} %copy-done.22) | copy-start | bytes 3145732
  55.0 0.9 copy-start.26
  55.8 3.5 %collective-permute-start.8 = (bf16[4,80,1024]{2,1,0:T(8,128)(2,1)S(1)}, bf16[4,80,1024]{2,1,0:T(8,128)(2,1)S(1)}, u32[]{:S(2)}, u32[]{:S(2)}) collective-permute-start(bf16[4,80,1024]{2,1,0:T(8,128)(2,1)S(1)} %get-tuple-element.83), channel_id=1, source_target_pairs={{0,4},{4,0},{8,12},{12,8},{16,20},{20,16},{24,28},{28,24},{1,5},{5... | collective-permute-start | bytes 1966088 | tf_op jit(solution)/shard_map/ppermute | solution.py:627
  55.8 13.2 %all-to-all-start.2 = ((bf16[8,4,64,128]{3,2,1,0:T(8,128)(2,1)}), bf16[8,4,64,128]{3,2,1,0:T(8,128)(2,1)S(1)}, u32[]{:S(2)}, u32[]{:S(2)}) async-start(bf16[8,4,64,128]{3,2,1,0:T(8,128)(2,1)} %get-tuple-element.80), calls=%async_computation.2 | async-start | bytes 1048576 | tf_op jit(solution)/shard_map/all_to_all | solution.py:567
  59.3 0.8 copy-start.5
  60.2 1.1 copy-start.6
  61.3 1.1 copy-start.27
  62.3 11.9 %copy-start.1 = (bf16[64,128,128]{2,1,0:T(8,128)(2,1)S(1)}, bf16[64,128,128]{2,1,0:T(8,128)(2,1)}, u32[]{:S(2)}) copy-start(bf16[64,128,128]{2,1,0:T(8,128)(2,1)} %get-tuple-element.68.far_table.table) | copy-start | bytes 6291460
  62.5 0.7 copy-start.13
  63.2 0.7 copy-start.14
  63.8 0.7 copy-start.15
  64.5 0.7 copy-start.24
  69.0 18.7 %collective-permute-start.9 = (bf16[80,1024]{1,0:T(8,128)(2,1)}, bf16[80,1024]{1,0:T(8,128)(2,1)}, u32[]{:S(2)}, u32[]{:S(2)}) collective-permute-start(bf16[80,1024]{1,0:T(8,128)(2,1)} %copy-done.15), channel_id=1, source_target_pairs={{0,8},{4,12},{8,16},{12,20},{16,24},{20,28},{24,0},{28,4},{1,9},{5... | collective-permute-start | bytes 491528 | tf_op jit(solution)/shard_map/ppermute | solution.py:633
  71.9 15.8 %collective-permute-start.10 = (bf16[80,1024]{1,0:T(8,128)(2,1)}, bf16[80,1024]{1,0:T(8,128)(2,1)}, u32[]{:S(2)}, u32[]{:S(2)}) collective-permute-start(bf16[80,1024]{1,0:T(8,128)(2,1)} %copy-done.14), channel_id=1, source_target_pairs={{0,16},{4,20},{8,24},{12,28},{16,0},{20,4},{24,8},{28,12},{1,17},{... | collective-permute-start | bytes 491528 | tf_op jit(solution)/shard_map/ppermute | solution.py:633
  72.8 14.9 %collective-permute-start.11 = (bf16[80,1024]{1,0:T(8,128)(2,1)}, bf16[80,1024]{1,0:T(8,128)(2,1)}, u32[]{:S(2)}, u32[]{:S(2)}) collective-permute-start(bf16[80,1024]{1,0:T(8,128)(2,1)} %copy-done.13), channel_id=1, source_target_pairs={{0,24},{4,28},{8,0},{12,4},{16,8},{20,12},{24,16},{28,20},{1,25},{... | collective-permute-start | bytes 491528 | tf_op jit(solution)/shard_map/ppermute | solution.py:633
  74.3 1.0 copy-start.3
  81.9 0.8 copy-start.4
  82.7 0.8 copy-start.7
  83.5 0.6 copy-start.16
  84.2 25.0 %all-to-all-start.3 = ((bf16[8,4,64,128]{3,2,1,0:T(8,128)(2,1)}), bf16[8,4,64,128]{3,2,1,0:T(8,128)(2,1)S(1)}, u32[]{:S(2)}, u32[]{:S(2)}) async-start(bf16[8,4,64,128]{3,2,1,0:T(8,128)(2,1)} %copy-done.4), calls=%async_computation.3 | async-start | bytes 1048576 | tf_op jit(solution)/shard_map/all_to_all | solution.py:567
  87.7 2.9 %copy-start.8 = (bf16[2048,128]{1,0:T(8,128)(2,1)S(1)}, bf16[2048,128]{1,0:T(8,128)(2,1)}, u32[]{:S(2)}) copy-start(bf16[2048,128]{1,0:T(8,128)(2,1)} %copy-done.7) | copy-start | bytes 1572868
  87.7 2.9 %copy-start.17 = (f32[2,64,128]{2,1,0:T(8,128)S(1)}, f32[2,64,128]{2,1,0:T(8,128)}, u32[]{:S(2)}) copy-start(f32[2,64,128]{2,1,0:T(8,128)} %copy-done.16) | copy-start | bytes 196612
  87.7 1.0 copy-start.25
  88.7 1.9 %copy-start.31 = (f32[2,64,128]{2,1,0:T(8,128)S(1)}, f32[2,64,128]{2,1,0:T(8,128)}, u32[]{:S(2)}) copy-start(f32[2,64,128]{2,1,0:T(8,128)} %copy-done.30) | copy-start | bytes 196612
  96.4 11.6 %collective-permute-start.15 = (bf16[80,256]{1,0:T(8,128)(2,1)S(1)}, bf16[80,256]{1,0:T(8,128)(2,1)S(1)}, u32[]{:S(2)}, u32[]{:S(2)}) collective-permute-start(bf16[80,256]{1,0:T(8,128)(2,1)S(1)} %shard_map.214), channel_id=1, source_target_pairs={{0,3},{4,7},{1,11},{5,15},{2,19},{6,23},{3,27},{7,31},{8,0},{12,4}... | collective-permute-start | bytes 122888 | tf_op jit(solution)/shard_map/ppermute | solution.py:656
  99.3 8.7 %collective-permute-start.14 = (bf16[80,256]{1,0:T(8,128)(2,1)S(1)}, bf16[80,256]{1,0:T(8,128)(2,1)S(1)}, u32[]{:S(2)}, u32[]{:S(2)}) collective-permute-start(bf16[80,256]{1,0:T(8,128)(2,1)S(1)} %shard_map.214), channel_id=1, source_target_pairs={{0,2},{4,6},{1,10},{5,14},{2,18},{6,22},{3,26},{7,30},{8,3},{12,7}... | collective-permute-start | bytes 122888 | tf_op jit(solution)/shard_map/ppermute | solution.py:656
  99.9 13.1 %collective-permute-start.13 = (bf16[80,256]{1,0:T(8,128)(2,1)S(1)}, bf16[80,256]{1,0:T(8,128)(2,1)S(1)}, u32[]{:S(2)}, u32[]{:S(2)}) collective-permute-start(bf16[80,256]{1,0:T(8,128)(2,1)S(1)} %shard_map.214), channel_id=1, source_target_pairs={{0,1},{4,5},{1,9},{5,13},{2,17},{6,21},{3,25},{7,29},{8,2},{12,6},... | collective-permute-start | bytes 122888 | tf_op jit(solution)/shard_map/ppermute | solution.py:656
  100.0 13.0 %collective-permute-start.12 = (bf16[80,256]{1,0:T(8,128)(2,1)S(1)}, bf16[80,256]{1,0:T(8,128)(2,1)S(1)}, u32[]{:S(2)}, u32[]{:S(2)}) collective-permute-start(bf16[80,256]{1,0:T(8,128)(2,1)S(1)} %shard_map.214), channel_id=1, source_target_pairs={{0,0},{4,4},{1,8},{5,12},{2,16},{6,20},{3,24},{7,28},{8,1},{12,5},... | collective-permute-start | bytes 122888 | tf_op jit(solution)/shard_map/ppermute | solution.py:656
  100.6 13.3 %collective-permute-start.18 = (bf16[80,1024]{1,0:T(8,128)(2,1)}, bf16[80,1024]{1,0:T(8,128)(2,1)S(1)}, u32[]{:S(2)}, u32[]{:S(2)}) collective-permute-start(bf16[80,1024]{1,0:T(8,128)(2,1)} %shard_map.213.refs_0_), channel_id=1, source_target_pairs={{0,3},{1,0},{2,1},{3,2},{4,7},{5,4},{6,5},{7,6},{8,11},{9,8},{10,9... | collective-permute-start | bytes 491528 | tf_op jit(solution)/shard_map/ppermute | solution.py:657
  108.0 9.0 %collective-permute-start.17 = (bf16[80,1024]{1,0:T(8,128)(2,1)}, bf16[80,1024]{1,0:T(8,128)(2,1)S(1)}, u32[]{:S(2)}, u32[]{:S(2)}) collective-permute-start(bf16[80,1024]{1,0:T(8,128)(2,1)} %shard_map.213.refs_0_), channel_id=1, source_target_pairs={{0,2},{1,3},{2,0},{3,1},{4,6},{5,7},{6,4},{7,5},{8,10},{9,11},{10,... | collective-permute-start | bytes 491528 | tf_op jit(solution)/shard_map/ppermute | solution.py:657
  108.0 9.0 %collective-permute-start.16 = (bf16[80,1024]{1,0:T(8,128)(2,1)}, bf16[80,1024]{1,0:T(8,128)(2,1)S(1)}, u32[]{:S(2)}, u32[]{:S(2)}) collective-permute-start(bf16[80,1024]{1,0:T(8,128)(2,1)} %shard_map.213.refs_0_), channel_id=1, source_target_pairs={{0,1},{1,2},{2,3},{3,0},{4,5},{5,6},{6,7},{7,4},{8,9},{9,10},{10,1... | collective-permute-start | bytes 491528 | tf_op jit(solution)/shard_map/ppermute | solution.py:657
  109.2 1.0 copy-start.10
  110.2 1.0 copy-start.12
  113.0 5.9 %copy-start.18 = (f32[64,64]{1,0:T(8,128)S(1)}, f32[64,64]{1,0:T(8,128)}, u32[]{:S(2)}) copy-start(f32[64,64]{1,0:T(8,128)} %refs_4_.1) | copy-start | bytes 49156
  113.0 5.9 %copy-start.19 = (f32[64,64]{1,0:T(8,128)S(1)}, f32[64,64]{1,0:T(8,128)}, u32[]{:S(2)}) copy-start(f32[64,64]{1,0:T(8,128)} %refs_6_.1) | copy-start | bytes 49156
  113.0 5.9 %copy-start.20 = (f32[64,64]{1,0:T(8,128)S(1)}, f32[64,64]{1,0:T(8,128)}, u32[]{:S(2)}) copy-start(f32[64,64]{1,0:T(8,128)} %refs_7_.1) | copy-start | bytes 49156
  113.0 5.9 %copy-start.29 = (f32[64,64]{1,0:T(8,128)S(1)}, f32[64,64]{1,0:T(8,128)}, u32[]{:S(2)}) copy-start(f32[64,64]{1,0:T(8,128)} %copy-done.28) | copy-start | bytes 49156

commit v3 on v2

--- a/solution.py
+++ b/solution.py
@@ -10,7 +10,7 @@
 
 EPSILON = 1e-05
 LANES = 128
-GROUP = 8
+GROUPS = (32, 16, 16, 16)
 COST = (2, 8, 10, 6, 1, 3, 2, 8)
 BOTH = ("shard", "ctx")
 F32 = jnp.float32
@@ -46,8 +46,8 @@
 
         self.fetch = [(owner(*m, 0), here(*m)) for m in members]
         self.give = [[(here(*m), owner(*m, turn)) for m in members] for turn in range(chunks)]
-        self.rotate = [
-            [(a, (a + turn) % chunks) for a in range(chunks)] for turn in range(1, chunks)
+        self.fold = [
+            [(a, a ^ (1 << bit)) for a in range(chunks)] for bit in range((chunks - 1).bit_length())
         ]
         self.layers = layers
         self.climb = [
@@ -91,6 +91,17 @@
     piece[own:] = jnp.broadcast_to(row, (piece.shape[0] - own, wide)).astype(BF16)
 
 
+def copying(source, target, sem):
+    copy = pltpu.make_async_copy(source, target, sem)
+    copy.start()
+    return copy
+
+
+def wait_all(copies):
+    for copy in copies:
+        copy.wait()
+
+
 def valid_count(lengths, n, rows):
     return jnp.clip(lengths[n] - lax.axis_index("ctx") * rows, 0, rows)
 
@@ -111,7 +122,7 @@
     return pltpu.roll(values, LANES // 2, values.ndim - 1)
 
 
-def table_kernel(rows, pack, table, lines, firsts):
+def table_kernel(rows, pack, far_table, far_lines, firsts, table, lines, sems):
     chans = pack.shape[0]
     low2 = lax.broadcasted_iota(jnp.int32, (1, LANES), 1) < LANES // 2
     low3 = low2[None]
@@ -144,6 +155,7 @@
             table[here, size : 2 * size] = new.astype(BF16)
             part = jnp.concatenate([part, new], axis=1)
             size *= 2
+        copying(table.at[here], far_table.at[here], sems.at[at])
         real = jnp.where(low2, real, -real)
         whole = part.astype(BF16)
         hat = jnp.where(low2, real, -imag).astype(BF16)
@@ -162,7 +174,12 @@
             lines[here, k + 1 : k + 2] = line[:, None, :]
         return 0
 
-    lax.fori_loop(0, chans // step, block, 0)
+    count = chans // step
+    lax.fori_loop(0, count, block, 0, unroll=min(4, count))
+    for at in range(count):
+        here = pl.ds(at * step, step)
+        pltpu.make_async_copy(table.at[here], far_table.at[here], sems.at[at]).wait()
+    copying(lines, far_lines, sems.at[count]).wait()
 
 
 def upper_half(rows):
@@ -187,11 +204,37 @@
     return (c * 2 + core) * seqs + n
 
 
+def fetch_tables(size, far_table, table, far_lines, lines, sems):
+    count = table.shape[0] // size
+    copying(far_lines, lines, sems.at[count])
+    for at in range(count):
+        here = pl.ds(at * size, size)
+        copying(far_table.at[here], table.at[here], sems.at[at])
+
+
+def await_table(size, far_table, table, sems, at):
+    here = pl.ds(at * size, size)
+    pltpu.make_async_copy(far_table.at[here], table.at[here], sems.at[at]).wait()
+
+
+def await_lines(size, far_lines, lines, sems):
+    pltpu.make_async_copy(far_lines, lines, sems.at[lines.shape[0] // size]).wait()
+
+
+def gelu_and_slope(x):
+    c = math.sqrt(2.0 / math.pi)
+    square = x * x
+    t = jnp.tanh(c * x * (1.0 + 0.044715 * square))
+    half = 0.5 * (1.0 + t)
+    return x * half, half + 0.5 * x * (1.0 - t * t) * (c + 3.0 * 0.044715 * c * square)
+
+
 def forward_kernel(
-    chunks, rows, order, arrived, pack, far_table, lines, hidden, kept, inputs, mirrored, mixed, table, sem,
+    chunks, rows, order, arrived, pack, far_table, far_lines, far_hidden, far_kept,
+    inputs, mirrored, mixed, hidden, kept, table, lines, sems, out_sems,
 ):
-    fetch = pltpu.make_async_copy(far_table, table, sem)
-    fetch.start()
+    size = min(GROUPS[0], far_table.shape[0])
+    fetch_tables(size, far_table, table, far_lines, lines, sems)
     blocks, seqs, chans, _ = arrived.shape
     total = blocks * seqs
     each = 2 * seqs
@@ -208,10 +251,11 @@
             mirrored[here, :] = dot(x, mirror, (1, 0))
 
     def group(at, _):
-        members = range(GROUP)
-        mine = [pl.ds(at * GROUP + k, total, stride=chans) for k in members]
-        line = [lines[at * GROUP + k] for k in members]
-        ends = [dot(mirrored[mine[k], :].astype(BF16), table[at * GROUP + k], (1, 0)) for k in members]
+        members = range(size)
+        await_table(size, far_table, table, sems, at)
+        mine = [pl.ds(at * size + k, total, stride=chans) for k in members]
+        line = [lines[at * size + k] for k in members]
+        ends = [dot(mirrored[mine[k], :].astype(BF16), table[at * size + k], (1, 0)) for k in members]
         local = [
             dot(inputs[mine[k], :].astype(BF16), toeplitz(upper, line[k][0:1]), (1, 0)) for k in members
         ]
@@ -225,48 +269,48 @@
                     state += ends[k][each * c : each * (c + 1)]
             ends[k] = jnp.concatenate(carried, axis=0).astype(BF16)
         for k in members:
-            mixed[mine[k], :] = local[k] + dot(ends[k], table[at * GROUP + k], (1, 1))
+            mixed[mine[k], :] = local[k] + dot(ends[k], table[at * size + k], (1, 1))
         return 0
 
-    fetch.wait()
-    lax.fori_loop(0, chans // GROUP, group, 0)
+    await_lines(size, far_lines, lines, sems)
+    lax.fori_loop(0, chans // size, group, 0)
+    stored = []
     skip = pack[:, 256:257]
     for b in range(blocks):
         for n in range(seqs):
             here = pl.ds(place(order, seqs, b, n) * chans, chans)
             mix = mixed[here, :] + skip * inputs[here, :]
-            kept[here, :] = mix.astype(BF16)
-            hidden[b, n] = jax.nn.gelu(mix).astype(BF16)
-
-
-def weight_kernel(plan, *refs):
-    pieces, (w, bias) = refs[:-2], refs[-2:]
+            value, slope = gelu_and_slope(mix)
+            kept[here, :] = slope.astype(BF16)
+            hidden[b, n] = value.astype(BF16)
+        here = pl.ds(place(order, seqs, b, 0) * chans, seqs * chans)
+        stored.append(copying(hidden.at[b], far_hidden.at[b], out_sems.at[0, b]))
+        stored.append(copying(kept.at[here], far_kept.at[here], out_sems.at[1, b]))
+    wait_all(stored)
+
+
+def glu_kernel(plan, lengths, arrived, tokens, cotangent, *refs):
     layers = plan.layers
-    width = w.shape[0]
+    pieces, (block_out, leaving, outers, w) = refs[: 2 * layers], refs[2 * layers :]
+    seqs, rows, width = tokens.shape
+    blocks, _, chans, _ = arrived.shape
     own = width // plan.shards
     shard = lax.axis_index("shard")
     layer, core = shard // 2, lax.rem(shard, 2)
-    total = jnp.zeros((1, 2 * width), F32)
+    bias = jnp.zeros((1, 2 * width), F32)
     for side in range(2):
         for turn in range(layers):
             piece = pieces[side * layers + turn]
             home = 2 * lax.rem(layer + layers - turn, layers) + lax.rem(core + side, 2)
             w[pl.ds(pl.multiple_of(home * own, own), own), :] = piece[0:own]
-            total += piece[own : own + 1].astype(F32)
-    bias[...] = total
-
-
-def glu_kernel(lengths, arrived, tokens, cotangent, w, bias, block_out, leaving, outers):
-    seqs, rows, width = tokens.shape
-    blocks, _, chans, _ = arrived.shape
+            bias += piece[own : own + 1].astype(F32)
     position = lax.broadcasted_iota(jnp.int32, (rows, width), 0)
     for n in range(seqs):
         hidden = arrived[:, n].reshape(width, LANES).astype(F32).T.astype(BF16)
-        proj = dot(hidden, w[...], (1, 0)) + bias[...]
+        proj = dot(hidden, w[...], (1, 0)) + bias
         r, q = proj[0:rows, :width], proj[0:rows, width:]
         valid = jnp.where(position < valid_count(lengths, n, rows), 1.0, 0.0)
         open_ = jax.nn.sigmoid(q)
-        block_out[n] = (tokens[n].astype(F32) + valid * (r * open_)).astype(BF16)
         e = valid * cotangent[n].astype(F32)
         first = e * open_
         both = jnp.concatenate([first, first * r * (1.0 - open_)], axis=1).astype(BF16)
@@ -274,6 +318,7 @@
         back = dot(both, w[...], (1, 1))
         leaving[:, n] = back.T.astype(BF16).reshape(blocks, chans, LANES)
         outers[pl.ds(n * LANES, LANES), :] = both
+        block_out[n] = (tokens[n].astype(F32) + valid * (r * open_)).astype(BF16)
 
 
 def outer_kernel(plan, arrived, outers, kept, sent):
@@ -300,18 +345,12 @@
             out[z, own:] = tail
 
 
-def gelu_slope(x):
-    c = math.sqrt(2.0 / math.pi)
-    t = jnp.tanh(c * (x + 0.044715 * x * x * x))
-    return 0.5 * (1.0 + t) + 0.5 * x * (1.0 - t * t) * (c * (1.0 + 3.0 * 0.044715 * x * x))
-
-
 def backward_kernel(
-    chunks, rows, order, arrived, first, pack, far_table, lines, mixed,
-    leaving, kept, tallies, grads, local, cross, table, sem,
+    chunks, rows, order, arrived, first, pack, far_table, far_lines, far_slope,
+    far_leaving, far_kept, tallies,
+    grads, local, cross, slope, kept, leaving, table, lines, sems, more_sems,
 ):
-    fetch = pltpu.make_async_copy(far_table, table, sem)
-    fetch.start()
+    size = min(GROUPS[1], far_table.shape[0])
     blocks, seqs, chans, _ = arrived.shape
     total = blocks * seqs
     each = 2 * seqs
@@ -319,21 +358,29 @@
     skip, gain = pack[:, 256:257], pack[:, 257:258]
     mirror = mirror_matrix(rows)
     upper = upper_half(rows)
+    spans = [pl.ds(place(order, seqs, b, 0) * chans, seqs * chans) for b in range(blocks)]
+    fetched = [
+        copying(far_slope.at[span], slope.at[span], more_sems.at[0, b]) for b, span in enumerate(spans)
+    ]
+    fetch_tables(size, far_table, table, far_lines, lines, sems)
+    stored = []
     for b in range(blocks):
+        fetched[b].wait()
         for n in range(seqs):
             here = pl.ds(place(order, seqs, b, n) * chans, chans)
-            g = (arrived[b, n].astype(F32) * gelu_slope(mixed[here, :].astype(F32))).astype(BF16)
-            kept[here, :] = g
+            g = (arrived[b, n].astype(F32) * slope[here, :].astype(F32)).astype(BF16)
             grads[here, :] = g.astype(F32)
 
     def group(at, _):
-        members = range(GROUP)
-        which = [at * GROUP + k for k in members]
+        members = range(size)
+        await_table(size, far_table, table, sems, at)
+        which = [at * size + k for k in members]
         mine = [pl.ds(h, total, stride=chans) for h in which]
         line = [lines[h] for h in which]
         ends = [dot(grads[mine[k], :].astype(BF16), table[which[k]], (1, 0)) for k in members]
         for k in members:
             g = grads[mine[k], :].astype(BF16)
+            kept[which[k]] = g
             local[mine[k], :] = dot(g, toeplitz(upper, line[k][0:1]), (1, 1))
         for k in members:
             parts = [jnp.zeros((each, LANES), F32)]
@@ -348,8 +395,9 @@
             cross[mine[k], :] = dot(ends[k], table[which[k]], (1, 1))
         return 0
 
-    fetch.wait()
-    lax.fori_loop(0, chans // GROUP, group, 0)
+    await_lines(size, far_lines, lines, sems)
+    lax.fori_loop(0, chans // size, group, 0)
+    stored.append(copying(kept, far_kept, more_sems.at[1, 0]))
     gains = shifts = jnp.zeros((chans, LANES), F32)
     for b in range(blocks):
         for n in range(seqs):
@@ -361,84 +409,122 @@
             gains += m * xhat
             shifts += m
             leaving[b, n] = (gain * m).astype(BF16)
+        stored.append(copying(leaving.at[b], far_leaving.at[b], more_sems.at[2, b]))
     tallies[0] = gains
     tallies[1] = shifts
-
-
-def moment_kernel(
-    chunks, rows, order, first, pack, table, lines, firsts, kept, tallies, sums, mirrored, grads,
-    cross_one_a, cross_one_b, cross_two_a, cross_two_b, local_one, local_two,
+    wait_all(stored)
+
+
+def prefix_kernel(
+    chunks, rows, order, first, pack, far_table, far_lines, far_mirrored, far_prefix,
+    mirrored, kept, prefix, table, lines, sems, out_sems,
 ):
+    size = min(GROUPS[2], far_table.shape[0])
+    fetch_tables(size, far_table, table, far_lines, lines, sems)
     blocks, seqs, chans, _ = first.shape
     total = blocks * seqs
     each = 2 * seqs
     lane = lax.broadcasted_iota(jnp.int32, (1, LANES), 1).astype(F32)
     gain, shift = pack[:, 257:258], pack[:, 258:259]
     mirror = mirror_matrix(rows)
-    skips = jnp.zeros((chans, LANES), F32)
     for b in range(blocks):
         for n in range(seqs):
             here = pl.ds(place(order, seqs, b, n) * chans, chans)
             xhat = first[b, n].astype(F32)
             x = jnp.where(lane < xhat[0:1, LANES - 1 :], xhat * gain + shift, 0.0).astype(BF16)
             mirrored[here, :] = dot(x, mirror, (1, 0))
-            g = kept[here, :].astype(F32)
-            grads[here, :] = g
-            skips += g * x.astype(F32)
+
+    def group(at, _):
+        members = range(size)
+        await_table(size, far_table, table, sems, at)
+        which = [at * size + k for k in members]
+        line = [lines[h] for h in which]
+        ends = []
+        for k in members:
+            x_back = mirrored[pl.ds(which[k], total, stride=chans), :]
+            kept[which[k]] = x_back.astype(BF16)
+            stack = jnp.concatenate([x_back, x_back * lane], axis=0).astype(BF16)
+            ends.append(dot(stack, table[which[k]], (1, 0)))
+        for k in members:
+
+            def onward(state):
+                return state * line[k][1:2] + swap(state) * line[k][2:3]
+
+            state, slope = ends[k][0:each], ends[k][total : total + each]
+            states, slopes = [state], [state + slope]
+            for c in range(1, chunks - 1):
+                slope = onward(slope + float(rows) * state) + ends[k][total + each * c : total + each * (c + 1)]
+                state = onward(state) + ends[k][each * c : each * (c + 1)]
+                states.append(state)
+                slopes.append(state + slope)
+            prefix[which[k]] = jnp.concatenate(states + slopes, axis=0).astype(BF16)
+        return 0
+
+    await_lines(size, far_lines, lines, sems)
+    lax.fori_loop(0, chans // size, group, 0)
+    wait_all([copying(kept, far_mirrored, out_sems.at[0]), copying(prefix, far_prefix, out_sems.at[1])])
+
+
+def moment_kernel(
+    chunks, rows, far_table, far_mirrored, far_prefix, far_grads, firsts, tallies, sums,
+    cross_one_a, cross_one_b, cross_two_a, cross_two_b, local_one, local_two, corrs,
+    table, mirrored, prefix, grads, sems,
+):
+    size = min(GROUPS[3], far_table.shape[0])
+    chans, total, _ = far_grads.shape
+    each = total // chunks
+    count = chans // size
+    pairs = (
+        (far_grads, grads), (far_table, table), (far_mirrored, mirrored), (far_prefix, prefix)
+    )
+    for at in range(count):
+        here = pl.ds(at * size, size)
+        for k, (far, near) in enumerate(pairs):
+            copying(far.at[here], near.at[here], sems.at[k, at])
+    lane = lax.broadcasted_iota(jnp.int32, (1, LANES), 1).astype(F32)
     square = (rows, LANES)
     behind = lax.broadcasted_iota(jnp.int32, square, 1) <= (
         LANES - rows + lax.broadcasted_iota(jnp.int32, square, 0)
     )
 
-    def group(place_at, _):
-        members = range(GROUP)
-        which = [place_at * GROUP + k for k in members]
-        mine = [pl.ds(h, total, stride=chans) for h in which]
-        line = [lines[h] for h in which]
-        ends, outer, pairs = [], [], []
-        for k in members:
-            x_back, g = mirrored[mine[k], :], grads[mine[k], :]
-            stack = jnp.concatenate([x_back, g, x_back * lane, g * lane], axis=0).astype(BF16)
+    def group(at, _):
+        members = range(size)
+        which = [at * size + k for k in members]
+        here = pl.ds(at * size, size)
+        for k, (far, near) in enumerate(pairs):
+            pltpu.make_async_copy(far.at[here], near.at[here], sems.at[k, at]).wait()
+        ends, outer, both = [], [], []
+        for k in members:
+            g = grads[which[k]]
+            stack = jnp.concatenate([g, (g.astype(F32) * lane).astype(BF16)], axis=0)
             ends.append(dot(stack, table[which[k]], (1, 0)))
         for k in members:
-            g = grads[mine[k], :].astype(BF16)
-            outer.append(dot(mirrored[mine[k], :].astype(BF16), g, (0, 0)))
-        for k in members:
-            swapped = swap(ends[k])
-
-            def at(kind, c, of=ends[k]):
-                start = kind * total + each * c
-                return of[start : start + each]
-
-            def onward(state):
-                return state * line[k][1:2] + swap(state) * line[k][2:3]
-
-            one_a = one_b = two_a = two_b = jnp.zeros((each, LANES), F32)
-            state, slope = at(0, 0), at(2, 0)
-            for c in range(1, chunks):
-                both = state + slope
-                one_a += state * at(1, c)
-                one_b += state * at(1, c, swapped)
-                two_a += both * at(1, c) + state * at(3, c)
-                two_b += both * at(1, c, swapped) + state * at(3, c, swapped)
-                if c < chunks - 1:
-                    slope = onward(slope + float(rows) * state) + at(2, c)
-                    state = onward(state) + at(0, c)
+            outer.append(dot(mirrored[which[k]], grads[which[k]], (0, 0)))
+        for k in members:
+            one = pl.ds(which[k], 1)
+            later, later_slope = ends[k][each:total], ends[k][total + each :]
+            before = prefix[which[k]].astype(F32)
+            state, slope = before[0 : total - each], before[total - each :]
+            swapped, swapped_slope = swap(later), swap(later_slope)
             for into, value in (
-                (cross_one_a, one_a), (cross_one_b, one_b), (cross_two_a, two_a), (cross_two_b, two_b),
+                (cross_one_a, state * later),
+                (cross_one_b, state * swapped),
+                (cross_two_a, slope * later + state * later_slope),
+                (cross_two_b, slope * swapped + state * swapped_slope),
             ):
-                into[pl.ds(which[k], 1), :] = jnp.sum(value, axis=0, keepdims=True)
+                into[one, :] = jnp.sum(value, axis=0, keepdims=True)
             slid = pltpu.roll(outer[k][0:rows], LANES - rows + 1, 1, stride=1, stride_axis=0)
             corr = jnp.sum(jnp.where(behind, slid, 0.0), axis=0, keepdims=True)
+            corrs[one, :] = corr
             pair = jnp.concatenate([corr, corr * lane, jnp.zeros((6, LANES), F32)], axis=0)
-            pairs.append(pair.astype(BF16))
-        for k in members:
-            turned = dot(pairs[k], table[which[k]], (1, 0))
+            both.append(pair.astype(BF16))
+        for k in members:
+            turned = dot(both[k], table[which[k]], (1, 0))
             local_one[pl.ds(which[k], 1), :] = turned[0:1]
             local_two[pl.ds(which[k], 1), :] = turned[1:2]
         return 0
 
-    lax.fori_loop(0, chans // GROUP, group, 0)
+    lax.fori_loop(0, count, group, 0)
     low = lax.broadcasted_iota(jnp.int32, (1, LANES), 1) < LANES // 2
     for k, (a, b, near) in enumerate(
         ((cross_one_a, cross_one_b, local_one), (cross_two_a, cross_two_b, local_two))
@@ -451,8 +537,8 @@
     )
     row = lax.broadcasted_iota(jnp.int32, (16, 2 * LANES), 0)
     tail = jnp.zeros((16, 2 * LANES), F32)
-    for k, part in enumerate((skips, tallies[0], tallies[1])):
-        column = jnp.sum(part, axis=1, keepdims=True)
+    columns = [corrs[:, 0:1]] + [jnp.sum(tallies[k], axis=1, keepdims=True) for k in range(2)]
+    for k, column in enumerate(columns):
         line = jnp.sum(jnp.where(diagonal, column, 0.0), axis=0, keepdims=True)
         tail = jnp.where(row == k, line, tail)
     sums[chans:, :] = tail.astype(BF16)
@@ -479,26 +565,20 @@
         slots[lax.rem(mine + count - turn, count)] = part[...]
 
 
-def owner_kernel(chunks, *refs):
-    parts, (grad, bias, slots) = refs[:chunks], refs[chunks:]
-    own, segment = grad.shape[0], bias.shape[1]
-    ordered(parts, slots)
-    total = slots[0].astype(F32)
-    for k in range(1, chunks):
-        total += slots[k].astype(F32)
-    grad[...] = total[0:own]
+def owner_kernel(chunks, subs, *refs):
+    parts, inputs, outs = refs[:chunks], refs[chunks : chunks + 6], refs[chunks + 6 :]
+    one, two, decay, scale_in, real, imag = inputs
+    grad_weight, grad_bias, grad_decay, grad_freq, grad_real, grad_imag, *vectors, slots = outs
+    own, states = decay.shape
+    grad_weight[...] = one[0:own].astype(F32) + two[0:own].astype(F32)
+    line = one[own : own + 1].astype(F32) + two[own : own + 1].astype(F32)
+    segment = grad_bias.shape[1]
     shard = lax.axis_index("shard")
     row = jnp.zeros((1, segment), F32)
-    for s in range(total.shape[1] // segment):
-        row = jnp.where(shard == s, total[own : own + 1, s * segment : (s + 1) * segment], row)
-    bias[...] = row
-
-
-def state_kernel(chunks, subs, *refs):
-    parts, (decay, scale_in, real, imag), outs = refs[:chunks], refs[chunks : chunks + 4], refs[chunks + 4 :]
-    grad_decay, grad_freq, grad_real, grad_imag, *vectors, slots = outs
+    for s in range(line.shape[1] // segment):
+        row = jnp.where(shard == s, line[:, s * segment : (s + 1) * segment], row)
+    grad_bias[...] = row
     ordered(parts, slots)
-    own, states = decay.shape
     chans = own // subs
     sums = []
     for sub in range(subs):
@@ -537,7 +617,7 @@
         kernel,
         out_shape=[(pltpu.HBM if len(o) > 2 else jax.ShapeDtypeStruct)(*o[:2]) for o in outs],
         in_specs=ins,
-        out_specs=[VMEM] * len(outs),
+        out_specs=[HBM if len(o) > 2 else VMEM for o in outs],
         scratch_shapes=list(scratch),
         compiler_params=PARAMS,
         cost_estimate=pl.CostEstimate(
@@ -582,95 +662,118 @@
         pack = lax.dynamic_slice_in_dim(pack, lax.rem(mine, subs) * chans, chans, 0)
     pack = lax.ppermute(pack, BOTH, plan.fetch)
 
-    wire = ((blocks, seqs, chans, LANES), BF16)
-    (first,) = call(norm_kernel, COST[0], [wire], [SMEM, VMEM])(lengths, tokens)
+    def here(shape, dtype=BF16):
+        return pltpu.VMEM(shape, dtype)
+
+    def sems(*shape):
+        return pltpu.SemaphoreType.DMA(shape)
+
+    wire = ((blocks, seqs, chans, LANES), BF16, 1)
+    flow, like_tokens = wire[:2], (tokens.shape, BF16)
+    on_wire, on_rows = here(wire[0]), here(tokens.shape)
+    (first,) = call(
+        norm_kernel, COST[0], [flow], [SMEM, VMEM]
+    )(lengths, *in_hbm(tokens))
     first = exchange(first)
     piece, pack = lax.optimization_barrier((piece, pack))
     near = [piece] + [lax.ppermute(piece, "shard", route) for route in plan.climb]
-    table_type = ((chans, LANES, LANES), BF16, 1)
+    table_type, line_type = ((chans, LANES, LANES), BF16, 1), ((chans, 8, LANES), F32, 1)
+    tables = [here(*table_type[:2]), here(*line_type[:2])]
     table, lines, firsts = call(
         functools.partial(table_kernel, rows),
         COST[1],
-        [table_type, ((chans, 8, LANES), F32), ((2, chans, LANES), F32)],
+        [table_type, line_type, ((2, chans, LANES), F32)],
         [VMEM],
+        tables + [sems(chans // 8 + 1)],
     )(pack)
-    buffer = pltpu.VMEM((total * chans, LANES), F32)
-    line = pltpu.VMEM((chans, LANES), F32)
-    fetched = [pltpu.VMEM(*table_type[:2]), pltpu.SemaphoreType.DMA]
-    low = ((total * chans, LANES), BF16)
-    hidden, mixed = call(
+    far_tables = in_hbm(table, lines)
+    buffer, line = here((total * chans, LANES), F32), here((chans, LANES), F32)
+    low = ((total * chans, LANES), BF16, 1)
+    low_buffer = here(*low[:2])
+    tables.append(sems(chans // 8 + 1))
+    hidden, slope = call(
         functools.partial(forward_kernel, chunks, rows, plan.order),
         COST[2],
         [wire, low],
-        [VMEM, VMEM, HBM, VMEM],
-        [buffer, buffer, buffer] + fetched,
-    )(first, pack, table, lines)
+        [VMEM, VMEM, HBM, HBM],
+        [buffer, buffer, buffer, on_wire, low_buffer] + tables + [sems(2, blocks)],
+    )(first, pack, *far_tables)
+    prefix_type = ((chans, 2 * (total - 2 * seqs), LANES), BF16, 1)
+    by_channel = ((chans, total, LANES), BF16, 1)
+    mirrored, prefix = call(
+        functools.partial(prefix_kernel, chunks, rows, plan.order),
+        6,
+        [by_channel, prefix_type],
+        [VMEM, VMEM, HBM, HBM],
+        [buffer, here(*by_channel[:2]), here(*prefix_type[:2])] + tables + [sems(2)],
+    )(first, pack, *far_tables)
     hidden, near = lax.optimization_barrier((hidden, near))
     across = [lax.ppermute(p, "shard", plan.across) for p in near]
     hidden = exchange(hidden)
-    weight, bias = call(
-        functools.partial(weight_kernel, plan),
-        2,
-        [((width, 2 * width), BF16), ((1, 2 * width), F32)],
-        [VMEM] * (2 * plan.layers),
-    )(*near, *across)
+    block_out, back, outers = call(
+        functools.partial(glu_kernel, plan),
+        COST[3],
+        [like_tokens, flow, ((seqs * LANES, 2 * width), BF16)],
+        [SMEM] + [VMEM] * (3 + 2 * plan.layers),
+        [here((width, 2 * width))],
+    )(lengths, hidden, *in_hbm(tokens, cotangent), *near, *across)
+    back = exchange(back)
     half = ((plan.layers, own + 16, 2 * width), BF16)
-    block_out, back, outers = call(
-        glu_kernel,
-        COST[3],
-        [(tokens.shape, BF16), wire, ((seqs * LANES, 2 * width), BF16)],
-        [SMEM] + [VMEM] * 5,
-    )(lengths, hidden, tokens, cotangent, weight, bias)
-    back = exchange(back)
-    kept, sent = call(functools.partial(outer_kernel, plan), 2, [half, half], [VMEM] * 2)(hidden, outers)
+    kept, sent = call(functools.partial(outer_kernel, plan), 2, [half, half], [VMEM] * 2)(
+        hidden, outers
+    )
 
     came = lax.ppermute(sent, "shard", plan.across)
     slab = ((own + 16, 2 * width), BF16)
     shares = call(
         functools.partial(share_kernel, plan.layers), COST[6], [slab] * plan.layers, [VMEM] * 2
     )(kept, came)
-    back, shares = lax.optimization_barrier((back, shares))
     climbed = [lax.ppermute(v, "shard", route) for v, route in zip(shares[1:], plan.climb)]
     leaving, local_grads, tallies = call(
         functools.partial(backward_kernel, chunks, rows, plan.order),
         COST[4],
-        [wire, low, ((2, chans, LANES), F32)],
-        [VMEM, VMEM, VMEM, HBM, VMEM, VMEM],
-        [buffer, buffer, buffer] + fetched,
-    )(back, first, pack, table, lines, mixed)
+        [wire, by_channel, ((2, chans, LANES), F32)],
+        [VMEM, VMEM, VMEM, HBM, HBM, HBM],
+        [buffer, buffer, buffer, low_buffer, here(*by_channel[:2]), on_wire]
+        + tables
+        + [sems(3, blocks)],
+    )(back, first, pack, *far_tables, *in_hbm(slope))
     (owned,) = call(add_kernel, 1, [slab], [VMEM] * plan.layers)(shares[0], *climbed)
-    tallies, owned = lax.optimization_barrier((tallies, owned))
+    first_sum = owned
+    for route in plan.fold[:-1]:
+        (owned,) = call(add_kernel, 1, [slab], [VMEM] * 2)(owned, lax.ppermute(owned, "ctx", route))
+    folded = lax.ppermute(owned, "ctx", plan.fold[-1])
+    tallies, first_sum = lax.optimization_barrier((tallies, first_sum))
     state = (chans + 16, 2 * LANES)
     (sums,) = call(
-        functools.partial(moment_kernel, chunks, rows, plan.order),
+        functools.partial(moment_kernel, chunks, rows),
         COST[7],
         [(state, BF16)],
-        [VMEM] * 7,
-        [buffer, buffer] + [line] * 6,
-    )(first, pack, table, lines, firsts, local_grads, tallies)
+        [HBM] * 4 + [VMEM] * 2,
+        [line] * 7
+        + [tables[0], here(*by_channel[:2]), here(*prefix_type[:2]), here(*by_channel[:2])]
+        + [sems(4, chans // 8)],
+    )(far_tables[0], *in_hbm(mirrored, prefix, local_grads), firsts, tallies)
     leaving = exchange(leaving)
-    (tokens_grad,) = call(final_kernel, COST[5], [(tokens.shape, BF16)], [VMEM] * 3)(
-        leaving, tokens, cotangent
+    (tokens_grad,) = call(
+        final_kernel,
+        COST[5],
+        [like_tokens],
+        [VMEM] * 3,
+    )(
+        leaving, *in_hbm(tokens, cotangent)
     )
 
     parts = [lax.ppermute(sums, BOTH, route) for route in plan.give]
-    wholes = [owned] + [lax.ppermute(owned, "ctx", route) for route in plan.rotate]
-    tokens_grad, parts, wholes = lax.optimization_barrier((tokens_grad, parts, wholes))
-    grad_weight, grad_bias = call(
-        functools.partial(owner_kernel, chunks),
+    tokens_grad, parts = lax.optimization_barrier((tokens_grad, parts))
+    matrix, vector = ((own, states), F32), ((1, own), F32)
+    grad_weight, grad_bias, *grads = call(
+        functools.partial(owner_kernel, chunks, subs),
         2,
-        [(out_weight.shape, F32), ((1, segment), F32)],
-        [VMEM] * chunks,
-        [pltpu.VMEM((chunks,) + slab[0], BF16)],
-    )(*wholes)
-    matrix, vector = ((own, states), F32), ((1, own), F32)
-    grads = call(
-        functools.partial(state_kernel, chunks, subs),
-        2,
-        [matrix] * 4 + [vector] * 3,
-        [VMEM] * (chunks + 4),
-        [pltpu.VMEM((chunks,) + state, BF16)],
-    )(*parts, decay_rate, scale, coef_real, coef_imag)
+        [(out_weight.shape, F32), ((1, segment), F32)] + [matrix] * 4 + [vector] * 3,
+        [VMEM] * (chunks + 6),
+        [here((chunks,) + state)],
+    )(*parts, owned, folded, *in_hbm(decay_rate, scale, coef_real, coef_imag))
     return (
         block_out,
         tokens_grad,

time: 120 us -> 99.3 us (0.83)
  local copies, waits for them, and re-layouts: 17.4 us -> 0.01 us
  waiting for transfers between devices: 15.5 us -> 13.2 us
    unnamed x64 -> x4, local copies, waits for them, and re-layouts: 17.4 us -> 0.01 us
    ppermute x3 -> x1, starting transfers between devices: 8.54 us -> 2.08 us  [per_device(): lax.ppermute(owned, 'ctx', route)]
    ppermute x4, starting transfers between devices: 4.22 us -> 9.61 us  [per_device(): parts = [lax.ppermute(sums, BOTH, route) for route in plan.give]]
    ppermute x3 -> x1, waiting for transfers between devices: 4.04 us -> 0.01 us  [per_device(): lax.ppermute(owned, 'ctx', route)]
    ppermute x4, waiting for transfers between devices: 0.01 us -> 3.15 us  [per_device(): parts = [lax.ppermute(sums, BOTH, route) for route in plan.give]]
    pallas_call x1, Pallas kernels: 1.85 us -> 0.09 us  [per_device(): call(add_kernel, 1, [slab], [VMEM] * plan.layers)(shares[0], *climbed)]
    pallas_call x8, Pallas kernels: 23.3 us -> 24.7 us  [the longest x1 4.52 us: per_device(): call(functools.partial(glu_kernel, plan), COST[3], [like_tokens, flow, ((...]
    all_to_all x4, waiting for transfers between devices: 10.1 us -> 8.81 us  [exchange(): lax.all_to_all(buffer, BOTH, 0, 0, axis_index_groups=plan.groups, tiled=T...]
  transfers between devices with their start and end apart: 23 -> 22, of which waited for: 8 -> 8; matrix products, arithmetic and copies ran while one was open for 0% -> 0% of each run, Pallas kernels for 28% -> 33%
where the time goes in v3:
time: 99.3 us; the launch traced here: 98.6 us
  starting transfers between devices  43.7 us (44%)
  Pallas kernels  40.8 us (41%)
  waiting for transfers between devices  13.2 us (13%)
    all_to_all x4, starting transfers between devices, exchange(): lax.all_to_all(buffer, BOTH, 0, 0, axis_index_groups=plan.groups, tiled=T...  21 us
    ppermute x4, starting transfers between devices, per_device(): parts = [lax.ppermute(sums, BOTH, route) for route in plan.give]  9.61 us
    all_to_all x4, waiting for transfers between devices, exchange(): lax.all_to_all(buffer, BOTH, 0, 0, axis_index_groups=plan.groups, tiled=T...  8.81 us
    pallas_call x1, Pallas kernels, per_device(): call(functools.partial(backward_kernel, chunks, rows, plan.order), COST[4...  7.09 us
    pallas_call x1, Pallas kernels, per_device(): call(functools.partial(forward_kernel, chunks, rows, plan.order), COST[2]...  6.84 us
    ppermute x3, starting transfers between devices, per_device(): lax.ppermute(v, 'shard', route)  5.18 us
    pallas_call x1, Pallas kernels, per_device(): call(functools.partial(glu_kernel, plan), COST[3], [like_tokens, flow, ((...  4.52 us
    pallas_call x1, Pallas kernels, per_device(): call(functools.partial(moment_kernel, chunks, rows), COST[7], [(state, BF...  4.51 us
  transfers between devices with their start and end apart: 22, of which 8 were waited for; matrix products, arithmetic and copies ran while one was open for 0% of the time, Pallas kernels for 33%

profile of v3, /device:TPU:0, one launch (start us, length us, event | category | flops | bytes accessed | tf_op | source)
XLA Modules:
  0.0 98.6 jit_solution(8632574744456461111)
XLA Ops:
  0.6 0.0 copy-start
  0.7 1.2 %shard_map.204 = (f32[64,384]{1,0:T(8,128)S(1)}, f32[64,64]{1,0:T(8,128)S(1)}, bf16[80,1024]{1,0:T(8,128)(2,1)S(1)}) custom-call(f32[64,64]{1,0:T(8,128)} %refs_6_.1, f32[64,64]{1,0:T(8,128)} %freq.1, f32[64,64]{1,0:T(8,128)} %refs_8_.1, f32[64,64]{1,0:T(8,128)} %refs_9_.1, f32[1,64]{1,0:T(1,128)} %bitcast.8, f32[1,64]{1,0:T(1,128)} %bitcast.9, ...), custom_call_target="tpu_custom_call" | custom-call | flops 2000000000 | bytes 7000000 | tf_op jit(solution)/shard_map/pallas_call | solution.py:650
  1.8 0.0 copy-start.1
  1.8 0.7 collective-permute-start
  2.5 0.0 copy-done
  2.5 2.4 %shard_map.203 = bf16[8,4,64,128]{3,2,1,0:T(8,128)(2,1)} custom-call(s32[4]{0:T(128)S(1)} %copy-done, bf16[4,96,512]{2,1,0:T(8,128)(2,1)} %tokens.5), custom_call_target="tpu_custom_call" | custom-call | flops 2000000000 | bytes 7000000 | tf_op jit(solution)/shard_map/pallas_call | solution.py:674
  4.9 0.0 copy-done.1
  4.9 9.9 %all-to-all-start = ((bf16[8,4,64,128]{3,2,1,0:T(8,128)(2,1)}), bf16[8,4,64,128]{3,2,1,0:T(8,128)(2,1)S(1)}, u32[]{:S(2)}, u32[]{:S(2)}) async-start(bf16[8,4,64,128]{3,2,1,0:T(8,128)(2,1)} %shard_map.203), calls=%async_computation | async-start | bytes 1048576 | tf_op jit(solution)/shard_map/all_to_all | solution.py:647
  14.8 0.0 collective-permute-done.pack
  14.9 0.6 collective-permute-start.1
  15.5 2.2 %collective-permute-start.2 = (bf16[80,1024]{1,0:T(8,128)(2,1)S(1)}, bf16[80,1024]{1,0:T(8,128)(2,1)S(1)}, u32[]{:S(2)}, u32[]{:S(2)}) collective-permute-start(bf16[80,1024]{1,0:T(8,128)(2,1)S(1)} %get-tuple-element.63.refs_0_), channel_id=1, source_target_pairs={{0,16},{4,20},{8,24},{12,28},{16,0},{20,4},{24,8},{28,12},{1,17},{... | collective-permute-start | bytes 491528 | tf_op jit(solution)/shard_map/ppermute | solution.py:679
  17.7 1.1 %collective-permute-start.3 = (bf16[80,1024]{1,0:T(8,128)(2,1)S(1)}, bf16[80,1024]{1,0:T(8,128)(2,1)S(1)}, u32[]{:S(2)}, u32[]{:S(2)}) collective-permute-start(bf16[80,1024]{1,0:T(8,128)(2,1)S(1)} %get-tuple-element.63.refs_0_), channel_id=1, source_target_pairs={{0,24},{4,28},{8,0},{12,4},{16,8},{20,12},{24,16},{28,20},{1,25},{... | collective-permute-start | bytes 491528 | tf_op jit(solution)/shard_map/ppermute | solution.py:679
  18.7 4.4 %shard_map.205 = (bf16[64,128,128]{2,1,0:T(8,128)(2,1)}, f32[64,8,128]{2,1,0:T(8,128)}, f32[2,64,128]{2,1,0:T(8,128)S(1)}) custom-call(f32[64,384]{1,0:T(8,128)S(1)} %collective-permute-done.pack), custom_call_target="tpu_custom_call" | custom-call | flops 8000000000 | bytes 28000000 | tf_op jit(solution)/shard_map/pallas_call | solution.py:682
  23.2 1.4 %all-to-all-done.arrived.first = bf16[8,4,64,128]{3,2,1,0:T(8,128)(2,1)S(1)} async-done(((bf16[8,4,64,128]{3,2,1,0:T(8,128)(2,1)}), bf16[8,4,64,128]{3,2,1,0:T(8,128)(2,1)S(1)}, u32[]{:S(2)}, u32[]{:S(2)}) %all-to-all-start) | async-done | bytes 524320 | tf_op jit(solution)/shard_map/all_to_all | solution.py:647
  24.6 6.8 %shard_map.206 = (bf16[8,4,64,128]{3,2,1,0:T(8,128)(2,1)}, bf16[2048,128]{1,0:T(8,128)(2,1)}) custom-call(bf16[8,4,64,128]{3,2,1,0:T(8,128)(2,1)S(1)} %all-to-all-done.arrived.first, f32[64,384]{1,0:T(8,128)S(1)} %collective-permute-done.pack, bf16[64,128,128]{2,1,0:T(8,128)(2,1)} %get-tuple-element.58.far_table, f32[64,8,128]{2,1,0:T(8,128)} %get-tuple-element.59.far_lines), custom_call_target="tpu_custom_call" | custom-call | flops 10000000000 | bytes 35000000 | tf_op jit(solution)/shard_map/pallas_call | solution.py:694
  31.4 0.0 collective-permute-done.1.refs_1_
  31.4 0.0 collective-permute-done.2.refs_2_
  31.5 0.0 collective-permute-done.3.refs_3_
  31.5 3.5 %all-to-all-start.1 = ((bf16[8,4,64,128]{3,2,1,0:T(8,128)(2,1)}), bf16[8,4,64,128]{3,2,1,0:T(8,128)(2,1)S(1)}, u32[]{:S(2)}, u32[]{:S(2)}) async-start(bf16[8,4,64,128]{3,2,1,0:T(8,128)(2,1)} %get-tuple-element.62), calls=%async_computation.1 | async-start | bytes 1048576 | tf_op jit(solution)/shard_map/all_to_all | solution.py:647
  35.0 0.4 collective-permute-start.4
  35.4 0.2 collective-permute-start.5
  35.6 0.3 collective-permute-start.6
  35.9 0.2 collective-permute-start.7
  36.1 0.4 collective-permute-done.4.refs_4_
  36.4 0.3 collective-permute-done.5.refs_5_
  36.8 0.2 collective-permute-done.6.refs_6_
  37.0 0.3 collective-permute-done.7.refs_7_
  37.3 7.4 %all-to-all-done.1.arrived = bf16[8,4,64,128]{3,2,1,0:T(8,128)(2,1)S(1)} async-done(((bf16[8,4,64,128]{3,2,1,0:T(8,128)(2,1)}), bf16[8,4,64,128]{3,2,1,0:T(8,128)(2,1)S(1)}, u32[]{:S(2)}, u32[]{:S(2)}) %all-to-all-start.1) | async-done | bytes 524320 | tf_op jit(solution)/shard_map/all_to_all | solution.py:647
  44.7 4.5 %shard_map.207 = (bf16[4,96,512]{2,1,0:T(8,128)(2,1)}, bf16[8,4,64,128]{3,2,1,0:T(8,128)(2,1)}, bf16[512,1024]{1,0:T(8,128)(2,1)S(1)}) custom-call(s32[4]{0:T(128)S(1)} %copy-done, bf16[8,4,64,128]{3,2,1,0:T(8,128)(2,1)S(1)} %all-to-all-done.1.arrived, bf16[4,96,512]{2,1,0:T(8,128)(2,1)} %tokens.5, bf16[4,96,512]{2,1,0:T(8,128)(2,1)} %cotangent.3, ...), custom_call_target="tpu_custom_call" | custom-call | flops 6000000000 | bytes 21000000 | tf_op jit(solution)/shard_map/pallas_call | solution.py:713
  49.2 0.7 shard_map.211
  49.9 0.1 collective-permute-start.8
  50.0 3.5 %all-to-all-start.2 = ((bf16[8,4,64,128]{3,2,1,0:T(8,128)(2,1)}), bf16[8,4,64,128]{3,2,1,0:T(8,128)(2,1)S(1)}, u32[]{:S(2)}, u32[]{:S(2)}) async-start(bf16[8,4,64,128]{3,2,1,0:T(8,128)(2,1)} %get-tuple-element.68), calls=%async_computation.2 | async-start | bytes 1048576 | tf_op jit(solution)/shard_map/all_to_all | solution.py:647
  53.5 0.0 collective-permute-done.8.came
  53.5 0.2 shard_map.212
  53.7 1.8 %collective-permute-start.10 = (bf16[80,1024]{1,0:T(8,128)(2,1)S(1)}, bf16[80,1024]{1,0:T(8,128)(2,1)S(1)}, u32[]{:S(2)}, u32[]{:S(2)}) collective-permute-start(bf16[80,1024]{1,0:T(8,128)(2,1)S(1)} %get-tuple-element.81), channel_id=1, source_target_pairs={{0,16},{4,20},{8,24},{12,28},{16,0},{20,4},{24,8},{28,12},{1,17},{... | collective-permute-start | bytes 491528 | tf_op jit(solution)/shard_map/ppermute | solution.py:731
  55.5 3.4 %collective-permute-start.11 = (bf16[80,1024]{1,0:T(8,128)(2,1)S(1)}, bf16[80,1024]{1,0:T(8,128)(2,1)S(1)}, u32[]{:S(2)}, u32[]{:S(2)}) collective-permute-start(bf16[80,1024]{1,0:T(8,128)(2,1)S(1)} %get-tuple-element.82), channel_id=1, source_target_pairs={{0,24},{4,28},{8,0},{12,4},{16,8},{20,12},{24,16},{28,20},{1,25},{... | collective-permute-start | bytes 491528 | tf_op jit(solution)/shard_map/ppermute | solution.py:731
  58.9 0.0 collective-permute-start.9
  58.9 4.3 %shard_map.210 = (bf16[64,32,128]{2,1,0:T(8,128)(2,1)}, bf16[64,48,128]{2,1,0:T(8,128)(2,1)}) custom-call(bf16[8,4,64,128]{3,2,1,0:T(8,128)(2,1)S(1)} %all-to-all-done.arrived.first, f32[64,384]{1,0:T(8,128)S(1)} %collective-permute-done.pack, bf16[64,128,128]{2,1,0:T(8,128)(2,1)} %get-tuple-element.58.far_table, f32[64,8,128]{2,1,0:T(8,128)} %get-tuple-element.59.far_lines), custom_call_target="tpu_custom_call" | custom-call | flops 6000000000 | bytes 21000000 | tf_op jit(solution)/shard_map/pallas_call | solution.py:703
  63.2 0.0 all-to-all-done.2.arrived
  63.2 7.1 %shard_map.208 = (bf16[8,4,64,128]{3,2,1,0:T(8,128)(2,1)}, bf16[64,32,128]{2,1,0:T(8,128)(2,1)}, f32[2,64,128]{2,1,0:T(8,128)S(1)}) custom-call(bf16[8,4,64,128]{3,2,1,0:T(8,128)(2,1)S(1)} %all-to-all-done.2.arrived, bf16[8,4,64,128]{3,2,1,0:T(8,128)(2,1)S(1)} %all-to-all-done.arrived.first, f32[64,384]{1,0:T(8,128)S(1)} %collective-permute-done.pack, ...), custom_call_target="tpu_custom_call" | custom-call | flops 1000000000 | bytes 3500000 | tf_op jit(solution)/shard_map/pallas_call | solution.py:732
  70.3 4.1 %all-to-all-start.3 = ((bf16[8,4,64,128]{3,2,1,0:T(8,128)(2,1)}), bf16[8,4,64,128]{3,2,1,0:T(8,128)(2,1)S(1)}, u32[]{:S(2)}, u32[]{:S(2)}) async-start(bf16[8,4,64,128]{3,2,1,0:T(8,128)(2,1)} %get-tuple-element.70), calls=%async_computation.3 | async-start | bytes 1048576 | tf_op jit(solution)/shard_map/all_to_all | solution.py:647
  74.4 0.0 collective-permute-done.10.refs_2_
  74.4 0.0 collective-permute-done.11.refs_3_
  74.4 0.0 collective-permute-done.9.refs_1_
  74.4 0.1 shard_map.213.refs_0_
  74.5 2.1 %collective-permute-start.16 = (bf16[80,1024]{1,0:T(8,128)(2,1)S(1)}, bf16[80,1024]{1,0:T(8,128)(2,1)S(1)}, u32[]{:S(2)}, u32[]{:S(2)}) collective-permute-start(bf16[80,1024]{1,0:T(8,128)(2,1)S(1)} %shard_map.213.refs_0_), channel_id=1, source_target_pairs={{0,1},{1,0},{2,3},{3,2},{4,5},{5,4},{6,7},{7,6},{8,9},{9,8},{10,11... | collective-permute-start | bytes 491528 | tf_op jit(solution)/shard_map/ppermute | solution.py:744
  76.6 4.5 %shard_map.214 = bf16[80,256]{1,0:T(8,128)(2,1)S(1)} custom-call(bf16[64,128,128]{2,1,0:T(8,128)(2,1)} %get-tuple-element.58.far_table, bf16[64,32,128]{2,1,0:T(8,128)(2,1)} %get-tuple-element.71.far_mirrored, bf16[64,48,128]{2,1,0:T(8,128)(2,1)} %get-tuple-element.72.far_prefix, bf16[64,32,128]{2,1,0:T(8,128)(2,1)} %get-tuple-element.73.far_grads, ...), custom_call_target="tpu_custom_call" | custom-call | flops 8000000000 | bytes 28000000 | tf_op jit(solution)/shard_map/pallas_call | solution.py:748
  81.1 0.7 collective-permute-start.12
  81.8 4.8 %collective-permute-start.13 = (bf16[80,256]{1,0:T(8,128)(2,1)S(1)}, bf16[80,256]{1,0:T(8,128)(2,1)S(1)}, u32[]{:S(2)}, u32[]{:S(2)}) collective-permute-start(bf16[80,256]{1,0:T(8,128)(2,1)S(1)} %shard_map.214), channel_id=1, source_target_pairs={{0,1},{4,5},{1,9},{5,13},{2,17},{6,21},{3,25},{7,29},{8,2},{12,6},... | collective-permute-start | bytes 122888 | tf_op jit(solution)/shard_map/ppermute | solution.py:767
  86.6 3.3 %collective-permute-start.14 = (bf16[80,256]{1,0:T(8,128)(2,1)S(1)}, bf16[80,256]{1,0:T(8,128)(2,1)S(1)}, u32[]{:S(2)}, u32[]{:S(2)}) collective-permute-start(bf16[80,256]{1,0:T(8,128)(2,1)S(1)} %shard_map.214), channel_id=1, source_target_pairs={{0,2},{4,6},{1,10},{5,14},{2,18},{6,22},{3,26},{7,30},{8,3},{12,7}... | collective-permute-start | bytes 122888 | tf_op jit(solution)/shard_map/ppermute | solution.py:767
  89.9 0.8 collective-permute-start.15
  90.7 0.0 collective-permute-done.16.refs_1_
  90.8 0.1 collective-permute-start.17
  90.9 0.0 all-to-all-done.3.arrived
  90.9 2.9 %shard_map.209 = bf16[4,96,512]{2,1,0:T(8,128)(2,1)} custom-call(bf16[8,4,64,128]{3,2,1,0:T(8,128)(2,1)S(1)} %all-to-all-done.3.arrived, bf16[4,96,512]{2,1,0:T(8,128)(2,1)} %tokens.5, bf16[4,96,512]{2,1,0:T(8,128)(2,1)} %cotangent.3), custom_call_target="tpu_custom_call" | custom-call | flops 3000000000 | bytes 10500000 | tf_op jit(solution)/shard_map/pallas_call | solution.py:758
  93.8 0.0 collective-permute-done.12.refs_0_
  93.8 0.0 collective-permute-done.13.refs_1_
  93.8 0.9 collective-permute-done.14.refs_2_
  94.7 2.3 %collective-permute-done.15.refs_3_ = bf16[80,256]{1,0:T(8,128)(2,1)S(1)} collective-permute-done((bf16[80,256]{1,0:T(8,128)(2,1)S(1)}, bf16[80,256]{1,0:T(8,128)(2,1)S(1)}, u32[]{:S(2)}, u32[]{:S(2)}) %collective-permute-start.15) | collective-permute-done | bytes 40992 | tf_op jit(solution)/shard_map/ppermute | solution.py:767
  97.0 0.0 collective-permute-done.17.refs_5_
  97.0 1.6 %shard_map.216 = (f32[64,1024]{1,0:T(8,128)}, f32[1,128]{1,0:T(1,128)}, f32[64,64]{1,0:T(8,128)}, f32[64,64]{1,0:T(8,128)}, f32[64,64]{1,0:T(8,128)}, /*index=5*...) custom-call(bf16[80,256]{1,0:T(8,128)(2,1)S(1)} %collective-permute-done.12.refs_0_, ...), custom_call_target="tpu_custom_call" | custom-call | flops 2000000000 | bytes 7000000 | tf_op jit(solution)/shard_map/pallas_call | solution.py:770
  (1 shorter events, 0.0 us)
Async XLA Ops:
  0.6 1.9 %copy-start = (s32[4]{0:T(128)S(1)}, s32[4]{0:T(128)}, u32[]{:S(2)}) copy-start(s32[4]{0:T(128)} %lengths.3) | copy-start | bytes 52
  1.8 3.1 %copy-start.1 = (f32[64,64]{1,0:T(8,128)}, f32[64,64]{1,0:T(8,128)S(1)}, u32[]{:S(2)}) copy-start(f32[64,64]{1,0:T(8,128)S(1)} %get-tuple-element.89.refs_7_) | copy-start | bytes 49156
  1.8 13.0 %collective-permute-start = (f32[64,384]{1,0:T(8,128)S(1)}, f32[64,384]{1,0:T(8,128)S(1)}, u32[]{:S(2)}, u32[]{:S(2)}) collective-permute-start(f32[64,384]{1,0:T(8,128)S(1)} %get-tuple-element.56), channel_id=1, source_target_pairs={{0,0},{4,4},{8,1},{12,5},{16,2},{20,6},{24,3},{28,7},{1,8},{5,12},... | collective-permute-start | bytes 294920 | tf_op jit(solution)/shard_map/ppermute | solution.py:663
  4.9 19.7 %all-to-all-start = ((bf16[8,4,64,128]{3,2,1,0:T(8,128)(2,1)}), bf16[8,4,64,128]{3,2,1,0:T(8,128)(2,1)S(1)}, u32[]{:S(2)}, u32[]{:S(2)}) async-start(bf16[8,4,64,128]{3,2,1,0:T(8,128)(2,1)} %shard_map.203), calls=%async_computation | async-start | bytes 1048576 | tf_op jit(solution)/shard_map/all_to_all | solution.py:647
  14.9 16.6 %collective-permute-start.1 = (bf16[80,1024]{1,0:T(8,128)(2,1)S(1)}, bf16[80,1024]{1,0:T(8,128)(2,1)S(1)}, u32[]{:S(2)}, u32[]{:S(2)}) collective-permute-start(bf16[80,1024]{1,0:T(8,128)(2,1)S(1)} %get-tuple-element.63.refs_0_), channel_id=1, source_target_pairs={{0,8},{4,12},{8,16},{12,20},{16,24},{20,28},{24,0},{28,4},{1,9},{5... | collective-permute-start | bytes 491528 | tf_op jit(solution)/shard_map/ppermute | solution.py:679
  15.5 16.0 %collective-permute-start.2 = (bf16[80,1024]{1,0:T(8,128)(2,1)S(1)}, bf16[80,1024]{1,0:T(8,128)(2,1)S(1)}, u32[]{:S(2)}, u32[]{:S(2)}) collective-permute-start(bf16[80,1024]{1,0:T(8,128)(2,1)S(1)} %get-tuple-element.63.refs_0_), channel_id=1, source_target_pairs={{0,16},{4,20},{8,24},{12,28},{16,0},{20,4},{24,8},{28,12},{1,17},{... | collective-permute-start | bytes 491528 | tf_op jit(solution)/shard_map/ppermute | solution.py:679
  17.7 13.8 %collective-permute-start.3 = (bf16[80,1024]{1,0:T(8,128)(2,1)S(1)}, bf16[80,1024]{1,0:T(8,128)(2,1)S(1)}, u32[]{:S(2)}, u32[]{:S(2)}) collective-permute-start(bf16[80,1024]{1,0:T(8,128)(2,1)S(1)} %get-tuple-element.63.refs_0_), channel_id=1, source_target_pairs={{0,24},{4,28},{8,0},{12,4},{16,8},{20,12},{24,16},{28,20},{1,25},{... | collective-permute-start | bytes 491528 | tf_op jit(solution)/shard_map/ppermute | solution.py:679
  31.5 13.2 %all-to-all-start.1 = ((bf16[8,4,64,128]{3,2,1,0:T(8,128)(2,1)}), bf16[8,4,64,128]{3,2,1,0:T(8,128)(2,1)S(1)}, u32[]{:S(2)}, u32[]{:S(2)}) async-start(bf16[8,4,64,128]{3,2,1,0:T(8,128)(2,1)} %get-tuple-element.62), calls=%async_computation.1 | async-start | bytes 1048576 | tf_op jit(solution)/shard_map/all_to_all | solution.py:647
  35.0 1.5 %collective-permute-start.4 = (bf16[80,1024]{1,0:T(8,128)(2,1)S(1)}, bf16[80,1024]{1,0:T(8,128)(2,1)S(1)}, u32[]{:S(2)}, u32[]{:S(2)}) collective-permute-start(bf16[80,1024]{1,0:T(8,128)(2,1)S(1)} %get-tuple-element.63.refs_0_), channel_id=1, source_target_pairs={{0,4},{4,0},{8,12},{12,8},{16,20},{20,16},{24,28},{28,24},{1,5},{5... | collective-permute-start | bytes 491528 | tf_op jit(solution)/shard_map/ppermute | solution.py:711
  35.4 1.4 %collective-permute-start.5 = (bf16[80,1024]{1,0:T(8,128)(2,1)S(1)}, bf16[80,1024]{1,0:T(8,128)(2,1)S(1)}, u32[]{:S(2)}, u32[]{:S(2)}) collective-permute-start(bf16[80,1024]{1,0:T(8,128)(2,1)S(1)} %collective-permute-done.1.refs_1_), channel_id=1, source_target_pairs={{0,4},{4,0},{8,12},{12,8},{16,20},{20,16},{24,28},{28,24},{1,5},{5... | collective-permute-start | bytes 491528 | tf_op jit(solution)/shard_map/ppermute | solution.py:711
  35.6 1.5 %collective-permute-start.6 = (bf16[80,1024]{1,0:T(8,128)(2,1)S(1)}, bf16[80,1024]{1,0:T(8,128)(2,1)S(1)}, u32[]{:S(2)}, u32[]{:S(2)}) collective-permute-start(bf16[80,1024]{1,0:T(8,128)(2,1)S(1)} %collective-permute-done.2.refs_2_), channel_id=1, source_target_pairs={{0,4},{4,0},{8,12},{12,8},{16,20},{20,16},{24,28},{28,24},{1,5},{5... | collective-permute-start | bytes 491528 | tf_op jit(solution)/shard_map/ppermute | solution.py:711
  35.9 1.4 %collective-permute-start.7 = (bf16[80,1024]{1,0:T(8,128)(2,1)S(1)}, bf16[80,1024]{1,0:T(8,128)(2,1)S(1)}, u32[]{:S(2)}, u32[]{:S(2)}) collective-permute-start(bf16[80,1024]{1,0:T(8,128)(2,1)S(1)} %collective-permute-done.3.refs_3_), channel_id=1, source_target_pairs={{0,4},{4,0},{8,12},{12,8},{16,20},{20,16},{24,28},{28,24},{1,5},{5... | collective-permute-start | bytes 491528 | tf_op jit(solution)/shard_map/ppermute | solution.py:711
  49.9 3.6 %collective-permute-start.8 = (bf16[4,80,1024]{2,1,0:T(8,128)(2,1)S(1)}, bf16[4,80,1024]{2,1,0:T(8,128)(2,1)S(1)}, u32[]{:S(2)}, u32[]{:S(2)}) collective-permute-start(bf16[4,80,1024]{2,1,0:T(8,128)(2,1)S(1)} %get-tuple-element.78), channel_id=1, source_target_pairs={{0,4},{4,0},{8,12},{12,8},{16,20},{20,16},{24,28},{28,24},{1,5},{5... | collective-permute-start | bytes 1966088 | tf_op jit(solution)/shard_map/ppermute | solution.py:726
  50.0 13.2 %all-to-all-start.2 = ((bf16[8,4,64,128]{3,2,1,0:T(8,128)(2,1)}), bf16[8,4,64,128]{3,2,1,0:T(8,128)(2,1)S(1)}, u32[]{:S(2)}, u32[]{:S(2)}) async-start(bf16[8,4,64,128]{3,2,1,0:T(8,128)(2,1)} %get-tuple-element.68), calls=%async_computation.2 | async-start | bytes 1048576 | tf_op jit(solution)/shard_map/all_to_all | solution.py:647
  53.7 20.7 %collective-permute-start.10 = (bf16[80,1024]{1,0:T(8,128)(2,1)S(1)}, bf16[80,1024]{1,0:T(8,128)(2,1)S(1)}, u32[]{:S(2)}, u32[]{:S(2)}) collective-permute-start(bf16[80,1024]{1,0:T(8,128)(2,1)S(1)} %get-tuple-element.81), channel_id=1, source_target_pairs={{0,16},{4,20},{8,24},{12,28},{16,0},{20,4},{24,8},{28,12},{1,17},{... | collective-permute-start | bytes 491528 | tf_op jit(solution)/shard_map/ppermute | solution.py:731
  55.5 18.9 %collective-permute-start.11 = (bf16[80,1024]{1,0:T(8,128)(2,1)S(1)}, bf16[80,1024]{1,0:T(8,128)(2,1)S(1)}, u32[]{:S(2)}, u32[]{:S(2)}) collective-permute-start(bf16[80,1024]{1,0:T(8,128)(2,1)S(1)} %get-tuple-element.82), channel_id=1, source_target_pairs={{0,24},{4,28},{8,0},{12,4},{16,8},{20,12},{24,16},{28,20},{1,25},{... | collective-permute-start | bytes 491528 | tf_op jit(solution)/shard_map/ppermute | solution.py:731
  58.9 15.5 %collective-permute-start.9 = (bf16[80,1024]{1,0:T(8,128)(2,1)S(1)}, bf16[80,1024]{1,0:T(8,128)(2,1)S(1)}, u32[]{:S(2)}, u32[]{:S(2)}) collective-permute-start(bf16[80,1024]{1,0:T(8,128)(2,1)S(1)} %get-tuple-element.80), channel_id=1, source_target_pairs={{0,8},{4,12},{8,16},{12,20},{16,24},{20,28},{24,0},{28,4},{1,9},{5... | collective-permute-start | bytes 491528 | tf_op jit(solution)/shard_map/ppermute | solution.py:731
  70.3 20.6 %all-to-all-start.3 = ((bf16[8,4,64,128]{3,2,1,0:T(8,128)(2,1)}), bf16[8,4,64,128]{3,2,1,0:T(8,128)(2,1)S(1)}, u32[]{:S(2)}, u32[]{:S(2)}) async-start(bf16[8,4,64,128]{3,2,1,0:T(8,128)(2,1)} %get-tuple-element.70), calls=%async_computation.3 | async-start | bytes 1048576 | tf_op jit(solution)/shard_map/all_to_all | solution.py:647
  74.5 16.2 %collective-permute-start.16 = (bf16[80,1024]{1,0:T(8,128)(2,1)S(1)}, bf16[80,1024]{1,0:T(8,128)(2,1)S(1)}, u32[]{:S(2)}, u32[]{:S(2)}) collective-permute-start(bf16[80,1024]{1,0:T(8,128)(2,1)S(1)} %shard_map.213.refs_0_), channel_id=1, source_target_pairs={{0,1},{1,0},{2,3},{3,2},{4,5},{5,4},{6,7},{7,6},{8,9},{9,8},{10,11... | collective-permute-start | bytes 491528 | tf_op jit(solution)/shard_map/ppermute | solution.py:744
  81.1 12.7 %collective-permute-start.12 = (bf16[80,256]{1,0:T(8,128)(2,1)S(1)}, bf16[80,256]{1,0:T(8,128)(2,1)S(1)}, u32[]{:S(2)}, u32[]{:S(2)}) collective-permute-start(bf16[80,256]{1,0:T(8,128)(2,1)S(1)} %shard_map.214), channel_id=1, source_target_pairs={{0,0},{4,4},{1,8},{5,12},{2,16},{6,20},{3,24},{7,28},{8,1},{12,5},... | collective-permute-start | bytes 122888 | tf_op jit(solution)/shard_map/ppermute | solution.py:767
  81.8 12.0 %collective-permute-start.13 = (bf16[80,256]{1,0:T(8,128)(2,1)S(1)}, bf16[80,256]{1,0:T(8,128)(2,1)S(1)}, u32[]{:S(2)}, u32[]{:S(2)}) collective-permute-start(bf16[80,256]{1,0:T(8,128)(2,1)S(1)} %shard_map.214), channel_id=1, source_target_pairs={{0,1},{4,5},{1,9},{5,13},{2,17},{6,21},{3,25},{7,29},{8,2},{12,6},... | collective-permute-start | bytes 122888 | tf_op jit(solution)/shard_map/ppermute | solution.py:767
  86.6 8.1 %collective-permute-start.14 = (bf16[80,256]{1,0:T(8,128)(2,1)S(1)}, bf16[80,256]{1,0:T(8,128)(2,1)S(1)}, u32[]{:S(2)}, u32[]{:S(2)}) collective-permute-start(bf16[80,256]{1,0:T(8,128)(2,1)S(1)} %shard_map.214), channel_id=1, source_target_pairs={{0,2},{4,6},{1,10},{5,14},{2,18},{6,22},{3,26},{7,30},{8,3},{12,7}... | collective-permute-start | bytes 122888 | tf_op jit(solution)/shard_map/ppermute | solution.py:767
  89.9 7.1 %collective-permute-start.15 = (bf16[80,256]{1,0:T(8,128)(2,1)S(1)}, bf16[80,256]{1,0:T(8,128)(2,1)S(1)}, u32[]{:S(2)}, u32[]{:S(2)}) collective-permute-start(bf16[80,256]{1,0:T(8,128)(2,1)S(1)} %shard_map.214), channel_id=1, source_target_pairs={{0,3},{4,7},{1,11},{5,15},{2,19},{6,23},{3,27},{7,31},{8,0},{12,4}... | collective-permute-start | bytes 122888 | tf_op jit(solution)/shard_map/ppermute | solution.py:767
  90.8 6.2 %collective-permute-start.17 = (bf16[80,1024]{1,0:T(8,128)(2,1)S(1)}, bf16[80,1024]{1,0:T(8,128)(2,1)S(1)}, u32[]{:S(2)}, u32[]{:S(2)}) collective-permute-start(bf16[80,1024]{1,0:T(8,128)(2,1)S(1)} %shard_map.215.refs_4_), channel_id=1, source_target_pairs={{0,2},{1,3},{2,0},{3,1},{4,6},{5,7},{6,4},{7,5},{8,10},{9,11},{10,... | collective-permute-start | bytes 491528 | tf_op jit(solution)/shard_map/ppermute | solution.py:745

commit v4 on v3

--- a/solution.py
+++ b/solution.py
@@ -10,7 +10,7 @@
 
 EPSILON = 1e-05
 LANES = 128
-GROUPS = (32, 16, 16, 16)
+GROUPS = (32, 32, 16, 16)
 COST = (2, 8, 10, 6, 1, 3, 2, 8)
 BOTH = ("shard", "ctx")
 F32 = jnp.float32
@@ -45,10 +45,11 @@
             return (2 * (c // subs) + core) * chunks + place
 
         self.fetch = [(owner(*m, 0), here(*m)) for m in members]
-        self.give = [[(here(*m), owner(*m, turn)) for m in members] for turn in range(chunks)]
-        self.fold = [
-            [(a, a ^ (1 << bit)) for a in range(chunks)] for bit in range((chunks - 1).bit_length())
+        self.give = [[(here(*m), owner(*m, turn)) for m in members] for turn in range(0, chunks, 2)]
+        self.rotate = [
+            [(a, (a + turn) % chunks) for a in range(chunks)] for turn in range(1, chunks)
         ]
+        self.beside = [(a, a ^ 1) for a in range(chunks)]
         self.layers = layers
         self.climb = [
             [(s, (s + 2 * turn) % shards) for s in range(shards)] for turn in range(1, layers)
@@ -106,16 +107,44 @@
     return jnp.clip(lengths[n] - lax.axis_index("ctx") * rows, 0, rows)
 
 
-def norm_kernel(lengths, tokens, out):
+def norm_kernel(tokens, out):
     seqs, rows, width = tokens.shape
-    blocks, _, chans, _ = out.shape
-    pad = LANES - rows
-    last = lax.broadcasted_iota(jnp.int32, (pad, width), 0) == pad - 1
-    for n in range(seqs):
-        xhat, _ = row_stats(tokens[n].astype(F32))
-        tail = jnp.where(last, valid_count(lengths, n, rows).astype(F32), 0.0)
-        full = jnp.concatenate([xhat, tail], axis=0)
-        out[:, n] = full.T.astype(BF16).reshape(blocks, chans, LANES)
+    xhat, _ = row_stats(tokens[...].reshape(seqs * rows, width).astype(F32))
+    out[...] = xhat.T.astype(BF16).reshape(out.shape)
+
+
+def split_lanes(wide, rows, count):
+    lane = lax.broadcasted_iota(jnp.int32, (1, LANES), 1)
+    pieces = []
+    for n in range(count):
+        at, off = divmod(n * rows, LANES)
+        turn = (LANES - off) % LANES
+        piece = wide[:, at * LANES : (at + 1) * LANES]
+        if turn:
+            piece = pltpu.roll(piece, turn, 1)
+        if off + rows > LANES:
+            after = pltpu.roll(wide[:, (at + 1) * LANES : (at + 2) * LANES], turn, 1)
+            piece = jnp.where(lane < turn, piece, after)
+        pieces.append(piece)
+    return pieces
+
+
+def join_lanes(pieces, rows):
+    lane = lax.broadcasted_iota(jnp.int32, (1, LANES), 1)
+    columns = [None] * (len(pieces) * rows // LANES)
+    for n, piece in enumerate(pieces):
+        at, off = divmod(n * rows, LANES)
+        turned = pltpu.roll(piece, off, 1) if off else piece
+        columns[at] = turned if off == 0 else jnp.where(lane < off, columns[at], turned)
+        if off + rows > LANES:
+            columns[at + 1] = turned
+    return jnp.concatenate(columns, axis=1)
+
+
+def count_of(lengths, partner, order, block, n, rows):
+    core, c = order[block]
+    own = lax.rem(lax.axis_index("shard"), 2) == core
+    return jnp.clip(jnp.where(own, lengths[n], partner[n]) - c * rows, 0, rows)
 
 
 def swap(values):
@@ -182,6 +211,17 @@
     copying(lines, far_lines, sems.at[count]).wait()
 
 
+def paired(lefts, rights, over):
+    outs = []
+    for k in range(0, len(lefts), 2):
+        rows = lefts[k].shape[0]
+        left = jnp.concatenate(lefts[k : k + 2], axis=0)
+        right = jnp.concatenate(rights[k : k + 2], axis=1 - over[1])
+        both = dot(left, right, over)
+        outs += [both[0:rows, 0:LANES], both[rows:, LANES:]]
+    return outs
+
+
 def upper_half(rows):
     square = (rows, LANES)
     return lax.broadcasted_iota(jnp.int32, square, 1) >= lax.broadcasted_iota(jnp.int32, square, 0)
@@ -230,23 +270,24 @@
 
 
 def forward_kernel(
-    chunks, rows, order, arrived, pack, far_table, far_lines, far_hidden, far_kept,
+    chunks, rows, order, lengths, partner, arrived, pack, far_table, far_lines, far_hidden, far_kept,
     inputs, mirrored, mixed, hidden, kept, table, lines, sems, out_sems,
 ):
     size = min(GROUPS[0], far_table.shape[0])
     fetch_tables(size, far_table, table, far_lines, lines, sems)
-    blocks, seqs, chans, _ = arrived.shape
+    blocks, chans, wide = arrived.shape
+    seqs = wide // rows
     total = blocks * seqs
     each = 2 * seqs
-    lane = lax.broadcasted_iota(jnp.int32, (1, LANES), 1).astype(F32)
+    lane = lax.broadcasted_iota(jnp.int32, (1, LANES), 1)
     gain, shift = pack[:, 257:258], pack[:, 258:259]
     mirror = mirror_matrix(rows)
     upper = upper_half(rows)
     for b in range(blocks):
-        for n in range(seqs):
+        for n, xhat in enumerate(split_lanes(arrived[b].astype(F32), rows, seqs)):
             here = pl.ds(place(order, seqs, b, n) * chans, chans)
-            xhat = arrived[b, n].astype(F32)
-            x = jnp.where(lane < xhat[0:1, LANES - 1 :], xhat * gain + shift, 0.0).astype(BF16)
+            inside = lane < count_of(lengths, partner, order, b, n, rows)
+            x = jnp.where(inside, xhat * gain + shift, 0.0).astype(BF16)
             inputs[here, :] = x.astype(F32)
             mirrored[here, :] = dot(x, mirror, (1, 0))
 
@@ -255,10 +296,13 @@
         await_table(size, far_table, table, sems, at)
         mine = [pl.ds(at * size + k, total, stride=chans) for k in members]
         line = [lines[at * size + k] for k in members]
-        ends = [dot(mirrored[mine[k], :].astype(BF16), table[at * size + k], (1, 0)) for k in members]
-        local = [
-            dot(inputs[mine[k], :].astype(BF16), toeplitz(upper, line[k][0:1]), (1, 0)) for k in members
-        ]
+        powers = [table[at * size + k] for k in members]
+        ends = paired([mirrored[mine[k], :].astype(BF16) for k in members], powers, (1, 0))
+        local = paired(
+            [inputs[mine[k], :].astype(BF16) for k in members],
+            [toeplitz(upper, line[k][0:1]) for k in members],
+            (1, 0),
+        )
         for k in members:
             state = ends[k][0:each]
             carried = [jnp.zeros((each, LANES), F32)]
@@ -268,8 +312,9 @@
                     state = state * line[k][1:2] + swap(state) * line[k][2:3]
                     state += ends[k][each * c : each * (c + 1)]
             ends[k] = jnp.concatenate(carried, axis=0).astype(BF16)
-        for k in members:
-            mixed[mine[k], :] = local[k] + dot(ends[k], table[at * size + k], (1, 1))
+        far = paired(ends, [table[at * size + k] for k in members], (1, 1))
+        for k in members:
+            mixed[mine[k], :] = local[k] + far[k]
         return 0
 
     await_lines(size, far_lines, lines, sems)
@@ -277,12 +322,14 @@
     stored = []
     skip = pack[:, 256:257]
     for b in range(blocks):
+        values = []
         for n in range(seqs):
             here = pl.ds(place(order, seqs, b, n) * chans, chans)
             mix = mixed[here, :] + skip * inputs[here, :]
             value, slope = gelu_and_slope(mix)
-            kept[here, :] = slope.astype(BF16)
-            hidden[b, n] = value.astype(BF16)
+            kept[here, :] = jnp.where(lane < rows, slope, 0.0).astype(BF16)
+            values.append(value)
+        hidden[b] = join_lanes(values, rows).astype(BF16)
         here = pl.ds(place(order, seqs, b, 0) * chans, seqs * chans)
         stored.append(copying(hidden.at[b], far_hidden.at[b], out_sems.at[0, b]))
         stored.append(copying(kept.at[here], far_kept.at[here], out_sems.at[1, b]))
@@ -293,7 +340,6 @@
     layers = plan.layers
     pieces, (block_out, leaving, outers, w) = refs[: 2 * layers], refs[2 * layers :]
     seqs, rows, width = tokens.shape
-    blocks, _, chans, _ = arrived.shape
     own = width // plan.shards
     shard = lax.axis_index("shard")
     layer, core = shard // 2, lax.rem(shard, 2)
@@ -305,56 +351,49 @@
             w[pl.ds(pl.multiple_of(home * own, own), own), :] = piece[0:own]
             bias += piece[own : own + 1].astype(F32)
     position = lax.broadcasted_iota(jnp.int32, (rows, width), 0)
+    hidden = arrived[...].reshape(width, seqs * rows).astype(F32).T.astype(BF16)
     for n in range(seqs):
-        hidden = arrived[:, n].reshape(width, LANES).astype(F32).T.astype(BF16)
-        proj = dot(hidden, w[...], (1, 0)) + bias
-        r, q = proj[0:rows, :width], proj[0:rows, width:]
+        here = slice(n * rows, (n + 1) * rows)
+        proj = dot(hidden[here], w[...], (1, 0)) + bias
+        r, q = proj[:, :width], proj[:, width:]
         valid = jnp.where(position < valid_count(lengths, n, rows), 1.0, 0.0)
         open_ = jax.nn.sigmoid(q)
         e = valid * cotangent[n].astype(F32)
         first = e * open_
-        both = jnp.concatenate([first, first * r * (1.0 - open_)], axis=1).astype(BF16)
-        both = jnp.concatenate([both, jnp.zeros((LANES - rows, 2 * width), BF16)], axis=0)
-        back = dot(both, w[...], (1, 1))
-        leaving[:, n] = back.T.astype(BF16).reshape(blocks, chans, LANES)
-        outers[pl.ds(n * LANES, LANES), :] = both
+        outers[here, :] = jnp.concatenate([first, first * r * (1.0 - open_)], axis=1).astype(BF16)
         block_out[n] = (tokens[n].astype(F32) + valid * (r * open_)).astype(BF16)
+    back = dot(outers[...], w[...], (1, 1))
+    leaving[...] = back.T.astype(BF16).reshape(leaving.shape)
 
 
 def outer_kernel(plan, arrived, outers, kept, sent):
-    blocks, seqs, chans, _ = arrived.shape
+    chans = arrived.shape[1]
     layers, subs = plan.layers, plan.subs
-    own = chans * subs
-    wide = outers.shape[1]
+    own, wide = chans * subs, outers.shape[1]
     core = lax.rem(lax.axis_index("shard"), 2)
     outer = outers[...]
     bias = jnp.sum(outer.astype(F32), axis=0, keepdims=True)
     tail = jnp.broadcast_to(bias, (kept.shape[1] - own, wide)).astype(BF16)
     for side, out in enumerate((sent, kept)):
         which = lax.rem(core + 1 - side, 2)
-        left = jnp.concatenate(
-            [
-                jnp.concatenate([arrived[(2 * z + which) * subs + sub, n] for n in range(seqs)], axis=1)
-                for z in range(layers)
-                for sub in range(subs)
-            ],
-            axis=0,
-        )
+        members = [(2 * z + which) * subs + sub for z in range(layers) for sub in range(subs)]
+        left = jnp.concatenate([arrived[member] for member in members], axis=0)
         out[:, 0:own] = dot(left, outer, (1, 0)).astype(BF16).reshape(layers, own, wide)
         for z in range(layers):
             out[z, own:] = tail
 
 
 def backward_kernel(
-    chunks, rows, order, arrived, first, pack, far_table, far_lines, far_slope,
+    chunks, rows, order, lengths, partner, arrived, first, pack, far_table, far_lines, far_slope,
     far_leaving, far_kept, tallies,
     grads, local, cross, slope, kept, leaving, table, lines, sems, more_sems,
 ):
     size = min(GROUPS[1], far_table.shape[0])
-    blocks, seqs, chans, _ = arrived.shape
+    blocks, chans, wide = arrived.shape
+    seqs = wide // rows
     total = blocks * seqs
     each = 2 * seqs
-    lane = lax.broadcasted_iota(jnp.int32, (1, LANES), 1).astype(F32)
+    lane = lax.broadcasted_iota(jnp.int32, (1, LANES), 1)
     skip, gain = pack[:, 256:257], pack[:, 257:258]
     mirror = mirror_matrix(rows)
     upper = upper_half(rows)
@@ -366,9 +405,9 @@
     stored = []
     for b in range(blocks):
         fetched[b].wait()
-        for n in range(seqs):
+        for n, back in enumerate(split_lanes(arrived[b].astype(F32), rows, seqs)):
             here = pl.ds(place(order, seqs, b, n) * chans, chans)
-            g = (arrived[b, n].astype(F32) * slope[here, :].astype(F32)).astype(BF16)
+            g = (back * slope[here, :].astype(F32)).astype(BF16)
             grads[here, :] = g.astype(F32)
 
     def group(at, _):
@@ -377,11 +416,13 @@
         which = [at * size + k for k in members]
         mine = [pl.ds(h, total, stride=chans) for h in which]
         line = [lines[h] for h in which]
-        ends = [dot(grads[mine[k], :].astype(BF16), table[which[k]], (1, 0)) for k in members]
-        for k in members:
-            g = grads[mine[k], :].astype(BF16)
-            kept[which[k]] = g
-            local[mine[k], :] = dot(g, toeplitz(upper, line[k][0:1]), (1, 1))
+        powers = [table[h] for h in which]
+        low = [grads[mine[k], :].astype(BF16) for k in members]
+        ends = paired(low, powers, (1, 0))
+        near = paired(low, [toeplitz(upper, line[k][0:1]) for k in members], (1, 1))
+        for k in members:
+            kept[which[k]] = low[k]
+            local[mine[k], :] = near[k]
         for k in members:
             parts = [jnp.zeros((each, LANES), F32)]
             state = ends[k][each * (chunks - 1) :]
@@ -391,8 +432,9 @@
                     state = state * line[k][1:2] + swap(state) * line[k][2:3]
                     state += ends[k][each * c : each * (c + 1)]
             ends[k] = jnp.concatenate(parts[::-1], axis=0).astype(BF16)
-        for k in members:
-            cross[mine[k], :] = dot(ends[k], table[which[k]], (1, 1))
+        far = paired(ends, powers, (1, 1))
+        for k in members:
+            cross[mine[k], :] = far[k]
         return 0
 
     await_lines(size, far_lines, lines, sems)
@@ -400,15 +442,16 @@
     stored.append(copying(kept, far_kept, more_sems.at[1, 0]))
     gains = shifts = jnp.zeros((chans, LANES), F32)
     for b in range(blocks):
-        for n in range(seqs):
+        inner = []
+        for n, xhat in enumerate(split_lanes(first[b].astype(F32), rows, seqs)):
             here = pl.ds(place(order, seqs, b, n) * chans, chans)
             grad = local[here, :] + skip * grads[here, :]
             grad += dot(cross[here, :].astype(BF16), mirror, (1, 0))
-            xhat = first[b, n].astype(F32)
-            m = jnp.where(lane < xhat[0:1, LANES - 1 :], grad, 0.0)
+            m = jnp.where(lane < count_of(lengths, partner, order, b, n, rows), grad, 0.0)
             gains += m * xhat
             shifts += m
-            leaving[b, n] = (gain * m).astype(BF16)
+            inner.append(gain * m)
+        leaving[b] = join_lanes(inner, rows).astype(BF16)
         stored.append(copying(leaving.at[b], far_leaving.at[b], more_sems.at[2, b]))
     tallies[0] = gains
     tallies[1] = shifts
@@ -416,22 +459,23 @@
 
 
 def prefix_kernel(
-    chunks, rows, order, first, pack, far_table, far_lines, far_mirrored, far_prefix,
+    chunks, rows, order, lengths, partner, first, pack, far_table, far_lines, far_mirrored, far_prefix,
     mirrored, kept, prefix, table, lines, sems, out_sems,
 ):
     size = min(GROUPS[2], far_table.shape[0])
     fetch_tables(size, far_table, table, far_lines, lines, sems)
-    blocks, seqs, chans, _ = first.shape
+    blocks, chans, wide = first.shape
+    seqs = wide // rows
     total = blocks * seqs
     each = 2 * seqs
     lane = lax.broadcasted_iota(jnp.int32, (1, LANES), 1).astype(F32)
     gain, shift = pack[:, 257:258], pack[:, 258:259]
     mirror = mirror_matrix(rows)
     for b in range(blocks):
-        for n in range(seqs):
+        for n, xhat in enumerate(split_lanes(first[b].astype(F32), rows, seqs)):
             here = pl.ds(place(order, seqs, b, n) * chans, chans)
-            xhat = first[b, n].astype(F32)
-            x = jnp.where(lane < xhat[0:1, LANES - 1 :], xhat * gain + shift, 0.0).astype(BF16)
+            inside = lane < count_of(lengths, partner, order, b, n, rows).astype(F32)
+            x = jnp.where(inside, xhat * gain + shift, 0.0).astype(BF16)
             mirrored[here, :] = dot(x, mirror, (1, 0))
 
     def group(at, _):
@@ -494,10 +538,11 @@
         for k, (far, near) in enumerate(pairs):
             pltpu.make_async_copy(far.at[here], near.at[here], sems.at[k, at]).wait()
         ends, outer, both = [], [], []
+        powers = [table[h] for h in which]
         for k in members:
             g = grads[which[k]]
-            stack = jnp.concatenate([g, (g.astype(F32) * lane).astype(BF16)], axis=0)
-            ends.append(dot(stack, table[which[k]], (1, 0)))
+            ends.append(jnp.concatenate([g, (g.astype(F32) * lane).astype(BF16)], axis=0))
+        ends = paired(ends, powers, (1, 0))
         for k in members:
             outer.append(dot(mirrored[which[k]], grads[which[k]], (0, 0)))
         for k in members:
@@ -516,10 +561,9 @@
             slid = pltpu.roll(outer[k][0:rows], LANES - rows + 1, 1, stride=1, stride_axis=0)
             corr = jnp.sum(jnp.where(behind, slid, 0.0), axis=0, keepdims=True)
             corrs[one, :] = corr
-            pair = jnp.concatenate([corr, corr * lane, jnp.zeros((6, LANES), F32)], axis=0)
-            both.append(pair.astype(BF16))
-        for k in members:
-            turned = dot(both[k], table[which[k]], (1, 0))
+            pair = jnp.concatenate([corr, corr * lane, jnp.zeros((14, LANES), F32)], axis=0)
+            both.append(pair)
+        for k, turned in enumerate(paired([p.astype(BF16) for p in both], powers, (1, 0))):
             local_one[pl.ds(which[k], 1), :] = turned[0:1]
             local_two[pl.ds(which[k], 1), :] = turned[1:2]
         return 0
@@ -558,34 +602,47 @@
     refs[-1][...] = total.astype(BF16)
 
 
-def ordered(parts, slots):
+def merge_kernel(subs, *refs):
+    parts, (out, slots) = refs[:-2], refs[-2:]
     count = len(parts)
     mine = lax.axis_index("ctx")
     for turn, part in enumerate(parts):
-        slots[lax.rem(mine + count - turn, count)] = part[...]
+        slots[lax.rem(mine // 2 + count - turn, count)] = part[...]
+    total = slots[0].astype(F32)
+    for k in range(1, count):
+        total += slots[k].astype(F32)
+    rows = total.shape[0]
+    if subs == 1:
+        out[...] = total.astype(BF16)
+    else:
+        out[...] = jnp.zeros(out.shape, BF16)
+        out[pl.ds(pl.multiple_of(lax.rem(mine, subs) * rows, rows), rows), :] = total.astype(BF16)
 
 
 def owner_kernel(chunks, subs, *refs):
-    parts, inputs, outs = refs[:chunks], refs[chunks : chunks + 6], refs[chunks + 6 :]
-    one, two, decay, scale_in, real, imag = inputs
-    grad_weight, grad_bias, grad_decay, grad_freq, grad_real, grad_imag, *vectors, slots = outs
+    slabs, refs = refs[:chunks], refs[chunks:]
+    one, two, decay, scale_in, real, imag = refs[:6]
+    grad_weight, grad_bias, grad_decay, grad_freq, grad_real, grad_imag, *vectors, slots = refs[6:]
     own, states = decay.shape
-    grad_weight[...] = one[0:own].astype(F32) + two[0:own].astype(F32)
-    line = one[own : own + 1].astype(F32) + two[own : own + 1].astype(F32)
+    wide = grad_weight.shape[1]
+    mine = lax.axis_index("ctx")
+    for turn, slab in enumerate(slabs):
+        slots[lax.rem(mine + chunks - turn, chunks)] = slab[...]
+    slab = slots[0].astype(F32)
+    for k in range(1, chunks):
+        slab += slots[k].astype(F32)
+    grad_weight[...] = slab[0:own]
+    line = slab[own : own + 1]
     segment = grad_bias.shape[1]
     shard = lax.axis_index("shard")
     row = jnp.zeros((1, segment), F32)
-    for s in range(line.shape[1] // segment):
+    for s in range(wide // segment):
         row = jnp.where(shard == s, line[:, s * segment : (s + 1) * segment], row)
     grad_bias[...] = row
-    ordered(parts, slots)
     chans = own // subs
-    sums = []
-    for sub in range(subs):
-        total = slots[sub].astype(F32)
-        for k in range(sub + subs, chunks, subs):
-            total += slots[k].astype(F32)
-        sums.append(total)
+    each = chans + 16
+    total = one[...].astype(F32) + two[...].astype(F32)
+    sums = [total[each * sub : each * (sub + 1)] for sub in range(subs)]
     moments = jnp.concatenate([t[0:chans] for t in sums], axis=0)
     one_re, one_im, two_re, two_im = (moments[:, k * states : (k + 1) * states] for k in range(4))
     scale = scale_in[...]
@@ -603,8 +660,9 @@
 
 def final_kernel(arrived, tokens, cotangent, out):
     seqs, rows, width = tokens.shape
+    inner = arrived[...].reshape(width, seqs * rows).astype(F32).T
     for n in range(seqs):
-        d = arrived[:, n].reshape(width, LANES).astype(F32).T[0:rows]
+        d = inner[n * rows : (n + 1) * rows]
         xhat, inv = row_stats(tokens[n].astype(F32))
         mean = jnp.mean(d, axis=-1, keepdims=True)
         along = jnp.mean(d * xhat, axis=-1, keepdims=True)
@@ -668,12 +726,13 @@
     def sems(*shape):
         return pltpu.SemaphoreType.DMA(shape)
 
-    wire = ((blocks, seqs, chans, LANES), BF16, 1)
+    wire = ((blocks, chans, seqs * rows), BF16, 1)
+    partner = lax.ppermute(lengths, "shard", plan.across)
     flow, like_tokens = wire[:2], (tokens.shape, BF16)
-    on_wire, on_rows = here(wire[0]), here(tokens.shape)
+    on_wire = here(wire[0])
     (first,) = call(
-        norm_kernel, COST[0], [flow], [SMEM, VMEM]
-    )(lengths, *in_hbm(tokens))
+        norm_kernel, COST[0], [flow], [VMEM]
+    )(tokens)
     first = exchange(first)
     piece, pack = lax.optimization_barrier((piece, pack))
     near = [piece] + [lax.ppermute(piece, "shard", route) for route in plan.climb]
@@ -695,25 +754,26 @@
         functools.partial(forward_kernel, chunks, rows, plan.order),
         COST[2],
         [wire, low],
-        [VMEM, VMEM, HBM, HBM],
+        [SMEM, SMEM, VMEM, VMEM, HBM, HBM],
         [buffer, buffer, buffer, on_wire, low_buffer] + tables + [sems(2, blocks)],
-    )(first, pack, *far_tables)
+    )(lengths, partner, first, pack, *far_tables)
     prefix_type = ((chans, 2 * (total - 2 * seqs), LANES), BF16, 1)
     by_channel = ((chans, total, LANES), BF16, 1)
     mirrored, prefix = call(
         functools.partial(prefix_kernel, chunks, rows, plan.order),
         6,
         [by_channel, prefix_type],
-        [VMEM, VMEM, HBM, HBM],
+        [SMEM, SMEM, VMEM, VMEM, HBM, HBM],
         [buffer, here(*by_channel[:2]), here(*prefix_type[:2])] + tables + [sems(2)],
-    )(first, pack, *far_tables)
+    )(lengths, partner, first, pack, *far_tables)
     hidden, near = lax.optimization_barrier((hidden, near))
     across = [lax.ppermute(p, "shard", plan.across) for p in near]
     hidden = exchange(hidden)
+    hidden, mirrored, prefix = lax.optimization_barrier((hidden, mirrored, prefix))
     block_out, back, outers = call(
         functools.partial(glu_kernel, plan),
         COST[3],
-        [like_tokens, flow, ((seqs * LANES, 2 * width), BF16)],
+        [like_tokens, flow, ((seqs * rows, 2 * width), BF16)],
         [SMEM] + [VMEM] * (3 + 2 * plan.layers),
         [here((width, 2 * width))],
     )(lengths, hidden, *in_hbm(tokens, cotangent), *near, *across)
@@ -733,17 +793,14 @@
         functools.partial(backward_kernel, chunks, rows, plan.order),
         COST[4],
         [wire, by_channel, ((2, chans, LANES), F32)],
-        [VMEM, VMEM, VMEM, HBM, HBM, HBM],
+        [SMEM, SMEM, VMEM, VMEM, VMEM, HBM, HBM, HBM],
         [buffer, buffer, buffer, low_buffer, here(*by_channel[:2]), on_wire]
         + tables
         + [sems(3, blocks)],
-    )(back, first, pack, *far_tables, *in_hbm(slope))
+    )(lengths, partner, back, first, pack, *far_tables, *in_hbm(slope))
     (owned,) = call(add_kernel, 1, [slab], [VMEM] * plan.layers)(shares[0], *climbed)
-    first_sum = owned
-    for route in plan.fold[:-1]:
-        (owned,) = call(add_kernel, 1, [slab], [VMEM] * 2)(owned, lax.ppermute(owned, "ctx", route))
-    folded = lax.ppermute(owned, "ctx", plan.fold[-1])
-    tallies, first_sum = lax.optimization_barrier((tallies, first_sum))
+    wholes = [owned] + [lax.ppermute(owned, "ctx", route) for route in plan.rotate]
+    tallies, owned = lax.optimization_barrier((tallies, owned))
     state = (chans + 16, 2 * LANES)
     (sums,) = call(
         functools.partial(moment_kernel, chunks, rows),
@@ -754,7 +811,7 @@
         + [tables[0], here(*by_channel[:2]), here(*prefix_type[:2]), here(*by_channel[:2])]
         + [sems(4, chans // 8)],
     )(far_tables[0], *in_hbm(mirrored, prefix, local_grads), firsts, tallies)
-    leaving = exchange(leaving)
+    leaving, wholes = lax.optimization_barrier((exchange(leaving), wholes))
     (tokens_grad,) = call(
         final_kernel,
         COST[5],
@@ -766,14 +823,23 @@
 
     parts = [lax.ppermute(sums, BOTH, route) for route in plan.give]
     tokens_grad, parts = lax.optimization_barrier((tokens_grad, parts))
+    (part,) = call(
+        functools.partial(merge_kernel, subs),
+        1,
+        [((subs * state[0], state[1]), BF16)],
+        [VMEM] * len(parts),
+        [here((len(parts),) + state)],
+    )(*parts)
     matrix, vector = ((own, states), F32), ((1, own), F32)
     grad_weight, grad_bias, *grads = call(
         functools.partial(owner_kernel, chunks, subs),
         2,
         [(out_weight.shape, F32), ((1, segment), F32)] + [matrix] * 4 + [vector] * 3,
         [VMEM] * (chunks + 6),
-        [here((chunks,) + state)],
-    )(*parts, owned, folded, *in_hbm(decay_rate, scale, coef_real, coef_imag))
+        [here((chunks,) + slab[0])],
+    )(
+        *wholes, part, lax.ppermute(part, "ctx", plan.beside), decay_rate, scale, coef_real, coef_imag
+    )
     return (
         block_out,
         tokens_grad,

time: 99.3 us -> 95 us (0.957)
  starting transfers between devices: 43.7 us -> 40.6 us
  Pallas kernels: 40.8 us -> 37.7 us
  waiting for transfers between devices: 13.2 us -> 14.3 us
    ppermute x4 -> x2, starting transfers between devices: 9.61 us -> 1.62 us  [per_device(): parts = [lax.ppermute(sums, BOTH, route) for route in plan.give]]
    ppermute x1 -> x3, waiting for transfers between devices: 0.01 us -> 5.06 us  [per_device(): lax.ppermute(owned, 'ctx', route)]
    all_to_all x4, waiting for transfers between devices: 8.81 us -> 4.74 us  [exchange(): lax.all_to_all(buffer, BOTH, 0, 0, axis_index_groups=plan.groups, tiled=T...]
    ppermute x4 -> x2, waiting for transfers between devices: 3.15 us -> 0.01 us  [per_device(): parts = [lax.ppermute(sums, BOTH, route) for route in plan.give]]
    ppermute x1 -> x2, waiting for transfers between devices: 0.01 us -> 2.69 us  [the longest x1 2.69 us: per_device(): lax.ppermute(part, 'ctx', plan.beside)]
    ppermute x1 -> x3, starting transfers between devices: 2.08 us -> 4.01 us  [per_device(): lax.ppermute(owned, 'ctx', route)]
    ppermute x3, waiting for transfers between devices: 0.01 us -> 1.78 us  [per_device(): lax.ppermute(piece, 'shard', route)]
    ppermute x1 -> x2, starting transfers between devices: 0.13 us -> 1.9 us  [the longest x1 1.38 us: per_device(): lax.ppermute(part, 'ctx', plan.beside)]
  transfers between devices with their start and end apart: 22 -> 23, of which waited for: 8 -> 6; matrix products, arithmetic and copies ran while one was open for 0% -> 0% of each run, Pallas kernels for 33% -> 35%
where the time goes in v4:
time: 95 us; the launch traced here: 93.5 us
  starting transfers between devices  40.6 us (43%)
  Pallas kernels  37.7 us (40%)
  waiting for transfers between devices  14.3 us (15%)
    all_to_all x4, starting transfers between devices, exchange(): lax.all_to_all(buffer, BOTH, 0, 0, axis_index_groups=plan.groups, tiled=T...  20.7 us
    pallas_call x1, Pallas kernels, per_device(): call(functools.partial(backward_kernel, chunks, rows, plan.order), COST[4...  7.13 us
    pallas_call x1, Pallas kernels, per_device(): call(functools.partial(forward_kernel, chunks, rows, plan.order), COST[2]...  6.49 us
    ppermute x3, starting transfers between devices, per_device(): lax.ppermute(v, 'shard', route)  5.91 us
    ppermute x3, waiting for transfers between devices, per_device(): lax.ppermute(owned, 'ctx', route)  5.06 us
    pallas_call x1, Pallas kernels, per_device(): call(functools.partial(prefix_kernel, chunks, rows, plan.order), 6, [by_c...  4.75 us
    all_to_all x4, waiting for transfers between devices, exchange(): lax.all_to_all(buffer, BOTH, 0, 0, axis_index_groups=plan.groups, tiled=T...  4.74 us
    ppermute x3, starting transfers between devices, per_device(): lax.ppermute(piece, 'shard', route)  4.72 us
  transfers between devices with their start and end apart: 23, of which 6 were waited for; matrix products, arithmetic and copies ran while one was open for 0% of the time, Pallas kernels for 35%

profile of v4, /device:TPU:0, one launch (start us, length us, event | category | flops | bytes accessed | tf_op | source)
XLA Modules:
  0.0 93.5 jit_solution(12003900103068454343)
XLA Ops:
  0.6 0.5 collective-permute-start
  1.2 1.2 %shard_map.204 = (f32[64,384]{1,0:T(8,128)S(1)}, f32[64,64]{1,0:T(8,128)S(1)}, bf16[80,1024]{1,0:T(8,128)(2,1)S(1)}) custom-call(f32[64,64]{1,0:T(8,128)} %refs_6_.1, f32[64,64]{1,0:T(8,128)} %freq.1, f32[64,64]{1,0:T(8,128)} %refs_8_.1, f32[64,64]{1,0:T(8,128)} %refs_9_.1, f32[1,64]{1,0:T(1,128)} %bitcast.8, f32[1,64]{1,0:T(1,128)} %bitcast.9, ...), custom_call_target="tpu_custom_call" | custom-call | flops 2000000000 | bytes 7000000 | tf_op jit(solution)/shard_map/pallas_call | solution.py:708
  2.4 0.7 collective-permute-start.1
  3.1 0.0 copy-done.1
  3.1 1.1 %shard_map.203 = bf16[8,64,384]{2,1,0:T(8,128)(2,1)} custom-call(bf16[4,96,512]{2,1,0:T(8,128)(2,1)S(1)} %copy-done.1), custom_call_target="tpu_custom_call" | custom-call | flops 2000000000 | bytes 7000000 | tf_op jit(solution)/shard_map/pallas_call | solution.py:733
  4.2 9.5 %all-to-all-start = ((bf16[8,64,384]{2,1,0:T(8,128)(2,1)}), bf16[8,64,384]{2,1,0:T(8,128)(2,1)S(1)}, u32[]{:S(2)}, u32[]{:S(2)}) async-start(bf16[8,64,384]{2,1,0:T(8,128)(2,1)} %shard_map.203), calls=%async_computation | async-start | bytes 786432 | tf_op jit(solution)/shard_map/all_to_all | solution.py:705
  13.7 0.0 collective-permute-done.1.pack
  13.7 0.0 copy-start
  13.7 4.2 %collective-permute-start.4 = (bf16[80,1024]{1,0:T(8,128)(2,1)S(1)}, bf16[80,1024]{1,0:T(8,128)(2,1)S(1)}, u32[]{:S(2)}, u32[]{:S(2)}) collective-permute-start(bf16[80,1024]{1,0:T(8,128)(2,1)S(1)} %get-tuple-element.72.refs_0_), channel_id=1, source_target_pairs={{0,24},{4,28},{8,0},{12,4},{16,8},{20,12},{24,16},{28,20},{1,25},{... | collective-permute-start | bytes 491528 | tf_op jit(solution)/shard_map/ppermute | solution.py:738
  17.9 0.0 collective-permute-start.3
  17.9 0.6 collective-permute-start.2
  18.5 4.4 %shard_map.205 = (bf16[64,128,128]{2,1,0:T(8,128)(2,1)}, f32[64,8,128]{2,1,0:T(8,128)}, f32[2,64,128]{2,1,0:T(8,128)S(1)}) custom-call(f32[64,384]{1,0:T(8,128)S(1)} %collective-permute-done.1.pack), custom_call_target="tpu_custom_call" | custom-call | flops 8000000000 | bytes 28000000 | tf_op jit(solution)/shard_map/pallas_call | solution.py:741
  22.9 0.0 collective-permute-done.partner
  22.9 0.0 all-to-all-done.arrived.first
  22.9 0.0 copy-done
  22.9 6.5 %shard_map.206 = (bf16[8,64,384]{2,1,0:T(8,128)(2,1)}, bf16[2048,128]{1,0:T(8,128)(2,1)}) custom-call(s32[4]{0:T(128)S(1)} %copy-done, s32[4]{0:T(128)S(1)} %collective-permute-done.partner, bf16[8,64,384]{2,1,0:T(8,128)(2,1)S(1)} %all-to-all-done.arrived.first, f32[64,384]{1,0:T(8,128)S(1)} %collective-permute-done.1.pack, ...), custom_call_target="tpu_custom_call" | custom-call | flops 10000000000 | bytes 35000000 | tf_op jit(solution)/shard_map/pallas_call | solution.py:753
  29.4 0.0 collective-permute-done.4.refs_3_
  29.5 1.8 %collective-permute-done.3.refs_2_ = bf16[80,1024]{1,0:T(8,128)(2,1)S(1)} collective-permute-done((bf16[80,1024]{1,0:T(8,128)(2,1)S(1)}, bf16[80,1024]{1,0:T(8,128)(2,1)S(1)}, u32[]{:S(2)}, u32[]{:S(2)}) %collective-permute-start.3) | collective-permute-done | bytes 163872 | tf_op jit(solution)/shard_map/ppermute | solution.py:738
  31.2 0.0 collective-permute-done.2.refs_1_
  31.2 4.2 %all-to-all-start.1 = ((bf16[8,64,384]{2,1,0:T(8,128)(2,1)}), bf16[8,64,384]{2,1,0:T(8,128)(2,1)S(1)}, u32[]{:S(2)}, u32[]{:S(2)}) async-start(bf16[8,64,384]{2,1,0:T(8,128)(2,1)} %get-tuple-element.68), calls=%async_computation.1 | async-start | bytes 786432 | tf_op jit(solution)/shard_map/all_to_all | solution.py:705
  35.5 0.5 collective-permute-start.5
  36.0 0.0 collective-permute-start.6
  36.0 0.5 collective-permute-start.7
  36.5 0.0 collective-permute-start.8
  36.5 4.7 %shard_map.207 = (bf16[64,32,128]{2,1,0:T(8,128)(2,1)}, bf16[64,48,128]{2,1,0:T(8,128)(2,1)}) custom-call(s32[4]{0:T(128)S(1)} %copy-done, s32[4]{0:T(128)S(1)} %collective-permute-done.partner, bf16[8,64,384]{2,1,0:T(8,128)(2,1)S(1)} %all-to-all-done.arrived.first, f32[64,384]{1,0:T(8,128)S(1)} %collective-permute-done.1.pack, ...), custom_call_target="tpu_custom_call" | custom-call | flops 6000000000 | bytes 21000000 | tf_op jit(solution)/shard_map/pallas_call | solution.py:762
  41.2 2.6 %all-to-all-done.1.arrived = bf16[8,64,384]{2,1,0:T(8,128)(2,1)S(1)} async-done(((bf16[8,64,384]{2,1,0:T(8,128)(2,1)}), bf16[8,64,384]{2,1,0:T(8,128)(2,1)S(1)}, u32[]{:S(2)}, u32[]{:S(2)}) %all-to-all-start.1) | async-done | bytes 393248 | tf_op jit(solution)/shard_map/all_to_all | solution.py:705
  43.8 0.0 collective-permute-done.5.refs_4_
  43.8 0.0 collective-permute-done.6.refs_5_
  43.8 0.0 collective-permute-done.7.refs_6_
  43.8 0.0 collective-permute-done.8.refs_7_
  43.8 3.5 %shard_map.208 = (bf16[4,96,512]{2,1,0:T(8,128)(2,1)}, bf16[8,64,384]{2,1,0:T(8,128)(2,1)}, bf16[384,1024]{1,0:T(8,128)(2,1)S(1)}) custom-call(s32[4]{0:T(128)S(1)} %copy-done, bf16[8,64,384]{2,1,0:T(8,128)(2,1)S(1)} %all-to-all-done.1.arrived, bf16[4,96,512]{2,1,0:T(8,128)(2,1)} %tokens.5, bf16[4,96,512]{2,1,0:T(8,128)(2,1)} %cotangent.3, ...), custom_call_target="tpu_custom_call" | custom-call | flops 6000000000 | bytes 21000000 | tf_op jit(solution)/shard_map/pallas_call | solution.py:773
  47.4 0.7 shard_map.210
  48.1 0.1 collective-permute-start.9
  48.2 3.5 %all-to-all-start.2 = ((bf16[8,64,384]{2,1,0:T(8,128)(2,1)}), bf16[8,64,384]{2,1,0:T(8,128)(2,1)S(1)}, u32[]{:S(2)}, u32[]{:S(2)}) async-start(bf16[8,64,384]{2,1,0:T(8,128)(2,1)} %get-tuple-element.77), calls=%async_computation.2 | async-start | bytes 786432 | tf_op jit(solution)/shard_map/all_to_all | solution.py:705
  51.7 0.0 collective-permute-done.9.came
  51.7 0.2 shard_map.211
  51.8 1.2 %collective-permute-start.10 = (bf16[80,1024]{1,0:T(8,128)(2,1)S(1)}, bf16[80,1024]{1,0:T(8,128)(2,1)S(1)}, u32[]{:S(2)}, u32[]{:S(2)}) collective-permute-start(bf16[80,1024]{1,0:T(8,128)(2,1)S(1)} %get-tuple-element.84), channel_id=1, source_target_pairs={{0,8},{4,12},{8,16},{12,20},{16,24},{20,28},{24,0},{28,4},{1,9},{5... | collective-permute-start | bytes 491528 | tf_op jit(solution)/shard_map/ppermute | solution.py:791
  53.0 1.9 %collective-permute-start.11 = (bf16[80,1024]{1,0:T(8,128)(2,1)S(1)}, bf16[80,1024]{1,0:T(8,128)(2,1)S(1)}, u32[]{:S(2)}, u32[]{:S(2)}) collective-permute-start(bf16[80,1024]{1,0:T(8,128)(2,1)S(1)} %get-tuple-element.85), channel_id=1, source_target_pairs={{0,16},{4,20},{8,24},{12,28},{16,0},{20,4},{24,8},{28,12},{1,17},{... | collective-permute-start | bytes 491528 | tf_op jit(solution)/shard_map/ppermute | solution.py:791
  54.9 2.8 %collective-permute-start.12 = (bf16[80,1024]{1,0:T(8,128)(2,1)S(1)}, bf16[80,1024]{1,0:T(8,128)(2,1)S(1)}, u32[]{:S(2)}, u32[]{:S(2)}) collective-permute-start(bf16[80,1024]{1,0:T(8,128)(2,1)S(1)} %get-tuple-element.86), channel_id=1, source_target_pairs={{0,24},{4,28},{8,0},{12,4},{16,8},{20,12},{24,16},{28,20},{1,25},{... | collective-permute-start | bytes 491528 | tf_op jit(solution)/shard_map/ppermute | solution.py:791
  57.8 2.2 %all-to-all-done.2.arrived = bf16[8,64,384]{2,1,0:T(8,128)(2,1)S(1)} async-done(((bf16[8,64,384]{2,1,0:T(8,128)(2,1)}), bf16[8,64,384]{2,1,0:T(8,128)(2,1)S(1)}, u32[]{:S(2)}, u32[]{:S(2)}) %all-to-all-start.2) | async-done | bytes 393248 | tf_op jit(solution)/shard_map/all_to_all | solution.py:705
  59.9 7.1 %shard_map.209 = (bf16[8,64,384]{2,1,0:T(8,128)(2,1)}, bf16[64,32,128]{2,1,0:T(8,128)(2,1)}, f32[2,64,128]{2,1,0:T(8,128)S(1)}) custom-call(s32[4]{0:T(128)S(1)} %copy-done, s32[4]{0:T(128)S(1)} %collective-permute-done.partner, bf16[8,64,384]{2,1,0:T(8,128)(2,1)S(1)} %all-to-all-done.2.arrived, bf16[8,64,384]{2,1,0:T(8,128)(2,1)S(1)} %all-to-all-done.arrived.first, ...), custom_call_target="tpu_custom_call" | custom-call | flops 1000000000 | bytes 3500000 | tf_op jit(solution)/shard_map/pallas_call | solution.py:792
  67.1 3.5 %all-to-all-start.3 = ((bf16[8,64,384]{2,1,0:T(8,128)(2,1)}), bf16[8,64,384]{2,1,0:T(8,128)(2,1)S(1)}, u32[]{:S(2)}, u32[]{:S(2)}) async-start(bf16[8,64,384]{2,1,0:T(8,128)(2,1)} %get-tuple-element.79), calls=%async_computation.3 | async-start | bytes 786432 | tf_op jit(solution)/shard_map/all_to_all | solution.py:705
  70.5 0.0 collective-permute-done.10.refs_1_
  70.5 0.0 collective-permute-done.11.refs_2_
  70.6 0.0 collective-permute-done.12.refs_3_
  70.6 0.1 shard_map.212.refs_0_
  70.7 2.9 %collective-permute-start.15 = (bf16[80,1024]{1,0:T(8,128)(2,1)S(1)}, bf16[80,1024]{1,0:T(8,128)(2,1)S(1)}, u32[]{:S(2)}, u32[]{:S(2)}) collective-permute-start(bf16[80,1024]{1,0:T(8,128)(2,1)S(1)} %shard_map.212.refs_0_), channel_id=1, source_target_pairs={{0,3},{1,0},{2,1},{3,2},{4,7},{5,4},{6,5},{7,6},{8,11},{9,8},{10,9... | collective-permute-start | bytes 491528 | tf_op jit(solution)/shard_map/ppermute | solution.py:802
  73.6 0.5 collective-permute-start.14
  74.1 0.6 collective-permute-start.13
  74.7 4.5 %shard_map.214 = bf16[80,256]{1,0:T(8,128)(2,1)S(1)} custom-call(bf16[64,128,128]{2,1,0:T(8,128)(2,1)} %get-tuple-element.64.far_table, bf16[64,32,128]{2,1,0:T(8,128)(2,1)} %get-tuple-element.88.far_mirrored, bf16[64,48,128]{2,1,0:T(8,128)(2,1)} %get-tuple-element.89.far_prefix, bf16[64,32,128]{2,1,0:T(8,128)(2,1)} %get-tuple-element.90.far_grads, ...), custom_call_target="tpu_custom_call" | custom-call | flops 8000000000 | bytes 28000000 | tf_op jit(solution)/shard_map/pallas_call | solution.py:805
  79.1 1.0 %collective-permute-start.17 = (bf16[80,256]{1,0:T(8,128)(2,1)S(1)}, bf16[80,256]{1,0:T(8,128)(2,1)S(1)}, u32[]{:S(2)}, u32[]{:S(2)}) collective-permute-start(bf16[80,256]{1,0:T(8,128)(2,1)S(1)} %shard_map.214), channel_id=1, source_target_pairs={{0,2},{4,6},{1,10},{5,14},{2,18},{6,22},{3,26},{7,30},{8,3},{12,7}... | collective-permute-start | bytes 122888 | tf_op jit(solution)/shard_map/ppermute | solution.py:824
  80.1 0.7 collective-permute-start.16
  80.8 0.0 all-to-all-done.3.arrived
  80.8 1.1 %collective-permute-done.15.refs_3_ = bf16[80,1024]{1,0:T(8,128)(2,1)S(1)} collective-permute-done((bf16[80,1024]{1,0:T(8,128)(2,1)S(1)}, bf16[80,1024]{1,0:T(8,128)(2,1)S(1)}, u32[]{:S(2)}, u32[]{:S(2)}) %collective-permute-start.15) | collective-permute-done | bytes 163872 | tf_op jit(solution)/shard_map/ppermute | solution.py:802
  81.9 0.0 collective-permute-done.14.refs_2_
  81.9 4.0 %collective-permute-done.13.refs_1_ = bf16[80,1024]{1,0:T(8,128)(2,1)S(1)} collective-permute-done((bf16[80,1024]{1,0:T(8,128)(2,1)S(1)}, bf16[80,1024]{1,0:T(8,128)(2,1)S(1)}, u32[]{:S(2)}, u32[]{:S(2)}) %collective-permute-start.13) | collective-permute-done | bytes 163872 | tf_op jit(solution)/shard_map/ppermute | solution.py:802
  85.8 2.6 %shard_map.213 = bf16[4,96,512]{2,1,0:T(8,128)(2,1)} custom-call(bf16[8,64,384]{2,1,0:T(8,128)(2,1)S(1)} %all-to-all-done.3.arrived, bf16[4,96,512]{2,1,0:T(8,128)(2,1)} %tokens.5, bf16[4,96,512]{2,1,0:T(8,128)(2,1)} %cotangent.3), custom_call_target="tpu_custom_call" | custom-call | flops 3000000000 | bytes 10500000 | tf_op jit(solution)/shard_map/pallas_call | solution.py:815
  88.4 0.0 collective-permute-done.17.refs_1_
  88.4 0.0 collective-permute-done.16.refs_0_
  88.5 1.4 %collective-permute-start.18 = (bf16[80,256]{1,0:T(8,128)(2,1)S(1)}, bf16[80,256]{1,0:T(8,128)(2,1)S(1)}, u32[]{:S(2)}, u32[]{:S(2)}) collective-permute-start(bf16[80,256]{1,0:T(8,128)(2,1)S(1)} %shard_map.215.refs_4_), channel_id=1, source_target_pairs={{0,1},{1,0},{2,3},{3,2},{4,5},{5,4},{6,7},{7,6},{8,9},{9,8},{10,11... | collective-permute-start | bytes 122888 | tf_op jit(solution)/shard_map/ppermute | solution.py:841
  89.9 2.7 %collective-permute-done.18.refs_5_ = bf16[80,256]{1,0:T(8,128)(2,1)S(1)} collective-permute-done((bf16[80,256]{1,0:T(8,128)(2,1)S(1)}, bf16[80,256]{1,0:T(8,128)(2,1)S(1)}, u32[]{:S(2)}, u32[]{:S(2)}) %collective-permute-start.18) | collective-permute-done | bytes 40992 | tf_op jit(solution)/shard_map/ppermute | solution.py:841
  92.6 0.0 copy-done.2
  92.6 0.0 copy-done.4
  92.6 0.9 shard_map.216
  (6 shorter events, 0.0 us)
Async XLA Ops:
  0.6 22.3 %collective-permute-start = (s32[4]{0:T(128)}, s32[4]{0:T(128)S(1)}, u32[]{:S(2)}, u32[]{:S(2)}) collective-permute-start(s32[4]{0:T(128)} %lengths.7), channel_id=1, source_target_pairs={{0,4},{4,0},{8,12},{12,8},{16,20},{20,16},{24,28},{28,24},{1,5},{5... | collective-permute-start | bytes 56 | tf_op jit(solution)/shard_map/ppermute | solution.py:730
  1.2 1.9 %copy-start.1 = (bf16[4,96,512]{2,1,0:T(8,128)(2,1)S(1)}, bf16[4,96,512]{2,1,0:T(8,128)(2,1)}, u32[]{:S(2)}) copy-start(bf16[4,96,512]{2,1,0:T(8,128)(2,1)} %tokens.5) | copy-start | bytes 1179652
  2.4 11.3 %collective-permute-start.1 = (f32[64,384]{1,0:T(8,128)S(1)}, f32[64,384]{1,0:T(8,128)S(1)}, u32[]{:S(2)}, u32[]{:S(2)}) collective-permute-start(f32[64,384]{1,0:T(8,128)S(1)} %get-tuple-element.62), channel_id=1, source_target_pairs={{0,0},{4,4},{8,1},{12,5},{16,2},{20,6},{24,3},{28,7},{1,8},{5,12},... | collective-permute-start | bytes 294920 | tf_op jit(solution)/shard_map/ppermute | solution.py:721
  4.2 18.7 %all-to-all-start = ((bf16[8,64,384]{2,1,0:T(8,128)(2,1)}), bf16[8,64,384]{2,1,0:T(8,128)(2,1)S(1)}, u32[]{:S(2)}, u32[]{:S(2)}) async-start(bf16[8,64,384]{2,1,0:T(8,128)(2,1)} %shard_map.203), calls=%async_computation | async-start | bytes 786432 | tf_op jit(solution)/shard_map/all_to_all | solution.py:705
  13.7 9.2 %copy-start = (s32[4]{0:T(128)S(1)}, s32[4]{0:T(128)}, u32[]{:S(2)}) copy-start(s32[4]{0:T(128)} %lengths.7) | copy-start | bytes 52
  13.7 15.7 %collective-permute-start.4 = (bf16[80,1024]{1,0:T(8,128)(2,1)S(1)}, bf16[80,1024]{1,0:T(8,128)(2,1)S(1)}, u32[]{:S(2)}, u32[]{:S(2)}) collective-permute-start(bf16[80,1024]{1,0:T(8,128)(2,1)S(1)} %get-tuple-element.72.refs_0_), channel_id=1, source_target_pairs={{0,24},{4,28},{8,0},{12,4},{16,8},{20,12},{24,16},{28,20},{1,25},{... | collective-permute-start | bytes 491528 | tf_op jit(solution)/shard_map/ppermute | solution.py:738
  17.9 13.3 %collective-permute-start.3 = (bf16[80,1024]{1,0:T(8,128)(2,1)S(1)}, bf16[80,1024]{1,0:T(8,128)(2,1)S(1)}, u32[]{:S(2)}, u32[]{:S(2)}) collective-permute-start(bf16[80,1024]{1,0:T(8,128)(2,1)S(1)} %get-tuple-element.72.refs_0_), channel_id=1, source_target_pairs={{0,16},{4,20},{8,24},{12,28},{16,0},{20,4},{24,8},{28,12},{1,17},{... | collective-permute-start | bytes 491528 | tf_op jit(solution)/shard_map/ppermute | solution.py:738
  17.9 13.3 %collective-permute-start.2 = (bf16[80,1024]{1,0:T(8,128)(2,1)S(1)}, bf16[80,1024]{1,0:T(8,128)(2,1)S(1)}, u32[]{:S(2)}, u32[]{:S(2)}) collective-permute-start(bf16[80,1024]{1,0:T(8,128)(2,1)S(1)} %get-tuple-element.72.refs_0_), channel_id=1, source_target_pairs={{0,8},{4,12},{8,16},{12,20},{16,24},{20,28},{24,0},{28,4},{1,9},{5... | collective-permute-start | bytes 491528 | tf_op jit(solution)/shard_map/ppermute | solution.py:738
  31.2 12.6 %all-to-all-start.1 = ((bf16[8,64,384]{2,1,0:T(8,128)(2,1)}), bf16[8,64,384]{2,1,0:T(8,128)(2,1)S(1)}, u32[]{:S(2)}, u32[]{:S(2)}) async-start(bf16[8,64,384]{2,1,0:T(8,128)(2,1)} %get-tuple-element.68), calls=%async_computation.1 | async-start | bytes 786432 | tf_op jit(solution)/shard_map/all_to_all | solution.py:705
  35.5 8.3 %collective-permute-start.5 = (bf16[80,1024]{1,0:T(8,128)(2,1)S(1)}, bf16[80,1024]{1,0:T(8,128)(2,1)S(1)}, u32[]{:S(2)}, u32[]{:S(2)}) collective-permute-start(bf16[80,1024]{1,0:T(8,128)(2,1)S(1)} %get-tuple-element.72.refs_0_), channel_id=1, source_target_pairs={{0,4},{4,0},{8,12},{12,8},{16,20},{20,16},{24,28},{28,24},{1,5},{5... | collective-permute-start | bytes 491528 | tf_op jit(solution)/shard_map/ppermute | solution.py:770
  36.0 7.8 %collective-permute-start.6 = (bf16[80,1024]{1,0:T(8,128)(2,1)S(1)}, bf16[80,1024]{1,0:T(8,128)(2,1)S(1)}, u32[]{:S(2)}, u32[]{:S(2)}) collective-permute-start(bf16[80,1024]{1,0:T(8,128)(2,1)S(1)} %collective-permute-done.2.refs_1_), channel_id=1, source_target_pairs={{0,4},{4,0},{8,12},{12,8},{16,20},{20,16},{24,28},{28,24},{1,5},{5... | collective-permute-start | bytes 491528 | tf_op jit(solution)/shard_map/ppermute | solution.py:770
  36.0 7.8 %collective-permute-start.7 = (bf16[80,1024]{1,0:T(8,128)(2,1)S(1)}, bf16[80,1024]{1,0:T(8,128)(2,1)S(1)}, u32[]{:S(2)}, u32[]{:S(2)}) collective-permute-start(bf16[80,1024]{1,0:T(8,128)(2,1)S(1)} %collective-permute-done.3.refs_2_), channel_id=1, source_target_pairs={{0,4},{4,0},{8,12},{12,8},{16,20},{20,16},{24,28},{28,24},{1,5},{5... | collective-permute-start | bytes 491528 | tf_op jit(solution)/shard_map/ppermute | solution.py:770
  36.5 7.3 %collective-permute-start.8 = (bf16[80,1024]{1,0:T(8,128)(2,1)S(1)}, bf16[80,1024]{1,0:T(8,128)(2,1)S(1)}, u32[]{:S(2)}, u32[]{:S(2)}) collective-permute-start(bf16[80,1024]{1,0:T(8,128)(2,1)S(1)} %collective-permute-done.4.refs_3_), channel_id=1, source_target_pairs={{0,4},{4,0},{8,12},{12,8},{16,20},{20,16},{24,28},{28,24},{1,5},{5... | collective-permute-start | bytes 491528 | tf_op jit(solution)/shard_map/ppermute | solution.py:770
  48.1 3.6 %collective-permute-start.9 = (bf16[4,80,1024]{2,1,0:T(8,128)(2,1)S(1)}, bf16[4,80,1024]{2,1,0:T(8,128)(2,1)S(1)}, u32[]{:S(2)}, u32[]{:S(2)}) collective-permute-start(bf16[4,80,1024]{2,1,0:T(8,128)(2,1)S(1)} %get-tuple-element.82), channel_id=1, source_target_pairs={{0,4},{4,0},{8,12},{12,8},{16,20},{20,16},{24,28},{28,24},{1,5},{5... | collective-permute-start | bytes 1966088 | tf_op jit(solution)/shard_map/ppermute | solution.py:786
  48.2 11.7 %all-to-all-start.2 = ((bf16[8,64,384]{2,1,0:T(8,128)(2,1)}), bf16[8,64,384]{2,1,0:T(8,128)(2,1)S(1)}, u32[]{:S(2)}, u32[]{:S(2)}) async-start(bf16[8,64,384]{2,1,0:T(8,128)(2,1)} %get-tuple-element.77), calls=%async_computation.2 | async-start | bytes 786432 | tf_op jit(solution)/shard_map/all_to_all | solution.py:705
  51.8 18.7 %collective-permute-start.10 = (bf16[80,1024]{1,0:T(8,128)(2,1)S(1)}, bf16[80,1024]{1,0:T(8,128)(2,1)S(1)}, u32[]{:S(2)}, u32[]{:S(2)}) collective-permute-start(bf16[80,1024]{1,0:T(8,128)(2,1)S(1)} %get-tuple-element.84), channel_id=1, source_target_pairs={{0,8},{4,12},{8,16},{12,20},{16,24},{20,28},{24,0},{28,4},{1,9},{5... | collective-permute-start | bytes 491528 | tf_op jit(solution)/shard_map/ppermute | solution.py:791
  53.0 17.5 %collective-permute-start.11 = (bf16[80,1024]{1,0:T(8,128)(2,1)S(1)}, bf16[80,1024]{1,0:T(8,128)(2,1)S(1)}, u32[]{:S(2)}, u32[]{:S(2)}) collective-permute-start(bf16[80,1024]{1,0:T(8,128)(2,1)S(1)} %get-tuple-element.85), channel_id=1, source_target_pairs={{0,16},{4,20},{8,24},{12,28},{16,0},{20,4},{24,8},{28,12},{1,17},{... | collective-permute-start | bytes 491528 | tf_op jit(solution)/shard_map/ppermute | solution.py:791
  54.9 15.7 %collective-permute-start.12 = (bf16[80,1024]{1,0:T(8,128)(2,1)S(1)}, bf16[80,1024]{1,0:T(8,128)(2,1)S(1)}, u32[]{:S(2)}, u32[]{:S(2)}) collective-permute-start(bf16[80,1024]{1,0:T(8,128)(2,1)S(1)} %get-tuple-element.86), channel_id=1, source_target_pairs={{0,24},{4,28},{8,0},{12,4},{16,8},{20,12},{24,16},{28,20},{1,25},{... | collective-permute-start | bytes 491528 | tf_op jit(solution)/shard_map/ppermute | solution.py:791
  67.1 13.7 %all-to-all-start.3 = ((bf16[8,64,384]{2,1,0:T(8,128)(2,1)}), bf16[8,64,384]{2,1,0:T(8,128)(2,1)S(1)}, u32[]{:S(2)}, u32[]{:S(2)}) async-start(bf16[8,64,384]{2,1,0:T(8,128)(2,1)} %get-tuple-element.79), calls=%async_computation.3 | async-start | bytes 786432 | tf_op jit(solution)/shard_map/all_to_all | solution.py:705
  70.7 11.2 %collective-permute-start.15 = (bf16[80,1024]{1,0:T(8,128)(2,1)S(1)}, bf16[80,1024]{1,0:T(8,128)(2,1)S(1)}, u32[]{:S(2)}, u32[]{:S(2)}) collective-permute-start(bf16[80,1024]{1,0:T(8,128)(2,1)S(1)} %shard_map.212.refs_0_), channel_id=1, source_target_pairs={{0,3},{1,0},{2,1},{3,2},{4,7},{5,4},{6,5},{7,6},{8,11},{9,8},{10,9... | collective-permute-start | bytes 491528 | tf_op jit(solution)/shard_map/ppermute | solution.py:802
  73.6 8.3 %collective-permute-start.14 = (bf16[80,1024]{1,0:T(8,128)(2,1)S(1)}, bf16[80,1024]{1,0:T(8,128)(2,1)S(1)}, u32[]{:S(2)}, u32[]{:S(2)}) collective-permute-start(bf16[80,1024]{1,0:T(8,128)(2,1)S(1)} %shard_map.212.refs_0_), channel_id=1, source_target_pairs={{0,2},{1,3},{2,0},{3,1},{4,6},{5,7},{6,4},{7,5},{8,10},{9,11},{10,... | collective-permute-start | bytes 491528 | tf_op jit(solution)/shard_map/ppermute | solution.py:802
  74.1 11.7 %collective-permute-start.13 = (bf16[80,1024]{1,0:T(8,128)(2,1)S(1)}, bf16[80,1024]{1,0:T(8,128)(2,1)S(1)}, u32[]{:S(2)}, u32[]{:S(2)}) collective-permute-start(bf16[80,1024]{1,0:T(8,128)(2,1)S(1)} %shard_map.212.refs_0_), channel_id=1, source_target_pairs={{0,1},{1,2},{2,3},{3,0},{4,5},{5,6},{6,7},{7,4},{8,9},{9,10},{10,1... | collective-permute-start | bytes 491528 | tf_op jit(solution)/shard_map/ppermute | solution.py:802
  79.1 9.3 %collective-permute-start.17 = (bf16[80,256]{1,0:T(8,128)(2,1)S(1)}, bf16[80,256]{1,0:T(8,128)(2,1)S(1)}, u32[]{:S(2)}, u32[]{:S(2)}) collective-permute-start(bf16[80,256]{1,0:T(8,128)(2,1)S(1)} %shard_map.214), channel_id=1, source_target_pairs={{0,2},{4,6},{1,10},{5,14},{2,18},{6,22},{3,26},{7,30},{8,3},{12,7}... | collective-permute-start | bytes 122888 | tf_op jit(solution)/shard_map/ppermute | solution.py:824
  80.1 8.3 %collective-permute-start.16 = (bf16[80,256]{1,0:T(8,128)(2,1)S(1)}, bf16[80,256]{1,0:T(8,128)(2,1)S(1)}, u32[]{:S(2)}, u32[]{:S(2)}) collective-permute-start(bf16[80,256]{1,0:T(8,128)(2,1)S(1)} %shard_map.214), channel_id=1, source_target_pairs={{0,0},{4,4},{1,8},{5,12},{2,16},{6,20},{3,24},{7,28},{8,1},{12,5},... | collective-permute-start | bytes 122888 | tf_op jit(solution)/shard_map/ppermute | solution.py:824
  88.4 4.1 %copy-start.2 = (f32[64,64]{1,0:T(8,128)S(1)}, f32[64,64]{1,0:T(8,128)}, u32[]{:S(2)}) copy-start(f32[64,64]{1,0:T(8,128)} %refs_6_.1) | copy-start | bytes 49156
  88.4 4.1 %copy-start.3 = (f32[64,64]{1,0:T(8,128)S(1)}, f32[64,64]{1,0:T(8,128)}, u32[]{:S(2)}) copy-start(f32[64,64]{1,0:T(8,128)} %refs_8_.1) | copy-start | bytes 49156
  88.4 4.1 %copy-start.4 = (f32[64,64]{1,0:T(8,128)S(1)}, f32[64,64]{1,0:T(8,128)}, u32[]{:S(2)}) copy-start(f32[64,64]{1,0:T(8,128)} %refs_9_.1) | copy-start | bytes 49156
  88.5 4.1 %collective-permute-start.18 = (bf16[80,256]{1,0:T(8,128)(2,1)S(1)}, bf16[80,256]{1,0:T(8,128)(2,1)S(1)}, u32[]{:S(2)}, u32[]{:S(2)}) collective-permute-start(bf16[80,256]{1,0:T(8,128)(2,1)S(1)} %shard_map.215.refs_4_), channel_id=1, source_target_pairs={{0,1},{1,0},{2,3},{3,2},{4,5},{5,4},{6,7},{7,6},{8,9},{9,8},{10,11... | collective-permute-start | bytes 122888 | tf_op jit(solution)/shard_map/ppermute | solution.py:841

commit v5 on v4

--- a/solution.py
+++ b/solution.py
@@ -85,11 +85,12 @@
         column = jnp.sum(jnp.where(diagonal, vector[...], 0.0), axis=1, keepdims=True)
         tail = jnp.where(lane == k, column, tail)
     pack[:, 2 * LANES :] = tail
-    piece[0:own] = weight[...].astype(BF16)
-    segment = lax.broadcasted_iota(jnp.int32, (1, wide), 1) // bias.shape[1]
-    repeated = jnp.concatenate([bias[...]] * (wide // bias.shape[1]), axis=1)
-    row = jnp.where(segment == lax.axis_index("shard"), repeated, 0.0)
-    piece[own:] = jnp.broadcast_to(row, (piece.shape[0] - own, wide)).astype(BF16)
+    segment = bias.shape[1]
+    flat = LANES * lax.broadcasted_iota(jnp.int32, (own, LANES), 0) + lane
+    repeated = jnp.concatenate([bias[...]] * (LANES // segment), axis=1)
+    piece[:, 0:wide] = weight[...].astype(BF16)
+    here = flat // segment == lax.axis_index("shard")
+    piece[:, wide:] = jnp.where(here, repeated, 0.0).astype(BF16)
 
 
 def copying(source, target, sem):
@@ -204,7 +205,7 @@
         return 0
 
     count = chans // step
-    lax.fori_loop(0, count, block, 0, unroll=min(4, count))
+    lax.fori_loop(0, count, block, 0, unroll=min(8, count))
     for at in range(count):
         here = pl.ds(at * step, step)
         pltpu.make_async_copy(table.at[here], far_table.at[here], sems.at[at]).wait()
@@ -343,13 +344,14 @@
     own = width // plan.shards
     shard = lax.axis_index("shard")
     layer, core = shard // 2, lax.rem(shard, 2)
-    bias = jnp.zeros((1, 2 * width), F32)
+    bias = jnp.zeros((16, LANES), F32)
     for side in range(2):
         for turn in range(layers):
             piece = pieces[side * layers + turn]
             home = 2 * lax.rem(layer + layers - turn, layers) + lax.rem(core + side, 2)
-            w[pl.ds(pl.multiple_of(home * own, own), own), :] = piece[0:own]
-            bias += piece[own : own + 1].astype(F32)
+            w[pl.ds(pl.multiple_of(home * own, own), own), :] = piece[:, 0 : 2 * width]
+            bias += piece[0:16, 2 * width :].astype(F32)
+    bias = jnp.concatenate([bias[k : k + 1] for k in range(2 * width // LANES)], axis=1)
     position = lax.broadcasted_iota(jnp.int32, (rows, width), 0)
     hidden = arrived[...].reshape(width, seqs * rows).astype(F32).T.astype(BF16)
     for n in range(seqs):
@@ -373,14 +375,16 @@
     core = lax.rem(lax.axis_index("shard"), 2)
     outer = outers[...]
     bias = jnp.sum(outer.astype(F32), axis=0, keepdims=True)
-    tail = jnp.broadcast_to(bias, (kept.shape[1] - own, wide)).astype(BF16)
+    tail = [bias[:, k * LANES : (k + 1) * LANES] for k in range(wide // LANES)]
+    tail.append(jnp.zeros((own - len(tail), LANES), F32))
+    tail = jnp.concatenate(tail, axis=0).astype(BF16)
     for side, out in enumerate((sent, kept)):
         which = lax.rem(core + 1 - side, 2)
         members = [(2 * z + which) * subs + sub for z in range(layers) for sub in range(subs)]
         left = jnp.concatenate([arrived[member] for member in members], axis=0)
-        out[:, 0:own] = dot(left, outer, (1, 0)).astype(BF16).reshape(layers, own, wide)
+        out[:, :, 0:wide] = dot(left, outer, (1, 0)).astype(BF16).reshape(layers, own, wide)
         for z in range(layers):
-            out[z, own:] = tail
+            out[z, :, wide:] = tail
 
 
 def backward_kernel(
@@ -631,13 +635,13 @@
     slab = slots[0].astype(F32)
     for k in range(1, chunks):
         slab += slots[k].astype(F32)
-    grad_weight[...] = slab[0:own]
-    line = slab[own : own + 1]
+    grad_weight[...] = slab[:, 0:wide]
     segment = grad_bias.shape[1]
     shard = lax.axis_index("shard")
     row = jnp.zeros((1, segment), F32)
     for s in range(wide // segment):
-        row = jnp.where(shard == s, line[:, s * segment : (s + 1) * segment], row)
+        at, off = divmod(s * segment, LANES)
+        row = jnp.where(shard == s, slab[at : at + 1, wide + off : wide + off + segment], row)
     grad_bias[...] = row
     chans = own // subs
     each = chans + 16
@@ -708,7 +712,7 @@
     pack, scale, piece = call(
         pack_kernel,
         2,
-        [((own, 3 * LANES), F32), ((own, states), F32), ((own + 16, 2 * width), BF16)],
+        [((own, 3 * LANES), F32), ((own, states), F32), ((own, 2 * width + LANES), BF16)],
         [VMEM] * 9,
     )(
         *in_hbm(
@@ -778,13 +782,13 @@
         [here((width, 2 * width))],
     )(lengths, hidden, *in_hbm(tokens, cotangent), *near, *across)
     back = exchange(back)
-    half = ((plan.layers, own + 16, 2 * width), BF16)
+    half = ((plan.layers, own, 2 * width + LANES), BF16)
     kept, sent = call(functools.partial(outer_kernel, plan), 2, [half, half], [VMEM] * 2)(
         hidden, outers
     )
 
     came = lax.ppermute(sent, "shard", plan.across)
-    slab = ((own + 16, 2 * width), BF16)
+    slab = ((own, 2 * width + LANES), BF16)
     shares = call(
         functools.partial(share_kernel, plan.layers), COST[6], [slab] * plan.layers, [VMEM] * 2
     )(kept, came)
@@ -811,7 +815,7 @@
         + [tables[0], here(*by_channel[:2]), here(*prefix_type[:2]), here(*by_channel[:2])]
         + [sems(4, chans // 8)],
     )(far_tables[0], *in_hbm(mirrored, prefix, local_grads), firsts, tallies)
-    leaving, wholes = lax.optimization_barrier((exchange(leaving), wholes))
+    leaving = exchange(leaving)
     (tokens_grad,) = call(
         final_kernel,
         COST[5],

time: 95 us -> 93.3 us (0.982)
  waiting for transfers between devices: 14.3 us -> 8.07 us
  starting transfers between devices: 40.6 us -> 46.4 us
    ppermute x3, waiting for transfers between devices: 5.06 us -> 0.02 us  [per_device(): lax.ppermute(owned, 'ctx', route)]
    ppermute x3, starting transfers between devices: 4.01 us -> 7.55 us  [per_device(): lax.ppermute(owned, 'ctx', route)]
    ppermute x1, starting transfers between devices: 1.38 us -> 2.91 us  [per_device(): lax.ppermute(part, 'ctx', plan.beside)]
    ppermute x2, starting transfers between devices: 1.62 us -> 2.63 us  [per_device(): parts = [lax.ppermute(sums, BOTH, route) for route in plan.give]]
  transfers between devices with their start and end apart: 23 -> 23, of which waited for: 6 -> 4; matrix products, arithmetic and copies ran while one was open for 0% -> 0% of each run, Pallas kernels for 35% -> 35%
where the time goes in v5:
time: 93.3 us; the launch traced here: 92.6 us
  starting transfers between devices  46.4 us (50%)
  Pallas kernels  37.2 us (40%)
  waiting for transfers between devices  8.07 us (9%)
    all_to_all x4, starting transfers between devices, exchange(): lax.all_to_all(buffer, BOTH, 0, 0, axis_index_groups=plan.groups, tiled=T...  20.7 us
    ppermute x3, starting transfers between devices, per_device(): lax.ppermute(owned, 'ctx', route)  7.55 us
    pallas_call x1, Pallas kernels, per_device(): call(functools.partial(backward_kernel, chunks, rows, plan.order), COST[4...  7.13 us
    pallas_call x1, Pallas kernels, per_device(): call(functools.partial(forward_kernel, chunks, rows, plan.order), COST[2]...  6.49 us
    ppermute x3, starting transfers between devices, per_device(): lax.ppermute(v, 'shard', route)  5.66 us
    all_to_all x4, waiting for transfers between devices, exchange(): lax.all_to_all(buffer, BOTH, 0, 0, axis_index_groups=plan.groups, tiled=T...  5 us
    pallas_call x1, Pallas kernels, per_device(): call(functools.partial(prefix_kernel, chunks, rows, plan.order), 6, [by_c...  4.75 us
    ppermute x3, starting transfers between devices, per_device(): lax.ppermute(piece, 'shard', route)  4.72 us
  transfers between devices with their start and end apart: 23, of which 4 were waited for; matrix products, arithmetic and copies ran while one was open for 0% of the time, Pallas kernels for 35%

profile of v5, /device:TPU:0, one launch (start us, length us, event | category | flops | bytes accessed | tf_op | source)
XLA Modules:
  0.0 92.6 jit_solution(12059527689687928662)
XLA Ops:
  0.6 0.5 collective-permute-start
  1.2 1.2 %shard_map.204 = (f32[64,384]{1,0:T(8,128)S(1)}, f32[64,64]{1,0:T(8,128)S(1)}, bf16[64,1152]{1,0:T(8,128)(2,1)S(1)}) custom-call(f32[64,64]{1,0:T(8,128)} %refs_6_.1, f32[64,64]{1,0:T(8,128)} %freq.1, f32[64,64]{1,0:T(8,128)} %refs_8_.1, f32[64,64]{1,0:T(8,128)} %refs_9_.1, f32[1,64]{1,0:T(1,128)} %bitcast.8, f32[1,64]{1,0:T(1,128)} %bitcast.9, ...), custom_call_target="tpu_custom_call" | custom-call | flops 2000000000 | bytes 7000000 | tf_op jit(solution)/shard_map/pallas_call | solution.py:712
  2.4 0.7 collective-permute-start.1
  3.1 0.0 copy-done.1
  3.1 1.1 %shard_map.203 = bf16[8,64,384]{2,1,0:T(8,128)(2,1)} custom-call(bf16[4,96,512]{2,1,0:T(8,128)(2,1)S(1)} %copy-done.1), custom_call_target="tpu_custom_call" | custom-call | flops 2000000000 | bytes 7000000 | tf_op jit(solution)/shard_map/pallas_call | solution.py:737
  4.2 9.5 %all-to-all-start = ((bf16[8,64,384]{2,1,0:T(8,128)(2,1)}), bf16[8,64,384]{2,1,0:T(8,128)(2,1)S(1)}, u32[]{:S(2)}, u32[]{:S(2)}) async-start(bf16[8,64,384]{2,1,0:T(8,128)(2,1)} %shard_map.203), calls=%async_computation | async-start | bytes 786432 | tf_op jit(solution)/shard_map/all_to_all | solution.py:709
  13.7 0.0 collective-permute-done.1.pack
  13.7 0.0 copy-start
  13.7 4.2 %collective-permute-start.4 = (bf16[64,1152]{1,0:T(8,128)(2,1)S(1)}, bf16[64,1152]{1,0:T(8,128)(2,1)S(1)}, u32[]{:S(2)}, u32[]{:S(2)}) collective-permute-start(bf16[64,1152]{1,0:T(8,128)(2,1)S(1)} %get-tuple-element.67.refs_0_), channel_id=1, source_target_pairs={{0,24},{4,28},{8,0},{12,4},{16,8},{20,12},{24,16},{28,20},{1,25},{... | collective-permute-start | bytes 442376 | tf_op jit(solution)/shard_map/ppermute | solution.py:742
  17.9 0.0 collective-permute-start.3
  17.9 0.6 collective-permute-start.2
  18.5 4.0 %shard_map.205 = (bf16[64,128,128]{2,1,0:T(8,128)(2,1)}, f32[64,8,128]{2,1,0:T(8,128)}, f32[2,64,128]{2,1,0:T(8,128)S(1)}) custom-call(f32[64,384]{1,0:T(8,128)S(1)} %collective-permute-done.1.pack), custom_call_target="tpu_custom_call" | custom-call | flops 8000000000 | bytes 28000000 | tf_op jit(solution)/shard_map/pallas_call | solution.py:745
  22.4 0.0 collective-permute-done.partner
  22.5 0.0 all-to-all-done.arrived.first
  22.5 0.0 copy-done
  22.5 6.5 %shard_map.206 = (bf16[8,64,384]{2,1,0:T(8,128)(2,1)}, bf16[2048,128]{1,0:T(8,128)(2,1)}) custom-call(s32[4]{0:T(128)S(1)} %copy-done, s32[4]{0:T(128)S(1)} %collective-permute-done.partner, bf16[8,64,384]{2,1,0:T(8,128)(2,1)S(1)} %all-to-all-done.arrived.first, f32[64,384]{1,0:T(8,128)S(1)} %collective-permute-done.1.pack, ...), custom_call_target="tpu_custom_call" | custom-call | flops 10000000000 | bytes 35000000 | tf_op jit(solution)/shard_map/pallas_call | solution.py:757
  29.0 0.0 collective-permute-done.4.refs_3_
  29.0 1.0 %collective-permute-done.3.refs_2_ = bf16[64,1152]{1,0:T(8,128)(2,1)S(1)} collective-permute-done((bf16[64,1152]{1,0:T(8,128)(2,1)S(1)}, bf16[64,1152]{1,0:T(8,128)(2,1)S(1)}, u32[]{:S(2)}, u32[]{:S(2)}) %collective-permute-start.3) | collective-permute-done | bytes 147488 | tf_op jit(solution)/shard_map/ppermute | solution.py:742
  30.0 0.0 collective-permute-done.2.refs_1_
  30.0 4.3 %all-to-all-start.1 = ((bf16[8,64,384]{2,1,0:T(8,128)(2,1)}), bf16[8,64,384]{2,1,0:T(8,128)(2,1)S(1)}, u32[]{:S(2)}, u32[]{:S(2)}) async-start(bf16[8,64,384]{2,1,0:T(8,128)(2,1)} %get-tuple-element.63), calls=%async_computation.1 | async-start | bytes 786432 | tf_op jit(solution)/shard_map/all_to_all | solution.py:709
  34.3 0.5 collective-permute-start.5
  34.8 0.0 collective-permute-start.6
  34.8 0.5 collective-permute-start.7
  35.3 0.0 collective-permute-start.8
  35.3 4.7 %shard_map.207 = (bf16[64,32,128]{2,1,0:T(8,128)(2,1)}, bf16[64,48,128]{2,1,0:T(8,128)(2,1)}) custom-call(s32[4]{0:T(128)S(1)} %copy-done, s32[4]{0:T(128)S(1)} %collective-permute-done.partner, bf16[8,64,384]{2,1,0:T(8,128)(2,1)S(1)} %all-to-all-done.arrived.first, f32[64,384]{1,0:T(8,128)S(1)} %collective-permute-done.1.pack, ...), custom_call_target="tpu_custom_call" | custom-call | flops 6000000000 | bytes 21000000 | tf_op jit(solution)/shard_map/pallas_call | solution.py:766
  40.1 2.6 %all-to-all-done.1.arrived = bf16[8,64,384]{2,1,0:T(8,128)(2,1)S(1)} async-done(((bf16[8,64,384]{2,1,0:T(8,128)(2,1)}), bf16[8,64,384]{2,1,0:T(8,128)(2,1)S(1)}, u32[]{:S(2)}, u32[]{:S(2)}) %all-to-all-start.1) | async-done | bytes 393248 | tf_op jit(solution)/shard_map/all_to_all | solution.py:709
  42.6 0.0 collective-permute-done.5.refs_4_
  42.6 0.0 collective-permute-done.6.refs_5_
  42.6 0.0 collective-permute-done.7.refs_6_
  42.6 0.0 collective-permute-done.8.refs_7_
  42.6 3.5 %shard_map.208 = (bf16[4,96,512]{2,1,0:T(8,128)(2,1)}, bf16[8,64,384]{2,1,0:T(8,128)(2,1)}, bf16[384,1024]{1,0:T(8,128)(2,1)S(1)}) custom-call(s32[4]{0:T(128)S(1)} %copy-done, bf16[8,64,384]{2,1,0:T(8,128)(2,1)S(1)} %all-to-all-done.1.arrived, bf16[4,96,512]{2,1,0:T(8,128)(2,1)} %tokens.5, bf16[4,96,512]{2,1,0:T(8,128)(2,1)} %cotangent.3, ...), custom_call_target="tpu_custom_call" | custom-call | flops 6000000000 | bytes 21000000 | tf_op jit(solution)/shard_map/pallas_call | solution.py:777
  46.2 0.7 shard_map.211
  46.9 0.1 collective-permute-start.9
  47.0 3.5 %all-to-all-start.2 = ((bf16[8,64,384]{2,1,0:T(8,128)(2,1)}), bf16[8,64,384]{2,1,0:T(8,128)(2,1)S(1)}, u32[]{:S(2)}, u32[]{:S(2)}) async-start(bf16[8,64,384]{2,1,0:T(8,128)(2,1)} %get-tuple-element.72), calls=%async_computation.2 | async-start | bytes 786432 | tf_op jit(solution)/shard_map/all_to_all | solution.py:709
  50.5 0.0 collective-permute-done.9.came
  50.5 0.2 shard_map.212
  50.6 1.9 %collective-permute-start.10 = (bf16[64,1152]{1,0:T(8,128)(2,1)S(1)}, bf16[64,1152]{1,0:T(8,128)(2,1)S(1)}, u32[]{:S(2)}, u32[]{:S(2)}) collective-permute-start(bf16[64,1152]{1,0:T(8,128)(2,1)S(1)} %get-tuple-element.84), channel_id=1, source_target_pairs={{0,8},{4,12},{8,16},{12,20},{16,24},{20,28},{24,0},{28,4},{1,9},{5... | collective-permute-start | bytes 442376 | tf_op jit(solution)/shard_map/ppermute | solution.py:795
  52.5 0.9 collective-permute-start.11
  53.5 2.8 %collective-permute-start.12 = (bf16[64,1152]{1,0:T(8,128)(2,1)S(1)}, bf16[64,1152]{1,0:T(8,128)(2,1)S(1)}, u32[]{:S(2)}, u32[]{:S(2)}) collective-permute-start(bf16[64,1152]{1,0:T(8,128)(2,1)S(1)} %get-tuple-element.86), channel_id=1, source_target_pairs={{0,24},{4,28},{8,0},{12,4},{16,8},{20,12},{24,16},{28,20},{1,25},{... | collective-permute-start | bytes 442376 | tf_op jit(solution)/shard_map/ppermute | solution.py:795
  56.3 2.4 %all-to-all-done.2.arrived = bf16[8,64,384]{2,1,0:T(8,128)(2,1)S(1)} async-done(((bf16[8,64,384]{2,1,0:T(8,128)(2,1)}), bf16[8,64,384]{2,1,0:T(8,128)(2,1)S(1)}, u32[]{:S(2)}, u32[]{:S(2)}) %all-to-all-start.2) | async-done | bytes 393248 | tf_op jit(solution)/shard_map/all_to_all | solution.py:709
  58.7 7.1 %shard_map.209 = (bf16[8,64,384]{2,1,0:T(8,128)(2,1)}, bf16[64,32,128]{2,1,0:T(8,128)(2,1)}, f32[2,64,128]{2,1,0:T(8,128)S(1)}) custom-call(s32[4]{0:T(128)S(1)} %copy-done, s32[4]{0:T(128)S(1)} %collective-permute-done.partner, bf16[8,64,384]{2,1,0:T(8,128)(2,1)S(1)} %all-to-all-done.2.arrived, bf16[8,64,384]{2,1,0:T(8,128)(2,1)S(1)} %all-to-all-done.arrived.first, ...), custom_call_target="tpu_custom_call" | custom-call | flops 1000000000 | bytes 3500000 | tf_op jit(solution)/shard_map/pallas_call | solution.py:796
  65.9 3.5 %all-to-all-start.3 = ((bf16[8,64,384]{2,1,0:T(8,128)(2,1)}), bf16[8,64,384]{2,1,0:T(8,128)(2,1)S(1)}, u32[]{:S(2)}, u32[]{:S(2)}) async-start(bf16[8,64,384]{2,1,0:T(8,128)(2,1)} %get-tuple-element.74), calls=%async_computation.3 | async-start | bytes 786432 | tf_op jit(solution)/shard_map/all_to_all | solution.py:709
  69.3 0.0 collective-permute-done.10.refs_1_
  69.4 0.0 collective-permute-done.11.refs_2_
  69.4 0.0 collective-permute-done.12.refs_3_
  69.4 0.1 shard_map.213.refs_0_
  69.5 4.5 %shard_map.214 = bf16[80,256]{1,0:T(8,128)(2,1)S(1)} custom-call(bf16[64,128,128]{2,1,0:T(8,128)(2,1)} %get-tuple-element.59.far_table, bf16[64,32,128]{2,1,0:T(8,128)(2,1)} %get-tuple-element.75.far_mirrored, bf16[64,48,128]{2,1,0:T(8,128)(2,1)} %get-tuple-element.76.far_prefix, bf16[64,32,128]{2,1,0:T(8,128)(2,1)} %get-tuple-element.77.far_grads, ...), custom_call_target="tpu_custom_call" | custom-call | flops 8000000000 | bytes 28000000 | tf_op jit(solution)/shard_map/pallas_call | solution.py:809
  73.9 2.0 %collective-permute-start.14 = (bf16[80,256]{1,0:T(8,128)(2,1)S(1)}, bf16[80,256]{1,0:T(8,128)(2,1)S(1)}, u32[]{:S(2)}, u32[]{:S(2)}) collective-permute-start(bf16[80,256]{1,0:T(8,128)(2,1)S(1)} %shard_map.214), channel_id=1, source_target_pairs={{0,2},{4,6},{1,10},{5,14},{2,18},{6,22},{3,26},{7,30},{8,3},{12,7}... | collective-permute-start | bytes 122888 | tf_op jit(solution)/shard_map/ppermute | solution.py:828
  75.9 0.7 collective-permute-start.13
  76.6 6.9 %collective-permute-start.17 = (bf16[64,1152]{1,0:T(8,128)(2,1)S(1)}, bf16[64,1152]{1,0:T(8,128)(2,1)S(1)}, u32[]{:S(2)}, u32[]{:S(2)}) collective-permute-start(bf16[64,1152]{1,0:T(8,128)(2,1)S(1)} %shard_map.213.refs_0_), channel_id=1, source_target_pairs={{0,3},{1,0},{2,1},{3,2},{4,7},{5,4},{6,5},{7,6},{8,11},{9,8},{10,9... | collective-permute-start | bytes 442376 | tf_op jit(solution)/shard_map/ppermute | solution.py:806
  83.5 0.0 collective-permute-start.16
  83.5 0.6 collective-permute-start.15
  84.1 0.0 all-to-all-done.3.arrived
  84.1 2.6 %shard_map.210 = bf16[4,96,512]{2,1,0:T(8,128)(2,1)} custom-call(bf16[8,64,384]{2,1,0:T(8,128)(2,1)S(1)} %all-to-all-done.3.arrived, bf16[4,96,512]{2,1,0:T(8,128)(2,1)} %tokens.5, bf16[4,96,512]{2,1,0:T(8,128)(2,1)} %cotangent.3), custom_call_target="tpu_custom_call" | custom-call | flops 3000000000 | bytes 10500000 | tf_op jit(solution)/shard_map/pallas_call | solution.py:819
  86.7 0.0 collective-permute-done.14.refs_1_
  86.7 0.0 collective-permute-done.13.refs_0_
  86.8 2.9 %collective-permute-start.18 = (bf16[80,256]{1,0:T(8,128)(2,1)S(1)}, bf16[80,256]{1,0:T(8,128)(2,1)S(1)}, u32[]{:S(2)}, u32[]{:S(2)}) collective-permute-start(bf16[80,256]{1,0:T(8,128)(2,1)S(1)} %shard_map.215.refs_4_), channel_id=1, source_target_pairs={{0,1},{1,0},{2,3},{3,2},{4,5},{5,4},{6,7},{7,6},{8,9},{9,8},{10,11... | collective-permute-start | bytes 122888 | tf_op jit(solution)/shard_map/ppermute | solution.py:845
  89.7 2.0 %collective-permute-done.18.refs_5_ = bf16[80,256]{1,0:T(8,128)(2,1)S(1)} collective-permute-done((bf16[80,256]{1,0:T(8,128)(2,1)S(1)}, bf16[80,256]{1,0:T(8,128)(2,1)S(1)}, u32[]{:S(2)}, u32[]{:S(2)}) %collective-permute-start.18) | collective-permute-done | bytes 40992 | tf_op jit(solution)/shard_map/ppermute | solution.py:845
  91.7 0.0 collective-permute-done.17.refs_3_
  91.7 0.0 collective-permute-done.16.refs_2_
  91.7 0.0 collective-permute-done.15.refs_1_
  91.7 0.0 copy-done.2
  91.7 0.0 copy-done.3
  91.7 0.9 shard_map.216
  (6 shorter events, 0.0 us)
Async XLA Ops:
  0.6 21.8 %collective-permute-start = (s32[4]{0:T(128)}, s32[4]{0:T(128)S(1)}, u32[]{:S(2)}, u32[]{:S(2)}) collective-permute-start(s32[4]{0:T(128)} %lengths.7), channel_id=1, source_target_pairs={{0,4},{4,0},{8,12},{12,8},{16,20},{20,16},{24,28},{28,24},{1,5},{5... | collective-permute-start | bytes 56 | tf_op jit(solution)/shard_map/ppermute | solution.py:734
  1.2 1.9 %copy-start.1 = (bf16[4,96,512]{2,1,0:T(8,128)(2,1)S(1)}, bf16[4,96,512]{2,1,0:T(8,128)(2,1)}, u32[]{:S(2)}) copy-start(bf16[4,96,512]{2,1,0:T(8,128)(2,1)} %tokens.5) | copy-start | bytes 1179652
  2.4 11.3 %collective-permute-start.1 = (f32[64,384]{1,0:T(8,128)S(1)}, f32[64,384]{1,0:T(8,128)S(1)}, u32[]{:S(2)}, u32[]{:S(2)}) collective-permute-start(f32[64,384]{1,0:T(8,128)S(1)} %get-tuple-element.57), channel_id=1, source_target_pairs={{0,0},{4,4},{8,1},{12,5},{16,2},{20,6},{24,3},{28,7},{1,8},{5,12},... | collective-permute-start | bytes 294920 | tf_op jit(solution)/shard_map/ppermute | solution.py:725
  4.2 18.2 %all-to-all-start = ((bf16[8,64,384]{2,1,0:T(8,128)(2,1)}), bf16[8,64,384]{2,1,0:T(8,128)(2,1)S(1)}, u32[]{:S(2)}, u32[]{:S(2)}) async-start(bf16[8,64,384]{2,1,0:T(8,128)(2,1)} %shard_map.203), calls=%async_computation | async-start | bytes 786432 | tf_op jit(solution)/shard_map/all_to_all | solution.py:709
  13.7 8.7 %copy-start = (s32[4]{0:T(128)S(1)}, s32[4]{0:T(128)}, u32[]{:S(2)}) copy-start(s32[4]{0:T(128)} %lengths.7) | copy-start | bytes 52
  13.7 15.2 %collective-permute-start.4 = (bf16[64,1152]{1,0:T(8,128)(2,1)S(1)}, bf16[64,1152]{1,0:T(8,128)(2,1)S(1)}, u32[]{:S(2)}, u32[]{:S(2)}) collective-permute-start(bf16[64,1152]{1,0:T(8,128)(2,1)S(1)} %get-tuple-element.67.refs_0_), channel_id=1, source_target_pairs={{0,24},{4,28},{8,0},{12,4},{16,8},{20,12},{24,16},{28,20},{1,25},{... | collective-permute-start | bytes 442376 | tf_op jit(solution)/shard_map/ppermute | solution.py:742
  17.9 12.1 %collective-permute-start.3 = (bf16[64,1152]{1,0:T(8,128)(2,1)S(1)}, bf16[64,1152]{1,0:T(8,128)(2,1)S(1)}, u32[]{:S(2)}, u32[]{:S(2)}) collective-permute-start(bf16[64,1152]{1,0:T(8,128)(2,1)S(1)} %get-tuple-element.67.refs_0_), channel_id=1, source_target_pairs={{0,16},{4,20},{8,24},{12,28},{16,0},{20,4},{24,8},{28,12},{1,17},{... | collective-permute-start | bytes 442376 | tf_op jit(solution)/shard_map/ppermute | solution.py:742
  17.9 12.1 %collective-permute-start.2 = (bf16[64,1152]{1,0:T(8,128)(2,1)S(1)}, bf16[64,1152]{1,0:T(8,128)(2,1)S(1)}, u32[]{:S(2)}, u32[]{:S(2)}) collective-permute-start(bf16[64,1152]{1,0:T(8,128)(2,1)S(1)} %get-tuple-element.67.refs_0_), channel_id=1, source_target_pairs={{0,8},{4,12},{8,16},{12,20},{16,24},{20,28},{24,0},{28,4},{1,9},{5... | collective-permute-start | bytes 442376 | tf_op jit(solution)/shard_map/ppermute | solution.py:742
  30.0 12.6 %all-to-all-start.1 = ((bf16[8,64,384]{2,1,0:T(8,128)(2,1)}), bf16[8,64,384]{2,1,0:T(8,128)(2,1)S(1)}, u32[]{:S(2)}, u32[]{:S(2)}) async-start(bf16[8,64,384]{2,1,0:T(8,128)(2,1)} %get-tuple-element.63), calls=%async_computation.1 | async-start | bytes 786432 | tf_op jit(solution)/shard_map/all_to_all | solution.py:709
  34.3 8.3 %collective-permute-start.5 = (bf16[64,1152]{1,0:T(8,128)(2,1)S(1)}, bf16[64,1152]{1,0:T(8,128)(2,1)S(1)}, u32[]{:S(2)}, u32[]{:S(2)}) collective-permute-start(bf16[64,1152]{1,0:T(8,128)(2,1)S(1)} %get-tuple-element.67.refs_0_), channel_id=1, source_target_pairs={{0,4},{4,0},{8,12},{12,8},{16,20},{20,16},{24,28},{28,24},{1,5},{5... | collective-permute-start | bytes 442376 | tf_op jit(solution)/shard_map/ppermute | solution.py:774
  34.8 7.8 %collective-permute-start.6 = (bf16[64,1152]{1,0:T(8,128)(2,1)S(1)}, bf16[64,1152]{1,0:T(8,128)(2,1)S(1)}, u32[]{:S(2)}, u32[]{:S(2)}) collective-permute-start(bf16[64,1152]{1,0:T(8,128)(2,1)S(1)} %collective-permute-done.2.refs_1_), channel_id=1, source_target_pairs={{0,4},{4,0},{8,12},{12,8},{16,20},{20,16},{24,28},{28,24},{1,5},{5... | collective-permute-start | bytes 442376 | tf_op jit(solution)/shard_map/ppermute | solution.py:774
  34.8 7.8 %collective-permute-start.7 = (bf16[64,1152]{1,0:T(8,128)(2,1)S(1)}, bf16[64,1152]{1,0:T(8,128)(2,1)S(1)}, u32[]{:S(2)}, u32[]{:S(2)}) collective-permute-start(bf16[64,1152]{1,0:T(8,128)(2,1)S(1)} %collective-permute-done.3.refs_2_), channel_id=1, source_target_pairs={{0,4},{4,0},{8,12},{12,8},{16,20},{20,16},{24,28},{28,24},{1,5},{5... | collective-permute-start | bytes 442376 | tf_op jit(solution)/shard_map/ppermute | solution.py:774
  35.3 7.3 %collective-permute-start.8 = (bf16[64,1152]{1,0:T(8,128)(2,1)S(1)}, bf16[64,1152]{1,0:T(8,128)(2,1)S(1)}, u32[]{:S(2)}, u32[]{:S(2)}) collective-permute-start(bf16[64,1152]{1,0:T(8,128)(2,1)S(1)} %collective-permute-done.4.refs_3_), channel_id=1, source_target_pairs={{0,4},{4,0},{8,12},{12,8},{16,20},{20,16},{24,28},{28,24},{1,5},{5... | collective-permute-start | bytes 442376 | tf_op jit(solution)/shard_map/ppermute | solution.py:774
  46.9 3.6 %collective-permute-start.9 = (bf16[4,64,1152]{2,1,0:T(8,128)(2,1)S(1)}, bf16[4,64,1152]{2,1,0:T(8,128)(2,1)S(1)}, u32[]{:S(2)}, u32[]{:S(2)}) collective-permute-start(bf16[4,64,1152]{2,1,0:T(8,128)(2,1)S(1)} %get-tuple-element.82), channel_id=1, source_target_pairs={{0,4},{4,0},{8,12},{12,8},{16,20},{20,16},{24,28},{28,24},{1,5},{5... | collective-permute-start | bytes 1769480 | tf_op jit(solution)/shard_map/ppermute | solution.py:790
  47.0 11.7 %all-to-all-start.2 = ((bf16[8,64,384]{2,1,0:T(8,128)(2,1)}), bf16[8,64,384]{2,1,0:T(8,128)(2,1)S(1)}, u32[]{:S(2)}, u32[]{:S(2)}) async-start(bf16[8,64,384]{2,1,0:T(8,128)(2,1)} %get-tuple-element.72), calls=%async_computation.2 | async-start | bytes 786432 | tf_op jit(solution)/shard_map/all_to_all | solution.py:709
  50.6 18.7 %collective-permute-start.10 = (bf16[64,1152]{1,0:T(8,128)(2,1)S(1)}, bf16[64,1152]{1,0:T(8,128)(2,1)S(1)}, u32[]{:S(2)}, u32[]{:S(2)}) collective-permute-start(bf16[64,1152]{1,0:T(8,128)(2,1)S(1)} %get-tuple-element.84), channel_id=1, source_target_pairs={{0,8},{4,12},{8,16},{12,20},{16,24},{20,28},{24,0},{28,4},{1,9},{5... | collective-permute-start | bytes 442376 | tf_op jit(solution)/shard_map/ppermute | solution.py:795
  52.5 16.8 %collective-permute-start.11 = (bf16[64,1152]{1,0:T(8,128)(2,1)S(1)}, bf16[64,1152]{1,0:T(8,128)(2,1)S(1)}, u32[]{:S(2)}, u32[]{:S(2)}) collective-permute-start(bf16[64,1152]{1,0:T(8,128)(2,1)S(1)} %get-tuple-element.85), channel_id=1, source_target_pairs={{0,16},{4,20},{8,24},{12,28},{16,0},{20,4},{24,8},{28,12},{1,17},{... | collective-permute-start | bytes 442376 | tf_op jit(solution)/shard_map/ppermute | solution.py:795
  53.5 15.9 %collective-permute-start.12 = (bf16[64,1152]{1,0:T(8,128)(2,1)S(1)}, bf16[64,1152]{1,0:T(8,128)(2,1)S(1)}, u32[]{:S(2)}, u32[]{:S(2)}) collective-permute-start(bf16[64,1152]{1,0:T(8,128)(2,1)S(1)} %get-tuple-element.86), channel_id=1, source_target_pairs={{0,24},{4,28},{8,0},{12,4},{16,8},{20,12},{24,16},{28,20},{1,25},{... | collective-permute-start | bytes 442376 | tf_op jit(solution)/shard_map/ppermute | solution.py:795
  65.9 18.2 %all-to-all-start.3 = ((bf16[8,64,384]{2,1,0:T(8,128)(2,1)}), bf16[8,64,384]{2,1,0:T(8,128)(2,1)S(1)}, u32[]{:S(2)}, u32[]{:S(2)}) async-start(bf16[8,64,384]{2,1,0:T(8,128)(2,1)} %get-tuple-element.74), calls=%async_computation.3 | async-start | bytes 786432 | tf_op jit(solution)/shard_map/all_to_all | solution.py:709
  73.9 12.8 %collective-permute-start.14 = (bf16[80,256]{1,0:T(8,128)(2,1)S(1)}, bf16[80,256]{1,0:T(8,128)(2,1)S(1)}, u32[]{:S(2)}, u32[]{:S(2)}) collective-permute-start(bf16[80,256]{1,0:T(8,128)(2,1)S(1)} %shard_map.214), channel_id=1, source_target_pairs={{0,2},{4,6},{1,10},{5,14},{2,18},{6,22},{3,26},{7,30},{8,3},{12,7}... | collective-permute-start | bytes 122888 | tf_op jit(solution)/shard_map/ppermute | solution.py:828
  75.9 10.8 %collective-permute-start.13 = (bf16[80,256]{1,0:T(8,128)(2,1)S(1)}, bf16[80,256]{1,0:T(8,128)(2,1)S(1)}, u32[]{:S(2)}, u32[]{:S(2)}) collective-permute-start(bf16[80,256]{1,0:T(8,128)(2,1)S(1)} %shard_map.214), channel_id=1, source_target_pairs={{0,0},{4,4},{1,8},{5,12},{2,16},{6,20},{3,24},{7,28},{8,1},{12,5},... | collective-permute-start | bytes 122888 | tf_op jit(solution)/shard_map/ppermute | solution.py:828
  76.6 15.1 %collective-permute-start.17 = (bf16[64,1152]{1,0:T(8,128)(2,1)S(1)}, bf16[64,1152]{1,0:T(8,128)(2,1)S(1)}, u32[]{:S(2)}, u32[]{:S(2)}) collective-permute-start(bf16[64,1152]{1,0:T(8,128)(2,1)S(1)} %shard_map.213.refs_0_), channel_id=1, source_target_pairs={{0,3},{1,0},{2,1},{3,2},{4,7},{5,4},{6,5},{7,6},{8,11},{9,8},{10,9... | collective-permute-start | bytes 442376 | tf_op jit(solution)/shard_map/ppermute | solution.py:806
  83.5 8.2 %collective-permute-start.16 = (bf16[64,1152]{1,0:T(8,128)(2,1)S(1)}, bf16[64,1152]{1,0:T(8,128)(2,1)S(1)}, u32[]{:S(2)}, u32[]{:S(2)}) collective-permute-start(bf16[64,1152]{1,0:T(8,128)(2,1)S(1)} %shard_map.213.refs_0_), channel_id=1, source_target_pairs={{0,2},{1,3},{2,0},{3,1},{4,6},{5,7},{6,4},{7,5},{8,10},{9,11},{10,... | collective-permute-start | bytes 442376 | tf_op jit(solution)/shard_map/ppermute | solution.py:806
  83.5 8.2 %collective-permute-start.15 = (bf16[64,1152]{1,0:T(8,128)(2,1)S(1)}, bf16[64,1152]{1,0:T(8,128)(2,1)S(1)}, u32[]{:S(2)}, u32[]{:S(2)}) collective-permute-start(bf16[64,1152]{1,0:T(8,128)(2,1)S(1)} %shard_map.213.refs_0_), channel_id=1, source_target_pairs={{0,1},{1,2},{2,3},{3,0},{4,5},{5,6},{6,7},{7,4},{8,9},{9,10},{10,1... | collective-permute-start | bytes 442376 | tf_op jit(solution)/shard_map/ppermute | solution.py:806
  86.7 5.0 %copy-start.2 = (f32[64,64]{1,0:T(8,128)S(1)}, f32[64,64]{1,0:T(8,128)}, u32[]{:S(2)}) copy-start(f32[64,64]{1,0:T(8,128)} %refs_6_.1) | copy-start | bytes 49156
  86.7 5.0 %copy-start.3 = (f32[64,64]{1,0:T(8,128)S(1)}, f32[64,64]{1,0:T(8,128)}, u32[]{:S(2)}) copy-start(f32[64,64]{1,0:T(8,128)} %refs_8_.1) | copy-start | bytes 49156
  86.7 5.0 %copy-start.4 = (f32[64,64]{1,0:T(8,128)S(1)}, f32[64,64]{1,0:T(8,128)}, u32[]{:S(2)}) copy-start(f32[64,64]{1,0:T(8,128)} %refs_9_.1) | copy-start | bytes 49156
  86.8 4.9 %collective-permute-start.18 = (bf16[80,256]{1,0:T(8,128)(2,1)S(1)}, bf16[80,256]{1,0:T(8,128)(2,1)S(1)}, u32[]{:S(2)}, u32[]{:S(2)}) collective-permute-start(bf16[80,256]{1,0:T(8,128)(2,1)S(1)} %shard_map.215.refs_4_), channel_id=1, source_target_pairs={{0,1},{1,0},{2,3},{3,2},{4,5},{5,4},{6,7},{7,6},{8,9},{9,8},{10,11... | collective-permute-start | bytes 122888 | tf_op jit(solution)/shard_map/ppermute | solution.py:845

commit v6 on v5

--- a/solution.py
+++ b/solution.py
@@ -41,7 +41,7 @@
             return (2 * z + core) * chunks + c
 
         def owner(z, core, c, turn):
-            place = (z * subs + c % subs + turn) % chunks
+            place = ((layers - 1 - z) * subs + c % subs + turn) % chunks
             return (2 * (c // subs) + core) * chunks + place
 
         self.fetch = [(owner(*m, 0), here(*m)) for m in members]

time: 93.3 us -> 88.6 us (0.950)
  starting transfers between devices: 46.4 us -> 41.3 us
    all_to_all x4, starting transfers between devices: 20.7 us -> 14.2 us  [exchange(): lax.all_to_all(buffer, BOTH, 0, 0, axis_index_groups=plan.groups, tiled=T...]
    ppermute x3, starting transfers between devices: 7.55 us -> 2.62 us  [per_device(): lax.ppermute(owned, 'ctx', route)]
    ppermute x1, starting transfers between devices: 0.67 us -> 4.68 us  [per_device(): pack = lax.ppermute(pack, BOTH, plan.fetch)]
    ppermute x2, starting transfers between devices: 2.63 us -> 5.11 us  [per_device(): parts = [lax.ppermute(sums, BOTH, route) for route in plan.give]]
    ppermute x1, starting transfers between devices: 2.91 us -> 1.51 us  [per_device(): lax.ppermute(part, 'ctx', plan.beside)]
    ppermute x3, starting transfers between devices: 4.72 us -> 5.88 us  [per_device(): lax.ppermute(piece, 'shard', route)]
    ppermute x1, waiting for transfers between devices: 1.98 us -> 3.08 us  [per_device(): lax.ppermute(part, 'ctx', plan.beside)]
  transfers between devices with their start and end apart: 23 -> 23, of which waited for: 4 -> 4; matrix products, arithmetic and copies ran while one was open for 0% -> 0% of each run, Pallas kernels for 35% -> 36%
where the time goes in v6:
time: 88.6 us; the launch traced here: 88 us
  starting transfers between devices  41.3 us (47%)
  Pallas kernels  37.2 us (42%)
  waiting for transfers between devices  8.56 us (10%)
  between operations  0.9 us (1%)
    all_to_all x4, starting transfers between devices, exchange(): lax.all_to_all(buffer, BOTH, 0, 0, axis_index_groups=plan.groups, tiled=T...  14.2 us
    pallas_call x1, Pallas kernels, per_device(): call(functools.partial(backward_kernel, chunks, rows, plan.order), COST[4...  7.13 us
    pallas_call x1, Pallas kernels, per_device(): call(functools.partial(forward_kernel, chunks, rows, plan.order), COST[2]...  6.49 us
    ppermute x3, starting transfers between devices, per_device(): lax.ppermute(piece, 'shard', route)  5.88 us
    ppermute x3, starting transfers between devices, per_device(): lax.ppermute(v, 'shard', route)  5.67 us
    ppermute x2, starting transfers between devices, per_device(): parts = [lax.ppermute(sums, BOTH, route) for route in plan.give]  5.11 us
    all_to_all x4, waiting for transfers between devices, exchange(): lax.all_to_all(buffer, BOTH, 0, 0, axis_index_groups=plan.groups, tiled=T...  4.99 us
    pallas_call x1, Pallas kernels, per_device(): call(functools.partial(prefix_kernel, chunks, rows, plan.order), 6, [by_c...  4.75 us
  transfers between devices with their start and end apart: 23, of which 4 were waited for; matrix products, arithmetic and copies ran while one was open for 0% of the time, Pallas kernels for 36%

profile of v6, /device:TPU:0, one launch (start us, length us, event | category | flops | bytes accessed | tf_op | source)
XLA Modules:
  0.0 88.0 jit_solution(1547835216862383103)
XLA Ops:
  0.6 0.5 collective-permute-start
  1.2 1.2 %shard_map.204 = (f32[64,384]{1,0:T(8,128)S(1)}, f32[64,64]{1,0:T(8,128)S(1)}, bf16[64,1152]{1,0:T(8,128)(2,1)S(1)}) custom-call(f32[64,64]{1,0:T(8,128)} %refs_6_.1, f32[64,64]{1,0:T(8,128)} %freq.1, f32[64,64]{1,0:T(8,128)} %refs_8_.1, f32[64,64]{1,0:T(8,128)} %refs_9_.1, f32[1,64]{1,0:T(1,128)} %bitcast.8, f32[1,64]{1,0:T(1,128)} %bitcast.9, ...), custom_call_target="tpu_custom_call" | custom-call | flops 2000000000 | bytes 7000000 | tf_op jit(solution)/shard_map/pallas_call | solution.py:712
  2.4 4.7 %collective-permute-start.1 = (f32[64,384]{1,0:T(8,128)S(1)}, f32[64,384]{1,0:T(8,128)S(1)}, u32[]{:S(2)}, u32[]{:S(2)}) collective-permute-start(f32[64,384]{1,0:T(8,128)S(1)} %get-tuple-element.57), channel_id=1, source_target_pairs={{3,0},{7,4},{11,1},{15,5},{19,2},{23,6},{27,3},{31,7},{2,8},{6,12}... | collective-permute-start | bytes 294920 | tf_op jit(solution)/shard_map/ppermute | solution.py:725
  7.1 0.0 copy-done.1
  7.1 1.1 %shard_map.203 = bf16[8,64,384]{2,1,0:T(8,128)(2,1)} custom-call(bf16[4,96,512]{2,1,0:T(8,128)(2,1)S(1)} %copy-done.1), custom_call_target="tpu_custom_call" | custom-call | flops 2000000000 | bytes 7000000 | tf_op jit(solution)/shard_map/pallas_call | solution.py:737
  8.2 3.5 %all-to-all-start = ((bf16[8,64,384]{2,1,0:T(8,128)(2,1)}), bf16[8,64,384]{2,1,0:T(8,128)(2,1)S(1)}, u32[]{:S(2)}, u32[]{:S(2)}) async-start(bf16[8,64,384]{2,1,0:T(8,128)(2,1)} %shard_map.203), calls=%async_computation | async-start | bytes 786432 | tf_op jit(solution)/shard_map/all_to_all | solution.py:709
  11.7 0.0 collective-permute-done.1.pack
  11.7 0.0 copy-start
  11.7 2.6 %collective-permute-start.4 = (bf16[64,1152]{1,0:T(8,128)(2,1)S(1)}, bf16[64,1152]{1,0:T(8,128)(2,1)S(1)}, u32[]{:S(2)}, u32[]{:S(2)}) collective-permute-start(bf16[64,1152]{1,0:T(8,128)(2,1)S(1)} %get-tuple-element.67.refs_0_), channel_id=1, source_target_pairs={{0,24},{4,28},{8,0},{12,4},{16,8},{20,12},{24,16},{28,20},{1,25},{... | collective-permute-start | bytes 442376 | tf_op jit(solution)/shard_map/ppermute | solution.py:742
  14.2 1.3 %collective-permute-start.3 = (bf16[64,1152]{1,0:T(8,128)(2,1)S(1)}, bf16[64,1152]{1,0:T(8,128)(2,1)S(1)}, u32[]{:S(2)}, u32[]{:S(2)}) collective-permute-start(bf16[64,1152]{1,0:T(8,128)(2,1)S(1)} %get-tuple-element.67.refs_0_), channel_id=1, source_target_pairs={{0,16},{4,20},{8,24},{12,28},{16,0},{20,4},{24,8},{28,12},{1,17},{... | collective-permute-start | bytes 442376 | tf_op jit(solution)/shard_map/ppermute | solution.py:742
  15.5 2.0 %collective-permute-start.2 = (bf16[64,1152]{1,0:T(8,128)(2,1)S(1)}, bf16[64,1152]{1,0:T(8,128)(2,1)S(1)}, u32[]{:S(2)}, u32[]{:S(2)}) collective-permute-start(bf16[64,1152]{1,0:T(8,128)(2,1)S(1)} %get-tuple-element.67.refs_0_), channel_id=1, source_target_pairs={{0,8},{4,12},{8,16},{12,20},{16,24},{20,28},{24,0},{28,4},{1,9},{5... | collective-permute-start | bytes 442376 | tf_op jit(solution)/shard_map/ppermute | solution.py:742
  17.6 4.0 %shard_map.205 = (bf16[64,128,128]{2,1,0:T(8,128)(2,1)}, f32[64,8,128]{2,1,0:T(8,128)}, f32[2,64,128]{2,1,0:T(8,128)S(1)}) custom-call(f32[64,384]{1,0:T(8,128)S(1)} %collective-permute-done.1.pack), custom_call_target="tpu_custom_call" | custom-call | flops 8000000000 | bytes 28000000 | tf_op jit(solution)/shard_map/pallas_call | solution.py:745
  21.6 0.0 collective-permute-done.partner
  21.6 0.0 all-to-all-done.arrived.first
  21.6 6.5 %shard_map.206 = (bf16[8,64,384]{2,1,0:T(8,128)(2,1)}, bf16[2048,128]{1,0:T(8,128)(2,1)}) custom-call(s32[4]{0:T(128)S(1)} %copy-done, s32[4]{0:T(128)S(1)} %collective-permute-done.partner, bf16[8,64,384]{2,1,0:T(8,128)(2,1)S(1)} %all-to-all-done.arrived.first, f32[64,384]{1,0:T(8,128)S(1)} %collective-permute-done.1.pack, ...), custom_call_target="tpu_custom_call" | custom-call | flops 10000000000 | bytes 35000000 | tf_op jit(solution)/shard_map/pallas_call | solution.py:757
  28.1 0.0 collective-permute-done.4.refs_3_
  28.1 0.4 collective-permute-done.3.refs_2_
  28.5 0.0 collective-permute-done.2.refs_1_
  28.6 3.8 %all-to-all-start.1 = ((bf16[8,64,384]{2,1,0:T(8,128)(2,1)}), bf16[8,64,384]{2,1,0:T(8,128)(2,1)S(1)}, u32[]{:S(2)}, u32[]{:S(2)}) async-start(bf16[8,64,384]{2,1,0:T(8,128)(2,1)} %get-tuple-element.63), calls=%async_computation.1 | async-start | bytes 786432 | tf_op jit(solution)/shard_map/all_to_all | solution.py:709
  32.4 0.5 collective-permute-start.5
  32.9 0.0 collective-permute-start.6
  32.9 0.5 collective-permute-start.7
  33.4 0.0 collective-permute-start.8
  33.4 4.7 %shard_map.207 = (bf16[64,32,128]{2,1,0:T(8,128)(2,1)}, bf16[64,48,128]{2,1,0:T(8,128)(2,1)}) custom-call(s32[4]{0:T(128)S(1)} %copy-done, s32[4]{0:T(128)S(1)} %collective-permute-done.partner, bf16[8,64,384]{2,1,0:T(8,128)(2,1)S(1)} %all-to-all-done.arrived.first, f32[64,384]{1,0:T(8,128)S(1)} %collective-permute-done.1.pack, ...), custom_call_target="tpu_custom_call" | custom-call | flops 6000000000 | bytes 21000000 | tf_op jit(solution)/shard_map/pallas_call | solution.py:766
  38.2 2.6 %all-to-all-done.1.arrived = bf16[8,64,384]{2,1,0:T(8,128)(2,1)S(1)} async-done(((bf16[8,64,384]{2,1,0:T(8,128)(2,1)}), bf16[8,64,384]{2,1,0:T(8,128)(2,1)S(1)}, u32[]{:S(2)}, u32[]{:S(2)}) %all-to-all-start.1) | async-done | bytes 393248 | tf_op jit(solution)/shard_map/all_to_all | solution.py:709
  40.7 0.0 collective-permute-done.5.refs_4_
  40.7 0.0 collective-permute-done.6.refs_5_
  40.7 0.0 collective-permute-done.7.refs_6_
  40.8 0.0 collective-permute-done.8.refs_7_
  40.8 3.6 %shard_map.208 = (bf16[4,96,512]{2,1,0:T(8,128)(2,1)}, bf16[8,64,384]{2,1,0:T(8,128)(2,1)}, bf16[384,1024]{1,0:T(8,128)(2,1)S(1)}) custom-call(s32[4]{0:T(128)S(1)} %copy-done, bf16[8,64,384]{2,1,0:T(8,128)(2,1)S(1)} %all-to-all-done.1.arrived, bf16[4,96,512]{2,1,0:T(8,128)(2,1)} %tokens.5, bf16[4,96,512]{2,1,0:T(8,128)(2,1)} %cotangent.3, ...), custom_call_target="tpu_custom_call" | custom-call | flops 6000000000 | bytes 21000000 | tf_op jit(solution)/shard_map/pallas_call | solution.py:777
  44.3 0.7 shard_map.211
  45.0 0.1 collective-permute-start.9
  45.1 3.5 %all-to-all-start.2 = ((bf16[8,64,384]{2,1,0:T(8,128)(2,1)}), bf16[8,64,384]{2,1,0:T(8,128)(2,1)S(1)}, u32[]{:S(2)}, u32[]{:S(2)}) async-start(bf16[8,64,384]{2,1,0:T(8,128)(2,1)} %get-tuple-element.72), calls=%async_computation.2 | async-start | bytes 786432 | tf_op jit(solution)/shard_map/all_to_all | solution.py:709
  48.6 0.0 collective-permute-done.9.came
  48.6 0.2 shard_map.212
  48.8 2.0 %collective-permute-start.10 = (bf16[64,1152]{1,0:T(8,128)(2,1)S(1)}, bf16[64,1152]{1,0:T(8,128)(2,1)S(1)}, u32[]{:S(2)}, u32[]{:S(2)}) collective-permute-start(bf16[64,1152]{1,0:T(8,128)(2,1)S(1)} %get-tuple-element.84), channel_id=1, source_target_pairs={{0,8},{4,12},{8,16},{12,20},{16,24},{20,28},{24,0},{28,4},{1,9},{5... | collective-permute-start | bytes 442376 | tf_op jit(solution)/shard_map/ppermute | solution.py:795
  50.7 0.9 %collective-permute-start.11 = (bf16[64,1152]{1,0:T(8,128)(2,1)S(1)}, bf16[64,1152]{1,0:T(8,128)(2,1)S(1)}, u32[]{:S(2)}, u32[]{:S(2)}) collective-permute-start(bf16[64,1152]{1,0:T(8,128)(2,1)S(1)} %get-tuple-element.85), channel_id=1, source_target_pairs={{0,16},{4,20},{8,24},{12,28},{16,0},{20,4},{24,8},{28,12},{1,17},{... | collective-permute-start | bytes 442376 | tf_op jit(solution)/shard_map/ppermute | solution.py:795
  51.6 2.8 %collective-permute-start.12 = (bf16[64,1152]{1,0:T(8,128)(2,1)S(1)}, bf16[64,1152]{1,0:T(8,128)(2,1)S(1)}, u32[]{:S(2)}, u32[]{:S(2)}) collective-permute-start(bf16[64,1152]{1,0:T(8,128)(2,1)S(1)} %get-tuple-element.86), channel_id=1, source_target_pairs={{0,24},{4,28},{8,0},{12,4},{16,8},{20,12},{24,16},{28,20},{1,25},{... | collective-permute-start | bytes 442376 | tf_op jit(solution)/shard_map/ppermute | solution.py:795
  54.4 2.4 %all-to-all-done.2.arrived = bf16[8,64,384]{2,1,0:T(8,128)(2,1)S(1)} async-done(((bf16[8,64,384]{2,1,0:T(8,128)(2,1)}), bf16[8,64,384]{2,1,0:T(8,128)(2,1)S(1)}, u32[]{:S(2)}, u32[]{:S(2)}) %all-to-all-start.2) | async-done | bytes 393248 | tf_op jit(solution)/shard_map/all_to_all | solution.py:709
  56.9 7.1 %shard_map.209 = (bf16[8,64,384]{2,1,0:T(8,128)(2,1)}, bf16[64,32,128]{2,1,0:T(8,128)(2,1)}, f32[2,64,128]{2,1,0:T(8,128)S(1)}) custom-call(s32[4]{0:T(128)S(1)} %copy-done, s32[4]{0:T(128)S(1)} %collective-permute-done.partner, bf16[8,64,384]{2,1,0:T(8,128)(2,1)S(1)} %all-to-all-done.2.arrived, bf16[8,64,384]{2,1,0:T(8,128)(2,1)S(1)} %all-to-all-done.arrived.first, ...), custom_call_target="tpu_custom_call" | custom-call | flops 1000000000 | bytes 3500000 | tf_op jit(solution)/shard_map/pallas_call | solution.py:796
  64.0 3.5 %all-to-all-start.3 = ((bf16[8,64,384]{2,1,0:T(8,128)(2,1)}), bf16[8,64,384]{2,1,0:T(8,128)(2,1)S(1)}, u32[]{:S(2)}, u32[]{:S(2)}) async-start(bf16[8,64,384]{2,1,0:T(8,128)(2,1)} %get-tuple-element.74), calls=%async_computation.3 | async-start | bytes 786432 | tf_op jit(solution)/shard_map/all_to_all | solution.py:709
  67.5 0.0 collective-permute-done.10.refs_1_
  67.5 0.0 collective-permute-done.11.refs_2_
  67.5 0.0 collective-permute-done.12.refs_3_
  67.5 0.1 shard_map.213.refs_0_
  67.6 4.5 %shard_map.214 = bf16[80,256]{1,0:T(8,128)(2,1)S(1)} custom-call(bf16[64,128,128]{2,1,0:T(8,128)(2,1)} %get-tuple-element.59.far_table, bf16[64,32,128]{2,1,0:T(8,128)(2,1)} %get-tuple-element.75.far_mirrored, bf16[64,48,128]{2,1,0:T(8,128)(2,1)} %get-tuple-element.76.far_prefix, bf16[64,32,128]{2,1,0:T(8,128)(2,1)} %get-tuple-element.77.far_grads, ...), custom_call_target="tpu_custom_call" | custom-call | flops 8000000000 | bytes 28000000 | tf_op jit(solution)/shard_map/pallas_call | solution.py:809
  72.1 2.0 %collective-permute-start.14 = (bf16[80,256]{1,0:T(8,128)(2,1)S(1)}, bf16[80,256]{1,0:T(8,128)(2,1)S(1)}, u32[]{:S(2)}, u32[]{:S(2)}) collective-permute-start(bf16[80,256]{1,0:T(8,128)(2,1)S(1)} %shard_map.214), channel_id=1, source_target_pairs={{0,1},{4,5},{1,9},{5,13},{2,17},{6,21},{3,25},{7,29},{8,0},{12,4},... | collective-permute-start | bytes 122888 | tf_op jit(solution)/shard_map/ppermute | solution.py:828
  74.0 3.1 %collective-permute-start.13 = (bf16[80,256]{1,0:T(8,128)(2,1)S(1)}, bf16[80,256]{1,0:T(8,128)(2,1)S(1)}, u32[]{:S(2)}, u32[]{:S(2)}) collective-permute-start(bf16[80,256]{1,0:T(8,128)(2,1)S(1)} %shard_map.214), channel_id=1, source_target_pairs={{0,3},{4,7},{1,11},{5,15},{2,19},{6,23},{3,27},{7,31},{8,2},{12,6}... | collective-permute-start | bytes 122888 | tf_op jit(solution)/shard_map/ppermute | solution.py:828
  77.2 0.6 collective-permute-start.17
  77.7 1.0 %collective-permute-start.16 = (bf16[64,1152]{1,0:T(8,128)(2,1)S(1)}, bf16[64,1152]{1,0:T(8,128)(2,1)S(1)}, u32[]{:S(2)}, u32[]{:S(2)}) collective-permute-start(bf16[64,1152]{1,0:T(8,128)(2,1)S(1)} %shard_map.213.refs_0_), channel_id=1, source_target_pairs={{0,2},{1,3},{2,0},{3,1},{4,6},{5,7},{6,4},{7,5},{8,10},{9,11},{10,... | collective-permute-start | bytes 442376 | tf_op jit(solution)/shard_map/ppermute | solution.py:806
  78.8 1.0 %collective-permute-start.15 = (bf16[64,1152]{1,0:T(8,128)(2,1)S(1)}, bf16[64,1152]{1,0:T(8,128)(2,1)S(1)}, u32[]{:S(2)}, u32[]{:S(2)}) collective-permute-start(bf16[64,1152]{1,0:T(8,128)(2,1)S(1)} %shard_map.213.refs_0_), channel_id=1, source_target_pairs={{0,1},{1,2},{2,3},{3,0},{4,5},{5,6},{6,7},{7,4},{8,9},{9,10},{10,1... | collective-permute-start | bytes 442376 | tf_op jit(solution)/shard_map/ppermute | solution.py:806
  79.8 0.0 all-to-all-done.3.arrived
  79.8 2.6 %shard_map.210 = bf16[4,96,512]{2,1,0:T(8,128)(2,1)} custom-call(bf16[8,64,384]{2,1,0:T(8,128)(2,1)S(1)} %all-to-all-done.3.arrived, bf16[4,96,512]{2,1,0:T(8,128)(2,1)} %tokens.5, bf16[4,96,512]{2,1,0:T(8,128)(2,1)} %cotangent.3), custom_call_target="tpu_custom_call" | custom-call | flops 3000000000 | bytes 10500000 | tf_op jit(solution)/shard_map/pallas_call | solution.py:819
  82.4 0.0 collective-permute-done.14.refs_1_
  82.4 0.0 collective-permute-done.13.refs_0_
  82.5 1.5 %collective-permute-start.18 = (bf16[80,256]{1,0:T(8,128)(2,1)S(1)}, bf16[80,256]{1,0:T(8,128)(2,1)S(1)}, u32[]{:S(2)}, u32[]{:S(2)}) collective-permute-start(bf16[80,256]{1,0:T(8,128)(2,1)S(1)} %shard_map.215.refs_4_), channel_id=1, source_target_pairs={{0,1},{1,0},{2,3},{3,2},{4,5},{5,4},{6,7},{7,6},{8,9},{9,8},{10,11... | collective-permute-start | bytes 122888 | tf_op jit(solution)/shard_map/ppermute | solution.py:845
  84.0 3.1 %collective-permute-done.18.refs_5_ = bf16[80,256]{1,0:T(8,128)(2,1)S(1)} collective-permute-done((bf16[80,256]{1,0:T(8,128)(2,1)S(1)}, bf16[80,256]{1,0:T(8,128)(2,1)S(1)}, u32[]{:S(2)}, u32[]{:S(2)}) %collective-permute-start.18) | collective-permute-done | bytes 40992 | tf_op jit(solution)/shard_map/ppermute | solution.py:845
  87.0 0.0 collective-permute-done.17.refs_3_
  87.0 0.0 collective-permute-done.16.refs_2_
  87.0 0.0 collective-permute-done.15.refs_1_
  87.1 0.0 copy-done.2
  87.1 0.0 copy-done.3
  87.1 0.0 copy-done.4
  87.1 0.9 %shard_map.216 = (f32[64,1024]{1,0:T(8,128)}, f32[1,128]{1,0:T(1,128)}, f32[64,64]{1,0:T(8,128)}, f32[64,64]{1,0:T(8,128)}, f32[64,64]{1,0:T(8,128)}, /*index=5*...) custom-call(bf16[64,1152]{1,0:T(8,128)(2,1)S(1)} %shard_map.213.refs_0_, ...), custom_call_target="tpu_custom_call" | custom-call | flops 2000000000 | bytes 7000000 | tf_op jit(solution)/shard_map/pallas_call | solution.py:838
  (6 shorter events, 0.0 us)
Async XLA Ops:
  0.6 20.9 %collective-permute-start = (s32[4]{0:T(128)}, s32[4]{0:T(128)S(1)}, u32[]{:S(2)}, u32[]{:S(2)}) collective-permute-start(s32[4]{0:T(128)} %lengths.7), channel_id=1, source_target_pairs={{0,4},{4,0},{8,12},{12,8},{16,20},{20,16},{24,28},{28,24},{1,5},{5... | collective-permute-start | bytes 56 | tf_op jit(solution)/shard_map/ppermute | solution.py:734
  1.2 5.9 %copy-start.1 = (bf16[4,96,512]{2,1,0:T(8,128)(2,1)S(1)}, bf16[4,96,512]{2,1,0:T(8,128)(2,1)}, u32[]{:S(2)}) copy-start(bf16[4,96,512]{2,1,0:T(8,128)(2,1)} %tokens.5) | copy-start | bytes 1179652
  2.4 9.3 %collective-permute-start.1 = (f32[64,384]{1,0:T(8,128)S(1)}, f32[64,384]{1,0:T(8,128)S(1)}, u32[]{:S(2)}, u32[]{:S(2)}) collective-permute-start(f32[64,384]{1,0:T(8,128)S(1)} %get-tuple-element.57), channel_id=1, source_target_pairs={{3,0},{7,4},{11,1},{15,5},{19,2},{23,6},{27,3},{31,7},{2,8},{6,12}... | collective-permute-start | bytes 294920 | tf_op jit(solution)/shard_map/ppermute | solution.py:725
  8.2 13.4 %all-to-all-start = ((bf16[8,64,384]{2,1,0:T(8,128)(2,1)}), bf16[8,64,384]{2,1,0:T(8,128)(2,1)S(1)}, u32[]{:S(2)}, u32[]{:S(2)}) async-start(bf16[8,64,384]{2,1,0:T(8,128)(2,1)} %shard_map.203), calls=%async_computation | async-start | bytes 786432 | tf_op jit(solution)/shard_map/all_to_all | solution.py:709
  11.7 9.9 %copy-start = (s32[4]{0:T(128)S(1)}, s32[4]{0:T(128)}, u32[]{:S(2)}) copy-start(s32[4]{0:T(128)} %lengths.7) | copy-start | bytes 52
  11.7 16.4 %collective-permute-start.4 = (bf16[64,1152]{1,0:T(8,128)(2,1)S(1)}, bf16[64,1152]{1,0:T(8,128)(2,1)S(1)}, u32[]{:S(2)}, u32[]{:S(2)}) collective-permute-start(bf16[64,1152]{1,0:T(8,128)(2,1)S(1)} %get-tuple-element.67.refs_0_), channel_id=1, source_target_pairs={{0,24},{4,28},{8,0},{12,4},{16,8},{20,12},{24,16},{28,20},{1,25},{... | collective-permute-start | bytes 442376 | tf_op jit(solution)/shard_map/ppermute | solution.py:742
  14.2 14.3 %collective-permute-start.3 = (bf16[64,1152]{1,0:T(8,128)(2,1)S(1)}, bf16[64,1152]{1,0:T(8,128)(2,1)S(1)}, u32[]{:S(2)}, u32[]{:S(2)}) collective-permute-start(bf16[64,1152]{1,0:T(8,128)(2,1)S(1)} %get-tuple-element.67.refs_0_), channel_id=1, source_target_pairs={{0,16},{4,20},{8,24},{12,28},{16,0},{20,4},{24,8},{28,12},{1,17},{... | collective-permute-start | bytes 442376 | tf_op jit(solution)/shard_map/ppermute | solution.py:742
  15.5 13.0 %collective-permute-start.2 = (bf16[64,1152]{1,0:T(8,128)(2,1)S(1)}, bf16[64,1152]{1,0:T(8,128)(2,1)S(1)}, u32[]{:S(2)}, u32[]{:S(2)}) collective-permute-start(bf16[64,1152]{1,0:T(8,128)(2,1)S(1)} %get-tuple-element.67.refs_0_), channel_id=1, source_target_pairs={{0,8},{4,12},{8,16},{12,20},{16,24},{20,28},{24,0},{28,4},{1,9},{5... | collective-permute-start | bytes 442376 | tf_op jit(solution)/shard_map/ppermute | solution.py:742
  28.6 12.2 %all-to-all-start.1 = ((bf16[8,64,384]{2,1,0:T(8,128)(2,1)}), bf16[8,64,384]{2,1,0:T(8,128)(2,1)S(1)}, u32[]{:S(2)}, u32[]{:S(2)}) async-start(bf16[8,64,384]{2,1,0:T(8,128)(2,1)} %get-tuple-element.63), calls=%async_computation.1 | async-start | bytes 786432 | tf_op jit(solution)/shard_map/all_to_all | solution.py:709
  32.4 8.3 %collective-permute-start.5 = (bf16[64,1152]{1,0:T(8,128)(2,1)S(1)}, bf16[64,1152]{1,0:T(8,128)(2,1)S(1)}, u32[]{:S(2)}, u32[]{:S(2)}) collective-permute-start(bf16[64,1152]{1,0:T(8,128)(2,1)S(1)} %get-tuple-element.67.refs_0_), channel_id=1, source_target_pairs={{0,4},{4,0},{8,12},{12,8},{16,20},{20,16},{24,28},{28,24},{1,5},{5... | collective-permute-start | bytes 442376 | tf_op jit(solution)/shard_map/ppermute | solution.py:774
  32.9 7.8 %collective-permute-start.6 = (bf16[64,1152]{1,0:T(8,128)(2,1)S(1)}, bf16[64,1152]{1,0:T(8,128)(2,1)S(1)}, u32[]{:S(2)}, u32[]{:S(2)}) collective-permute-start(bf16[64,1152]{1,0:T(8,128)(2,1)S(1)} %collective-permute-done.2.refs_1_), channel_id=1, source_target_pairs={{0,4},{4,0},{8,12},{12,8},{16,20},{20,16},{24,28},{28,24},{1,5},{5... | collective-permute-start | bytes 442376 | tf_op jit(solution)/shard_map/ppermute | solution.py:774
  32.9 7.8 %collective-permute-start.7 = (bf16[64,1152]{1,0:T(8,128)(2,1)S(1)}, bf16[64,1152]{1,0:T(8,128)(2,1)S(1)}, u32[]{:S(2)}, u32[]{:S(2)}) collective-permute-start(bf16[64,1152]{1,0:T(8,128)(2,1)S(1)} %collective-permute-done.3.refs_2_), channel_id=1, source_target_pairs={{0,4},{4,0},{8,12},{12,8},{16,20},{20,16},{24,28},{28,24},{1,5},{5... | collective-permute-start | bytes 442376 | tf_op jit(solution)/shard_map/ppermute | solution.py:774
  33.4 7.3 %collective-permute-start.8 = (bf16[64,1152]{1,0:T(8,128)(2,1)S(1)}, bf16[64,1152]{1,0:T(8,128)(2,1)S(1)}, u32[]{:S(2)}, u32[]{:S(2)}) collective-permute-start(bf16[64,1152]{1,0:T(8,128)(2,1)S(1)} %collective-permute-done.4.refs_3_), channel_id=1, source_target_pairs={{0,4},{4,0},{8,12},{12,8},{16,20},{20,16},{24,28},{28,24},{1,5},{5... | collective-permute-start | bytes 442376 | tf_op jit(solution)/shard_map/ppermute | solution.py:774
  45.0 3.6 %collective-permute-start.9 = (bf16[4,64,1152]{2,1,0:T(8,128)(2,1)S(1)}, bf16[4,64,1152]{2,1,0:T(8,128)(2,1)S(1)}, u32[]{:S(2)}, u32[]{:S(2)}) collective-permute-start(bf16[4,64,1152]{2,1,0:T(8,128)(2,1)S(1)} %get-tuple-element.82), channel_id=1, source_target_pairs={{0,4},{4,0},{8,12},{12,8},{16,20},{20,16},{24,28},{28,24},{1,5},{5... | collective-permute-start | bytes 1769480 | tf_op jit(solution)/shard_map/ppermute | solution.py:790
  45.1 11.7 %all-to-all-start.2 = ((bf16[8,64,384]{2,1,0:T(8,128)(2,1)}), bf16[8,64,384]{2,1,0:T(8,128)(2,1)S(1)}, u32[]{:S(2)}, u32[]{:S(2)}) async-start(bf16[8,64,384]{2,1,0:T(8,128)(2,1)} %get-tuple-element.72), calls=%async_computation.2 | async-start | bytes 786432 | tf_op jit(solution)/shard_map/all_to_all | solution.py:709
  48.8 18.7 %collective-permute-start.10 = (bf16[64,1152]{1,0:T(8,128)(2,1)S(1)}, bf16[64,1152]{1,0:T(8,128)(2,1)S(1)}, u32[]{:S(2)}, u32[]{:S(2)}) collective-permute-start(bf16[64,1152]{1,0:T(8,128)(2,1)S(1)} %get-tuple-element.84), channel_id=1, source_target_pairs={{0,8},{4,12},{8,16},{12,20},{16,24},{20,28},{24,0},{28,4},{1,9},{5... | collective-permute-start | bytes 442376 | tf_op jit(solution)/shard_map/ppermute | solution.py:795
  50.7 16.8 %collective-permute-start.11 = (bf16[64,1152]{1,0:T(8,128)(2,1)S(1)}, bf16[64,1152]{1,0:T(8,128)(2,1)S(1)}, u32[]{:S(2)}, u32[]{:S(2)}) collective-permute-start(bf16[64,1152]{1,0:T(8,128)(2,1)S(1)} %get-tuple-element.85), channel_id=1, source_target_pairs={{0,16},{4,20},{8,24},{12,28},{16,0},{20,4},{24,8},{28,12},{1,17},{... | collective-permute-start | bytes 442376 | tf_op jit(solution)/shard_map/ppermute | solution.py:795
  51.6 15.9 %collective-permute-start.12 = (bf16[64,1152]{1,0:T(8,128)(2,1)S(1)}, bf16[64,1152]{1,0:T(8,128)(2,1)S(1)}, u32[]{:S(2)}, u32[]{:S(2)}) collective-permute-start(bf16[64,1152]{1,0:T(8,128)(2,1)S(1)} %get-tuple-element.86), channel_id=1, source_target_pairs={{0,24},{4,28},{8,0},{12,4},{16,8},{20,12},{24,16},{28,20},{1,25},{... | collective-permute-start | bytes 442376 | tf_op jit(solution)/shard_map/ppermute | solution.py:795
  64.0 15.8 %all-to-all-start.3 = ((bf16[8,64,384]{2,1,0:T(8,128)(2,1)}), bf16[8,64,384]{2,1,0:T(8,128)(2,1)S(1)}, u32[]{:S(2)}, u32[]{:S(2)}) async-start(bf16[8,64,384]{2,1,0:T(8,128)(2,1)} %get-tuple-element.74), calls=%async_computation.3 | async-start | bytes 786432 | tf_op jit(solution)/shard_map/all_to_all | solution.py:709
  72.1 10.3 %collective-permute-start.14 = (bf16[80,256]{1,0:T(8,128)(2,1)S(1)}, bf16[80,256]{1,0:T(8,128)(2,1)S(1)}, u32[]{:S(2)}, u32[]{:S(2)}) collective-permute-start(bf16[80,256]{1,0:T(8,128)(2,1)S(1)} %shard_map.214), channel_id=1, source_target_pairs={{0,1},{4,5},{1,9},{5,13},{2,17},{6,21},{3,25},{7,29},{8,0},{12,4},... | collective-permute-start | bytes 122888 | tf_op jit(solution)/shard_map/ppermute | solution.py:828
  74.0 8.4 %collective-permute-start.13 = (bf16[80,256]{1,0:T(8,128)(2,1)S(1)}, bf16[80,256]{1,0:T(8,128)(2,1)S(1)}, u32[]{:S(2)}, u32[]{:S(2)}) collective-permute-start(bf16[80,256]{1,0:T(8,128)(2,1)S(1)} %shard_map.214), channel_id=1, source_target_pairs={{0,3},{4,7},{1,11},{5,15},{2,19},{6,23},{3,27},{7,31},{8,2},{12,6}... | collective-permute-start | bytes 122888 | tf_op jit(solution)/shard_map/ppermute | solution.py:828
  77.2 9.9 %collective-permute-start.17 = (bf16[64,1152]{1,0:T(8,128)(2,1)S(1)}, bf16[64,1152]{1,0:T(8,128)(2,1)S(1)}, u32[]{:S(2)}, u32[]{:S(2)}) collective-permute-start(bf16[64,1152]{1,0:T(8,128)(2,1)S(1)} %shard_map.213.refs_0_), channel_id=1, source_target_pairs={{0,3},{1,0},{2,1},{3,2},{4,7},{5,4},{6,5},{7,6},{8,11},{9,8},{10,9... | collective-permute-start | bytes 442376 | tf_op jit(solution)/shard_map/ppermute | solution.py:806
  77.7 9.3 %collective-permute-start.16 = (bf16[64,1152]{1,0:T(8,128)(2,1)S(1)}, bf16[64,1152]{1,0:T(8,128)(2,1)S(1)}, u32[]{:S(2)}, u32[]{:S(2)}) collective-permute-start(bf16[64,1152]{1,0:T(8,128)(2,1)S(1)} %shard_map.213.refs_0_), channel_id=1, source_target_pairs={{0,2},{1,3},{2,0},{3,1},{4,6},{5,7},{6,4},{7,5},{8,10},{9,11},{10,... | collective-permute-start | bytes 442376 | tf_op jit(solution)/shard_map/ppermute | solution.py:806
  78.8 8.3 %collective-permute-start.15 = (bf16[64,1152]{1,0:T(8,128)(2,1)S(1)}, bf16[64,1152]{1,0:T(8,128)(2,1)S(1)}, u32[]{:S(2)}, u32[]{:S(2)}) collective-permute-start(bf16[64,1152]{1,0:T(8,128)(2,1)S(1)} %shard_map.213.refs_0_), channel_id=1, source_target_pairs={{0,1},{1,2},{2,3},{3,0},{4,5},{5,6},{6,7},{7,4},{8,9},{9,10},{10,1... | collective-permute-start | bytes 442376 | tf_op jit(solution)/shard_map/ppermute | solution.py:806
  82.4 4.7 %copy-start.2 = (f32[64,64]{1,0:T(8,128)S(1)}, f32[64,64]{1,0:T(8,128)}, u32[]{:S(2)}) copy-start(f32[64,64]{1,0:T(8,128)} %refs_6_.1) | copy-start | bytes 49156
  82.4 4.7 %copy-start.3 = (f32[64,64]{1,0:T(8,128)S(1)}, f32[64,64]{1,0:T(8,128)}, u32[]{:S(2)}) copy-start(f32[64,64]{1,0:T(8,128)} %refs_8_.1) | copy-start | bytes 49156
  82.4 4.7 %copy-start.4 = (f32[64,64]{1,0:T(8,128)S(1)}, f32[64,64]{1,0:T(8,128)}, u32[]{:S(2)}) copy-start(f32[64,64]{1,0:T(8,128)} %refs_9_.1) | copy-start | bytes 49156
  82.5 4.6 %collective-permute-start.18 = (bf16[80,256]{1,0:T(8,128)(2,1)S(1)}, bf16[80,256]{1,0:T(8,128)(2,1)S(1)}, u32[]{:S(2)}, u32[]{:S(2)}) collective-permute-start(bf16[80,256]{1,0:T(8,128)(2,1)S(1)} %shard_map.215.refs_4_), channel_id=1, source_target_pairs={{0,1},{1,0},{2,3},{3,2},{4,5},{5,4},{6,7},{7,6},{8,9},{9,8},{10,11... | collective-permute-start | bytes 122888 | tf_op jit(solution)/shard_map/ppermute | solution.py:845
